TPU v7x, 512 devices: a whole 4x4x16 slice. The times are simulated.
512 devices in a mesh: row: 32 (over z_lo, x), col: 16 (over y, z_hi, core).
Axes of the slice: x: 4, y: 4, z: 16 (z_hi: 2, z_lo: 8; z = z_hi * 8 + z_lo), core: 2. Of those that a mesh axis runs over, the one named last changes fastest.
Arguments:
- iterate: float32 [3584, 9216], P('row', 'col'), may hold values from -0.09375 to 0.09375
Outputs:
- update: float32 [3584, 9216], P('row', 'col')
All inputs are finite; a program needn't handle non-finite values.
Results may differ from a plain program's by a relative error of at most 0.000068.
Values sent between devices are 32-bit elements; how exact they have to be, the bound alone decides.
No kernel may reach another device: no remote copies, remote signals or barrier semaphores. Data moves between devices by JAX's collectives and lax.ppermute only.
A program may use at most 64 MiB of HBM per device.

v0:
```python
import math

import jax
import jax.numpy as jnp
from jax import lax
from jax.sharding import PartitionSpec as P

M = 3584
N = 9216


HIGHEST_PREC = lax.Precision.HIGHEST
COEF_A = 3.4445
COEF_B = -4.775
COEF_C = 2.0315


def matmul(left, right):
    return jnp.dot(left, right, precision=HIGHEST_PREC, preferred_element_type=jnp.float32)


def body(iterate):
    col_count = lax.axis_size("col")
    slab_all = lax.all_gather(iterate, "row", axis=0, tiled=True)
    partial_value = matmul(iterate, slab_all.T)
    gram_panel = lax.psum(partial_value, "col")
    tile_width = gram_panel.shape[1] // col_count
    my_col = lax.axis_index("col")
    gram_tile = lax.dynamic_slice_in_dim(gram_panel, my_col * tile_width, tile_width, 1)
    gram_column = lax.all_gather(gram_tile, "row", axis=0, tiled=True)
    square_tile = matmul(gram_panel, gram_column)
    poly_tile = COEF_B * gram_tile + COEF_C * square_tile
    poly_panel = lax.all_gather(poly_tile, "col", axis=1, tiled=True)
    applied = matmul(poly_panel, slab_all)
    return (COEF_A * iterate + applied) * (0.2 * math.sqrt(max(M, N)))


def solution(mesh):
    placed = (P("row", "col"),)
    return jax.shard_map(
        body, mesh=mesh, in_specs=placed, out_specs=P("row", "col"), check_vma=False
    )
```

profile of v0, /device:TPU:1, one launch (start us, length us, event | category | flops | bytes accessed | tf_op | source)
XLA Modules:
  0.0 899.9 jit_solution(3289256013410741177)
XLA Ops:
  6.5 0.0 all-gather.4.cloned.1.call-start
  6.5 0.7 all-gather.4.cloned.1.call-update
  7.3 0.0 all-reduce.2.cloned.1.call-start
  7.3 227.7 %all-gather.4.cloned.1.call-done = f32[3584,576]{1,0:T(8,128)} async-done(((f32[112,576]{1,0:T(8,128)}), f32[3584,576]{1,0:T(8,128)}) %all-gather.4.cloned.1.call-update) | async-done | bytes 8257552 | tf_op jit(solution)/shard_map/all_gather | solution.py:24
  235.0 13.8 %fusion.2 = f32[112,3584]{1,0:T(8,128)} fusion(f32[112,576]{1,0:T(8,128)} %param.1, f32[3584,576]{1,0:T(8,128)} %all-gather.4.cloned.1.call-done), kind=kOutput, calls=%fused_computation.5 | convolution fusion | flops 2774532096 | bytes 10121216 | tf_op jit(solution)/shard_map/dot_general | solution.py:19
  248.8 0.0 copy-start
  248.8 0.0 all-reduce.2.cloned.1.call-update
  248.8 0.0 all-gather.6.cloned.1.call-start
  248.9 305.5 %all-reduce.2.cloned.1.call-done = f32[112,3584]{1,0:T(8,128)} async-done(((f32[112,3584]{1,0:T(8,128)}), f32[112,3584]{1,0:T(8,128)}) %all-reduce.2.cloned.1.call-update) | async-done | bytes 1605648 | tf_op jit(solution)/shard_map/psum | solution.py:26
  554.4 1.7 constant_dynamic-slice_fusion
  556.1 0.0 all-gather.6.cloned.1.call-update
  556.1 0.2 all-gather.8.cloned.1.call-start
  556.3 212.9 %all-gather.6.cloned.1.call-done = f32[3584,224]{1,0:T(8,128)} async-done(((f32[112,224]{1,0:T(8,128)}), f32[3584,224]{1,0:T(8,128)}) %all-gather.6.cloned.1.call-update) | async-done | bytes 3211280 | tf_op jit(solution)/shard_map/all_gather | solution.py:30
  769.2 4.3 fusion.1
  773.5 0.7 copy.2
  774.3 0.0 all-gather.8.cloned.1.call-update
  774.3 108.6 %all-gather.8.cloned.1.call-done = f32[112,3584]{0,1:T(8,128)} async-done(((f32[112,224]{0,1:T(8,128)}), f32[112,3584]{0,1:T(8,128)}) %all-gather.8.cloned.1.call-update) | async-done | bytes 1605648 | tf_op jit(solution)/shard_map/all_gather | solution.py:33
  882.9 0.0 copy-done
  882.9 10.5 %fusion = f32[112,576]{1,0:T(8,128)} fusion(f32[112,3584]{0,1:T(8,128)} %all-gather.8.cloned.1.call-done, f32[3584,576]{1,0:T(8,128)} %all-gather.4.cloned.1.call-done, f32[112,576]{1,0:T(8,128)S(1)} %copy-done), kind=kOutput, calls=%fused_computation.1 | convolution fusion | flops 2774725632 | bytes 10379264 | tf_op jit(solution)/shard_map/dot_general | solution.py:19
Async XLA Ops:
  6.5 228.4 %all-gather.4.cloned.1.call-start = ((), (), s32[]{:S(2)}) async-start(), calls=%async_computation | async-start | bytes 9461760 | tf_op jit(solution)/shard_map/all_gather | solution.py:24
  7.3 547.2 %all-reduce.2.cloned.1.call-start = ((), (), s32[]{:S(2)}) async-start(), calls=%async_computation.1 | async-start | bytes 3211264 | tf_op jit(solution)/shard_map/psum | solution.py:26
  248.8 634.1 %copy-start = (f32[112,576]{1,0:T(8,128)S(1)}, f32[112,576]{1,0:T(8,128)}, u32[]{:S(2)}) copy-start(f32[112,576]{1,0:T(8,128)} %param.1) | copy-start | bytes 774148
  248.8 520.3 %all-gather.6.cloned.1.call-start = ((), (), s32[]{:S(2)}) async-start(), calls=%async_computation.2 | async-start | bytes 3784704 | tf_op jit(solution)/shard_map/all_gather | solution.py:30
  556.1 326.8 %all-gather.8.cloned.1.call-start = ((), (), s32[]{:S(2)}) async-start(), calls=%async_computation.3 | async-start | bytes 1949696 | tf_op jit(solution)/shard_map/all_gather | solution.py:33
Sparse Core Ops, SparseCore 0:
  9.4 225.4 all-gather.3
  249.0 305.4 all-reduce.1
  556.7 212.4 all-gather.5
  774.4 108.4 all-gather.7
where the time goes:
time: 900 us
  waiting for transfers between devices  855 us (95%)
  matrix products  28.7 us (3%)
  between operations  13.1 us (1%)
    psum x1, waiting for transfers between devices, body(): gram_panel = lax.psum(partial_value, 'col')  306 us
    all_gather x1, waiting for transfers between devices, body(): slab_all = lax.all_gather(iterate, 'row', axis=0, tiled=True)  228 us
    all_gather x1, waiting for transfers between devices, body(): gram_column = lax.all_gather(gram_tile, 'row', axis=0, tiled=True)  213 us
    all_gather x1, waiting for transfers between devices, body(): poly_panel = lax.all_gather(poly_tile, 'col', axis=1, tiled=True)  109 us
    dot_general x3, matrix products, matmul(): jnp.dot(left, right, precision=HIGHEST_PREC, preferred_element_type=jnp.f...  28.7 us
  transfers between devices with their start and end apart: 4, of which 4 were waited for; matrix products, arithmetic and copies ran while one was open for 0% of the time, Pallas kernels for 0%

commit v1 on v0

v1 whole, which is shorter than its diff:
```python
import math

import jax
import jax.numpy as jnp
from jax import lax
from jax.sharding import PartitionSpec as P

M = 3584
N = 9216

HIGHEST_PREC = lax.Precision.HIGHEST
COEF_A = 3.4445
COEF_B = -4.775
COEF_C = 2.0315
AXES = ("row", "col")

X_GROUPS = [[zl * 4 + x for x in range(4)] for zl in range(8)]
ZLO_GROUPS = [[zl * 4 + x for zl in range(8)] for x in range(4)]
Y_GROUPS = [[y * 4 + k for y in range(4)] for k in range(4)]
CORE_GROUPS = [[p * 2, p * 2 + 1] for p in range(8)]


def device(x, y, z, core):
    return ((z % 8) * 4 + x) * 16 + y * 4 + (z // 8) * 2 + core


CHIPS = [(x, y, z) for x in range(4) for y in range(4) for z in range(16)]
FAR_GROUPS = [
    [device(x, y, (a * 4 + b), c) for a in range(4)]
    for x in range(4) for y in range(4) for b in range(4) for c in range(2)
]


def permute(value, target):
    pairs = [
        (device(x, y, z, c), device(*target(x, y, z, c))) for x, y, z in CHIPS for c in range(2)
    ]
    return lax.ppermute(value, AXES, pairs)


def z_shift(value, step):
    return permute(value, lambda x, y, z, c: (x, y, (z + step) % 16, c))


def dot(left, right, dims):
    return lax.dot_general(
        left, right, (dims, ((), ())), precision=HIGHEST_PREC, preferred_element_type=jnp.float32
    )


def rows_at(value, start, size):
    return lax.dynamic_slice_in_dim(value, start, size, 0)


def body(iterate):
    rows, cols = iterate.shape
    part = cols // 8
    row, col = lax.axis_index("row"), lax.axis_index("col")
    core = col % 2
    z = (col // 2 % 2) * 8 + row // 4

    with jax.named_scope("to_planes"):
        blocks = iterate.T.reshape(8, part, rows)
        blocks = lax.all_to_all(blocks, "row", 0, 0, axis_index_groups=ZLO_GROUPS)
        own = blocks.transpose(1, 0, 2).reshape(part, 8 * rows)
    with jax.named_scope("faces"):
        across = permute(own, lambda x, y, z, c: (y, x, z, c))
        left = lax.all_gather(own, "col", axis=0, tiled=True, axis_index_groups=Y_GROUPS)
        right = lax.all_gather(across, "row", axis=0, tiled=True, axis_index_groups=X_GROUPS)
    size = left.shape[1]
    half, chunk = size // 2, size // 8

    with jax.named_scope("gram"):
        partial = dot(left, right, ((0,), (0,)))
        other = rows_at(partial, (1 - core) * half, half)
        mine = rows_at(partial, core * half, half)
        total = mine + permute(other, lambda x, y, z, c: (x, y, z, 1 - c))
    with jax.named_scope("reduce_near"):
        here = rows_at(total, z % 4 * chunk, chunk)
        up = z_shift(rows_at(total, (z + 1) % 4 * chunk, chunk), 1)
        down = z_shift(rows_at(total, (z + 3) % 4 * chunk, chunk), -1)
        start = (z + 2) % 4 * chunk
        up_two = z_shift(rows_at(total, start, chunk // 2), 2)
        down_two = z_shift(rows_at(total, start + chunk // 2, chunk // 2), -2)
        near = here + up + down + jnp.concatenate([up_two, down_two], 0)
    with jax.named_scope("reduce_far"):
        pieces = near.reshape(4, chunk // 4, size)
        pieces = lax.all_to_all(pieces, AXES, 0, 0, axis_index_groups=FAR_GROUPS)
        piece = jnp.sum(pieces, 0)
    with jax.named_scope("gather_far"):
        pieces = jnp.broadcast_to(piece, (4,) + piece.shape)
        pieces = lax.all_to_all(pieces, AXES, 0, 0, axis_index_groups=FAR_GROUPS)
        near = pieces.reshape(chunk, size)
    with jax.named_scope("gather_near"):
        from_below = z_shift(near, 1)
        from_above = z_shift(near, -1)
        first = z_shift(near[: chunk // 2], -2)
        second = z_shift(near[chunk // 2 :], 2)
        total = jnp.zeros((half, size), jnp.float32)
        put = lax.dynamic_update_slice_in_dim
        total = put(total, near, z % 4 * chunk, 0)
        total = put(total, from_below, (z + 3) % 4 * chunk, 0)
        total = put(total, from_above, (z + 1) % 4 * chunk, 0)
        total = put(total, first, start, 0)
        total = put(total, second, start + chunk // 2, 0)
    with jax.named_scope("gather_core"):
        gram = lax.all_gather(total, "col", axis=0, tiled=True, axis_index_groups=CORE_GROUPS)

    with jax.named_scope("first_product"):
        product = dot(left, gram, ((1,), (0,)))
        parts = product.reshape(4, part, size)
        parts = lax.all_to_all(parts, "row", 0, 0, axis_index_groups=X_GROUPS)
        inner = COEF_B * across + COEF_C * jnp.sum(parts, 0)
        inner = lax.all_gather(inner, "row", axis=0, tiled=True, axis_index_groups=X_GROUPS)
    with jax.named_scope("second_product"):
        product = dot(inner, gram, ((1,), (1,)))
        parts = product.reshape(4, part, size)
        parts = lax.all_to_all(parts, "col", 0, 0, axis_index_groups=Y_GROUPS)
        applied = jnp.sum(parts, 0)
    with jax.named_scope("to_blocks"):
        blocks = applied.reshape(part, 8, rows).transpose(1, 0, 2)
        blocks = lax.all_to_all(blocks, "row", 0, 0, axis_index_groups=ZLO_GROUPS)
        applied = blocks.reshape(cols, rows).T
    return (COEF_A * iterate + applied) * (0.2 * math.sqrt(max(M, N)))


def solution(mesh):
    placed = (P("row", "col"),)
    return jax.shard_map(
        body, mesh=mesh, in_specs=placed, out_specs=P("row", "col"), check_vma=False
    )
```

time: 900 us -> 323 us (0.36)
  the two profiles are of different devices: /device:TPU:1 before, /device:TPU:2 now
where the time goes in v1:
time: 323 us; the launch traced here: 322 us
  blocking collectives  173 us (54%)
  waiting for transfers between devices  53 us (16%)
  starting transfers between devices  48.7 us (15%)
  matrix products  15.7 us (5%)
  between operations  13.9 us (4%)
  local copies, waits for them, and re-layouts  10.9 us (3%)
  other arithmetic  6.7 us (2%)
    all_to_all x2, blocking collectives, body(): pieces = lax.all_to_all(pieces, AXES, 0, 0, axis_index_groups=FAR_GROUPS)  62.3 us
    ppermute x10, starting transfers between devices, permute(): return lax.ppermute(value, AXES, pairs)  36.1 us
    all_to_all x1, blocking collectives, body(): blocks = lax.all_to_all(blocks, 'row', 0, 0, axis_index_groups=ZLO_GROUPS)  25.7 us
    all_gather x1, blocking collectives, body(): lax.all_gather(own, 'col', axis=0, tiled=True, axis_index_groups=Y_GROUPS)  20.4 us
    ppermute x10, waiting for transfers between devices, permute(): return lax.ppermute(value, AXES, pairs)  18.9 us
    all_to_all x1, blocking collectives, body(): parts = lax.all_to_all(parts, 'row', 0, 0, axis_index_groups=X_GROUPS)  18.9 us
    all_to_all x1, waiting for transfers between devices, body(): blocks = lax.all_to_all(blocks, 'row', 0, 0, axis_index_groups=ZLO_GROUPS)  17.8 us
    all_to_all x1, blocking collectives, body(): parts = lax.all_to_all(parts, 'col', 0, 0, axis_index_groups=Y_GROUPS)  16.7 us
  transfers between devices with their start and end apart: 12, of which 7 were waited for; matrix products, arithmetic and copies ran while one was open for 1% of the time, Pallas kernels for 0%

profile of v1, /device:TPU:2, one launch (start us, length us, event | category | flops | bytes accessed | tf_op | source)
XLA Modules:
  0.0 321.8 jit_solution(45845168098575685)
XLA Ops:
  8.3 12.5 %all-to-all-start = ((f32[8,72,112]{2,1,0:T(8,128)}), f32[8,72,112]{2,1,0:T(8,128)S(1)}, u32[]{:S(2)}, u32[]{:S(2)}) async-start(f32[8,72,112]{2,1,0:T(8,128)} %bitcast.1), calls=%async_computation | async-start | bytes 589824 | tf_op jit(solution)/shard_map/to_planes/all_to_all | solution.py:64
  20.9 17.8 %all-to-all-done = f32[8,72,112]{2,1,0:T(8,128)S(1)} async-done(((f32[8,72,112]{2,1,0:T(8,128)}), f32[8,72,112]{2,1,0:T(8,128)S(1)}, u32[]{:S(2)}, u32[]{:S(2)}) %all-to-all-start) | async-done | bytes 258080 | tf_op jit(solution)/shard_map/to_planes/all_to_all | solution.py:64
  38.9 3.5 %collective-permute-start = (f32[72,896]{1,0:T(8,128)S(1)}, f32[72,896]{1,0:T(8,128)S(1)}, u32[]{:S(2)}, u32[]{:S(2)}) collective-permute-start(f32[72,896]{1,0:T(8,128)S(1)} %reshape.27), channel_id=1, source_target_pairs={{0,0},{1,1},{64,64},{65,65},{128,128},{129,129},{192,192},{193,193... | collective-permute-start | bytes 774152 | tf_op jit(solution)/shard_map/faces/ppermute | solution.py:38
  42.4 20.4 %all_gather.12 = f32[288,896]{1,0:T(8,128)S(1)} all-gather(f32[72,896]{1,0:T(8,128)S(1)} %reshape.27), channel_id=1, replica_groups={{0,4,8,12},{1,5,9,13},{2,6,10,14},{3,7,11,15},{16,20,24,28},{17,21,25,2..., dimensions={0}, use_global_device_ids=true | all-gather | bytes 1290240 | tf_op jit(solution)/shard_map/faces/all_gather | solution.py:68
  62.8 15.1 %all_gather.13 = f32[288,896]{1,0:T(8,128)S(1)} all-gather(f32[72,896]{1,0:T(8,128)S(1)} %collective-permute-done), channel_id=1, replica_groups={{0,16,32,48},{64,80,96,112},{128,144,160,176},{192,208,224,240},{256,27..., dimensions={0}, use_global_device_ids=true | all-gather | bytes 1290240 | tf_op jit(solution)/shard_map/faces/all_gather | solution.py:69
  77.9 5.7 %fusion.2 = f32[896,896]{1,0:T(8,128)S(1)} fusion(f32[288,896]{1,0:T(8,128)S(1)} %all_gather.12, f32[288,896]{1,0:T(8,128)S(1)} %all_gather.13), kind=kOutput, calls=%fused_computation.16 | convolution fusion | flops 2774532096 | bytes 5275648 | tf_op jit(solution)/shard_map/gram/dot_general | solution.py:46
  87.0 3.7 %collective-permute-done.1 = f32[448,896]{1,0:T(8,128)} collective-permute-done((f32[448,896]{1,0:T(8,128)}, f32[448,896]{1,0:T(8,128)}, u32[]{:S(2)}, u32[]{:S(2)}) %collective-permute-start.1) | collective-permute-done | bytes 1605664 | tf_op jit(solution)/shard_map/gram/ppermute | solution.py:38
  93.5 5.5 %collective-permute-start.2 = (f32[112,896]{1,0:T(8,128)S(1)}, f32[112,896]{1,0:T(8,128)S(1)}, u32[]{:S(2)}, u32[]{:S(2)}) collective-permute-start(f32[112,896]{1,0:T(8,128)S(1)} %get-tuple-element.5), channel_id=1, source_target_pairs={{0,64},{1,65},{64,128},{65,129},{128,192},{129,193},{192,256},{193... | collective-permute-start | bytes 1204232 | tf_op jit(solution)/shard_map/reduce_near/ppermute | solution.py:38
  98.9 3.4 %collective-permute-start.3 = (f32[112,896]{1,0:T(8,128)S(1)}, f32[112,896]{1,0:T(8,128)S(1)}, u32[]{:S(2)}, u32[]{:S(2)}) collective-permute-start(f32[112,896]{1,0:T(8,128)S(1)} %get-tuple-element.6), channel_id=1, source_target_pairs={{0,450},{1,451},{64,0},{65,1},{128,64},{129,65},{192,128},{193,129... | collective-permute-start | bytes 1204232 | tf_op jit(solution)/shard_map/reduce_near/ppermute | solution.py:38
  105.4 6.0 %collective-permute-start.5 = (f32[56,896]{1,0:T(8,128)S(1)}, f32[56,896]{1,0:T(8,128)S(1)}, u32[]{:S(2)}, u32[]{:S(2)}) collective-permute-start(f32[56,896]{1,0:T(8,128)S(1)} %get-tuple-element.8), channel_id=1, source_target_pairs={{0,386},{1,387},{64,450},{65,451},{128,0},{129,1},{192,64},{193,65... | collective-permute-start | bytes 602120 | tf_op jit(solution)/shard_map/reduce_near/ppermute | solution.py:38
  111.4 8.4 %collective-permute-done.4 = f32[56,896]{1,0:T(8,128)S(1)} collective-permute-done((f32[56,896]{1,0:T(8,128)S(1)}, f32[56,896]{1,0:T(8,128)S(1)}, u32[]{:S(2)}, u32[]{:S(2)}) %collective-permute-start.4) | collective-permute-done | bytes 200736 | tf_op jit(solution)/shard_map/reduce_near/ppermute | solution.py:38
  121.5 33.5 %all_to_all.30 = f32[4,28,896]{2,1,0:T(8,128)S(1)} all-to-all(f32[4,28,896]{2,1,0:T(8,128)S(1)} %reshape.28), channel_id=1, replica_groups={{0,256,2,258},{1,257,3,259},{64,320,66,322},{65,321,67,323},{128,384,13..., dimensions={0} | all-to-all | bytes 802816 | tf_op jit(solution)/shard_map/reduce_far/all_to_all | solution.py:88
  155.1 28.8 %all_to_all.31 = f32[4,28,896]{2,1,0:T(8,128)S(1)} all-to-all(f32[4,28,896]{2,1,0:T(8,128)S(1)} %broadcast_in_dim.7), channel_id=1, replica_groups={{0,256,2,258},{1,257,3,259},{64,320,66,322},{65,321,67,323},{128,384,13..., dimensions={0} | all-to-all | bytes 802816 | tf_op jit(solution)/shard_map/gather_far/all_to_all | solution.py:92
  185.8 5.1 %collective-permute-start.7 = (f32[112,896]{1,0:T(8,128)S(1)}, f32[112,896]{1,0:T(8,128)}, u32[]{:S(2)}, u32[]{:S(2)}) collective-permute-start(f32[112,896]{1,0:T(8,128)S(1)} %reshape.29), channel_id=1, source_target_pairs={{0,450},{1,451},{64,0},{65,1},{128,64},{129,65},{192,128},{193,129... | collective-permute-start | bytes 1204232 | tf_op jit(solution)/shard_map/gather_near/ppermute | solution.py:38
  194.3 5.0 %collective-permute-start.9 = (f32[56,896]{1,0:T(8,128)}, f32[56,896]{1,0:T(8,128)S(1)}, u32[]{:S(2)}, u32[]{:S(2)}) collective-permute-start(f32[56,896]{1,0:T(8,128)} %slice.15), channel_id=1, source_target_pairs={{0,128},{1,129},{64,192},{65,193},{128,256},{129,257},{192,320},{1... | collective-permute-start | bytes 602120 | tf_op jit(solution)/shard_map/gather_near/ppermute | solution.py:38
  199.5 5.1 %collective-permute-done.7 = f32[112,896]{1,0:T(8,128)} collective-permute-done((f32[112,896]{1,0:T(8,128)S(1)}, f32[112,896]{1,0:T(8,128)}, u32[]{:S(2)}, u32[]{:S(2)}) %collective-permute-start.7) | collective-permute-done | bytes 401440 | tf_op jit(solution)/shard_map/gather_near/ppermute | solution.py:38
  209.1 16.3 %all-gather.2.cloned.1.call-done = f32[896,896]{1,0:T(8,128)} async-done(((f32[448,896]{1,0:T(8,128)}), f32[896,896]{1,0:T(8,128)}) %all-gather.2.cloned.1.call-update) | async-done | bytes 3211280 | tf_op jit(solution)/shard_map/gather_core/all_gather | solution.py:107
  225.4 5.9 %fusion.3 = f32[896,288]{0,1:T(8,128)S(1)} fusion(f32[896,896]{1,0:T(8,128)} %all-gather.2.cloned.1.call-done, f32[288,896]{1,0:T(8,128)S(1)} %copy-done.2), kind=kOutput, calls=%fused_computation.17 | convolution fusion | flops 2774532096 | bytes 5275648 | tf_op jit(solution)/shard_map/first_product/dot_general | solution.py:46
  231.3 18.9 %all_to_all.32 = f32[4,72,896]{2,1,0:T(8,128)} all-to-all(f32[4,72,896]{2,1,0:T(8,128)S(1)} %bitcast.21), channel_id=1, replica_groups={{0,16,32,48},{64,80,96,112},{128,144,160,176},{192,208,224,240},{256,27..., dimensions={0} | all-to-all | bytes 2064384 | tf_op jit(solution)/shard_map/first_product/all_to_all | solution.py:112
  250.2 2.1 reduce_sum.28
  253.4 13.9 %all_gather.15 = f32[288,896]{1,0:T(8,128)S(1)} all-gather(f32[72,896]{1,0:T(8,128)S(1)} %multiply_add_fusion), channel_id=1, replica_groups={{0,16,32,48},{64,80,96,112},{128,144,160,176},{192,208,224,240},{256,27..., dimensions={0}, use_global_device_ids=true | all-gather | bytes 1290240 | tf_op jit(solution)/shard_map/first_product/all_gather | solution.py:114
  267.2 4.0 %fusion.4 = f32[288,896]{1,0:T(8,128)S(1)} fusion(f32[288,896]{1,0:T(8,128)S(1)} %all_gather.15, f32[896,896]{1,0:T(8,128)S(1)} %copy-done), kind=kOutput, calls=%fused_computation.18 | convolution fusion | flops 2774532096 | bytes 5275648 | tf_op jit(solution)/shard_map/second_product/dot_general | solution.py:46
  271.2 16.7 %all_to_all.33 = f32[4,72,896]{2,1,0:T(8,128)S(1)} all-to-all(f32[4,72,896]{2,1,0:T(8,128)S(1)} %bitcast.20), channel_id=1, replica_groups={{0,4,8,12},{1,5,9,13},{2,6,10,14},{3,7,11,15},{16,20,24,28},{17,21,25,2..., dimensions={0} | all-to-all | bytes 2064384 | tf_op jit(solution)/shard_map/second_product/all_to_all | solution.py:118
  288.3 25.7 %all_to_all.34 = f32[8,72,112]{2,1,0:T(8,128)S(1)} all-to-all(f32[8,72,112]{2,1,0:T(8,128)S(1)} %copy.14), channel_id=1, replica_groups={{0,64,128,192,256,320,384,448},{16,80,144,208,272,336,400,464},{32,96,1..., dimensions={0} | all-to-all | bytes 516096 | tf_op jit(solution)/shard_map/to_blocks/all_to_all | solution.py:122
  (52 shorter events, 24.8 us)
Async XLA Ops:
  8.3 30.4 %all-to-all-start = ((f32[8,72,112]{2,1,0:T(8,128)}), f32[8,72,112]{2,1,0:T(8,128)S(1)}, u32[]{:S(2)}, u32[]{:S(2)}) async-start(f32[8,72,112]{2,1,0:T(8,128)} %bitcast.1), calls=%async_computation | async-start | bytes 589824 | tf_op jit(solution)/shard_map/to_planes/all_to_all | solution.py:64
  20.9 204.5 %all-gather.2.cloned.1.call-start = ((), (), s32[]{:S(2)}) async-start(), calls=%async_computation.6 | async-start | bytes 4816896 | tf_op jit(solution)/shard_map/gather_core/all_gather | solution.py:107
  38.9 23.9 %collective-permute-start = (f32[72,896]{1,0:T(8,128)S(1)}, f32[72,896]{1,0:T(8,128)S(1)}, u32[]{:S(2)}, u32[]{:S(2)}) collective-permute-start(f32[72,896]{1,0:T(8,128)S(1)} %reshape.27), channel_id=1, source_target_pairs={{0,0},{1,1},{64,64},{65,65},{128,128},{129,129},{192,192},{193,193... | collective-permute-start | bytes 774152 | tf_op jit(solution)/shard_map/faces/ppermute | solution.py:38
  62.8 20.9 %copy-start.1 = (f32[288,896]{1,0:T(8,128)}, f32[288,896]{1,0:T(8,128)S(1)}, u32[]{:S(2)}) copy-start(f32[288,896]{1,0:T(8,128)S(1)} %all_gather.12) | copy-start | bytes 3096580
  85.0 5.7 %collective-permute-start.1 = (f32[448,896]{1,0:T(8,128)}, f32[448,896]{1,0:T(8,128)}, u32[]{:S(2)}, u32[]{:S(2)}) collective-permute-start(f32[448,896]{1,0:T(8,128)} %constant_dynamic-slice_fusion.4), channel_id=1, source_target_pairs={{0,1},{1,0},{64,65},{65,64},{128,129},{129,128},{192,193},{193,192... | collective-permute-start | bytes 4816904 | tf_op jit(solution)/shard_map/gram/ppermute | solution.py:38
  92.2 1.2 copy-start.3
  93.5 26.8 %collective-permute-start.2 = (f32[112,896]{1,0:T(8,128)S(1)}, f32[112,896]{1,0:T(8,128)S(1)}, u32[]{:S(2)}, u32[]{:S(2)}) collective-permute-start(f32[112,896]{1,0:T(8,128)S(1)} %get-tuple-element.5), channel_id=1, source_target_pairs={{0,64},{1,65},{64,128},{65,129},{128,192},{129,193},{192,256},{193... | collective-permute-start | bytes 1204232 | tf_op jit(solution)/shard_map/reduce_near/ppermute | solution.py:38
  98.9 21.4 %collective-permute-start.3 = (f32[112,896]{1,0:T(8,128)S(1)}, f32[112,896]{1,0:T(8,128)S(1)}, u32[]{:S(2)}, u32[]{:S(2)}) collective-permute-start(f32[112,896]{1,0:T(8,128)S(1)} %get-tuple-element.6), channel_id=1, source_target_pairs={{0,450},{1,451},{64,0},{65,1},{128,64},{129,65},{192,128},{193,129... | collective-permute-start | bytes 1204232 | tf_op jit(solution)/shard_map/reduce_near/ppermute | solution.py:38
  103.4 16.4 %collective-permute-start.4 = (f32[56,896]{1,0:T(8,128)S(1)}, f32[56,896]{1,0:T(8,128)S(1)}, u32[]{:S(2)}, u32[]{:S(2)}) collective-permute-start(f32[56,896]{1,0:T(8,128)S(1)} %get-tuple-element.7), channel_id=1, source_target_pairs={{0,128},{1,129},{64,192},{65,193},{128,256},{129,257},{192,320},{1... | collective-permute-start | bytes 602120 | tf_op jit(solution)/shard_map/reduce_near/ppermute | solution.py:38
  105.4 15.0 %collective-permute-start.5 = (f32[56,896]{1,0:T(8,128)S(1)}, f32[56,896]{1,0:T(8,128)S(1)}, u32[]{:S(2)}, u32[]{:S(2)}) collective-permute-start(f32[56,896]{1,0:T(8,128)S(1)} %get-tuple-element.8), channel_id=1, source_target_pairs={{0,386},{1,387},{64,450},{65,451},{128,0},{129,1},{192,64},{193,65... | collective-permute-start | bytes 602120 | tf_op jit(solution)/shard_map/reduce_near/ppermute | solution.py:38
  183.9 15.6 %collective-permute-start.6 = (f32[112,896]{1,0:T(8,128)S(1)}, f32[112,896]{1,0:T(8,128)S(1)}, u32[]{:S(2)}, u32[]{:S(2)}) collective-permute-start(f32[112,896]{1,0:T(8,128)S(1)} %reshape.29), channel_id=1, source_target_pairs={{0,64},{1,65},{64,128},{65,129},{128,192},{129,193},{192,256},{193... | collective-permute-start | bytes 1204232 | tf_op jit(solution)/shard_map/gather_near/ppermute | solution.py:38
  185.8 18.9 %collective-permute-start.7 = (f32[112,896]{1,0:T(8,128)S(1)}, f32[112,896]{1,0:T(8,128)}, u32[]{:S(2)}, u32[]{:S(2)}) collective-permute-start(f32[112,896]{1,0:T(8,128)S(1)} %reshape.29), channel_id=1, source_target_pairs={{0,450},{1,451},{64,0},{65,1},{128,64},{129,65},{192,128},{193,129... | collective-permute-start | bytes 1204232 | tf_op jit(solution)/shard_map/gather_near/ppermute | solution.py:38
  191.7 15.2 %collective-permute-start.8 = (f32[56,896]{1,0:T(8,128)}, f32[56,896]{1,0:T(8,128)}, u32[]{:S(2)}, u32[]{:S(2)}) collective-permute-start(f32[56,896]{1,0:T(8,128)} %slice.13), channel_id=1, source_target_pairs={{0,386},{1,387},{64,450},{65,451},{128,0},{129,1},{192,64},{193,65... | collective-permute-start | bytes 602120 | tf_op jit(solution)/shard_map/gather_near/ppermute | solution.py:38
  194.3 13.5 %collective-permute-start.9 = (f32[56,896]{1,0:T(8,128)}, f32[56,896]{1,0:T(8,128)S(1)}, u32[]{:S(2)}, u32[]{:S(2)}) collective-permute-start(f32[56,896]{1,0:T(8,128)} %slice.15), channel_id=1, source_target_pairs={{0,128},{1,129},{64,192},{65,193},{128,256},{129,257},{192,320},{1... | collective-permute-start | bytes 602120 | tf_op jit(solution)/shard_map/gather_near/ppermute | solution.py:38
  199.5 25.9 %copy-start.2 = (f32[288,896]{1,0:T(8,128)S(1)}, f32[288,896]{1,0:T(8,128)}, u32[]{:S(2)}) copy-start(f32[288,896]{1,0:T(8,128)} %copy-done.1) | copy-start | bytes 3096580
  207.9 1.2 copy-start.4
  250.2 17.0 %copy-start = (f32[896,896]{1,0:T(8,128)S(1)}, f32[896,896]{1,0:T(8,128)}, u32[]{:S(2)}) copy-start(f32[896,896]{1,0:T(8,128)} %all-gather.2.cloned.1.call-done) | copy-start | bytes 9633796
  288.0 26.2 %copy-start.5 = (f32[112,576]{1,0:T(8,128)S(1)}, f32[112,576]{1,0:T(8,128)}, u32[]{:S(2)}) copy-start(f32[112,576]{1,0:T(8,128)} %param.1) | copy-start | bytes 774148
Sparse Core Ops, SparseCore 0:
  209.2 16.1 all-gather.1

commit v2 on v0

v2 whole, which is shorter than its diff:
```python
import math

import jax
import jax.numpy as jnp
from jax import lax
from jax.sharding import PartitionSpec as P

M = 3584
N = 9216

PREC = lax.Precision.HIGHEST
COEF_A = 3.4445
COEF_B = -4.775
COEF_C = 2.0315
AXES = ("row", "col")

X_GROUPS = [[zl * 4 + x for x in range(4)] for zl in range(8)]
B_GROUPS = [[(q * 4 + b) * 4 + x for b in range(4)] for q in range(2) for x in range(4)]
Y_GROUPS = [[y * 4 + k for y in range(4)] for k in range(4)]


def device(x, y, z, core):
    return ((z % 8) * 4 + x) * 16 + y * 4 + (z // 8) * 2 + core


CHIPS = [(x, y, z) for x in range(4) for y in range(4) for z in range(16)]
A_GROUPS = [
    [device(x, y, (a * 4 + b), c) for a in range(4)]
    for x in range(4) for y in range(4) for b in range(4) for c in range(2)
]


def permute(value, target):
    pairs = [
        (device(x, y, z, c), device(*target(x, y, z, c))) for x, y, z in CHIPS for c in range(2)
    ]
    return lax.ppermute(value, AXES, pairs)


def swap_q(value):
    return permute(value, lambda x, y, z, c: (x, y, z ^ 4, c))


def swap_core(value):
    return permute(value, lambda x, y, z, c: (x, y, z, 1 - c))


def b_shift(value, step):
    return permute(value, lambda x, y, z, c: (x, y, z // 4 * 4 + (z + step) % 4, c))


def dot(left, right, dims):
    return lax.dot_general(
        left, right, (dims, ((), ())), precision=PREC, preferred_element_type=jnp.float32
    )


def rows_at(value, start, size):
    return lax.dynamic_slice_in_dim(value, start, size, 0)


def ordered(index, own, other):
    return jnp.where(index == 0, own, other), jnp.where(index == 0, other, own)


def body(iterate):
    rows, cols = iterate.shape
    depth = cols // 2
    row, col = lax.axis_index("row"), lax.axis_index("col")
    core = col % 2
    x, b, q = row % 4, row // 4 % 4, row // 16

    with jax.named_scope("swap_columns"):
        flipped = iterate.T
        own = rows_at(flipped, q * depth, depth)
        other = swap_q(rows_at(flipped, (1 - q) * depth, depth))
        block = jnp.concatenate(ordered(q, own, other), 1)
    with jax.named_scope("faces"):
        shifted = [block] + [b_shift(block, s) for s in (1, 2, 3)]
        right = lax.all_gather(block, "row", axis=0, axis_index_groups=X_GROUPS)
        right = right.transpose(1, 0, 2).reshape(depth, 8 * rows)
        left = jnp.zeros((4,) + block.shape, jnp.float32)
        for s in range(4):
            left = lax.dynamic_update_slice_in_dim(left, shifted[s][None], (b + 4 - s) % 4, 0)
        left = left.transpose(1, 0, 2).reshape(depth, 8 * rows)
    size = 8 * rows
    half, chunk = size // 2, size // 8

    with jax.named_scope("gram"):
        partial = dot(left, right, ((0,), (0,)))
        total = rows_at(partial, core * half, half) + swap_core(
            rows_at(partial, (1 - core) * half, half)
        )
    with jax.named_scope("reduce_y"):
        parts = lax.all_to_all(
            total.reshape(4, chunk, size), "col", 0, 0, axis_index_groups=Y_GROUPS
        )
        near = jnp.sum(parts, 0)
    with jax.named_scope("reduce_a"):
        parts = near.reshape(4, chunk // 4, size)
        parts = lax.all_to_all(parts, AXES, 0, 0, axis_index_groups=A_GROUPS)
        piece = jnp.sum(parts, 0)
    with jax.named_scope("gather_a"):
        parts = jnp.broadcast_to(piece, (4,) + piece.shape)
        parts = lax.all_to_all(parts, AXES, 0, 0, axis_index_groups=A_GROUPS)
        near = parts.reshape(chunk, size)
    with jax.named_scope("gather_y"):
        parts = jnp.broadcast_to(near, (4,) + near.shape)
        parts = lax.all_to_all(parts, "col", 0, 0, axis_index_groups=Y_GROUPS)
        total = parts.reshape(half, size)
    with jax.named_scope("gather_core"):
        gram = jnp.concatenate(ordered(core, total, swap_core(total)), 0)

    with jax.named_scope("first_product"):
        product = dot(left, gram, ((1,), (0,)))
        parts = product.reshape(4, depth // 4, size)
        parts = lax.all_to_all(parts, "row", 0, 0, axis_index_groups=X_GROUPS)
        mine = rows_at(right, x * (depth // 4), depth // 4)
        inner = COEF_B * mine + COEF_C * jnp.sum(parts, 0)
        inner = lax.all_gather(inner, "row", axis=0, tiled=True, axis_index_groups=X_GROUPS)
    with jax.named_scope("second_product"):
        product = dot(inner, gram, ((1,), (1,)))
        parts = product.reshape(depth, 4, 2 * rows).transpose(1, 0, 2)
        parts = lax.all_to_all(parts, "row", 0, 0, axis_index_groups=B_GROUPS)
        applied = jnp.sum(parts, 0)
    with jax.named_scope("swap_back"):
        first, second = applied[:, :rows], applied[:, rows:]
        own, other = ordered(q, first, second)
        applied = jnp.concatenate(ordered(q, own, swap_q(other)), 0).T
    return (COEF_A * iterate + applied) * (0.2 * math.sqrt(max(M, N)))


def solution(mesh):
    placed = (P("row", "col"),)
    return jax.shard_map(
        body, mesh=mesh, in_specs=placed, out_specs=P("row", "col"), check_vma=False
    )
```

time: 900 us -> 315 us (0.35)
  waiting for transfers between devices: 855 us -> 55.1 us
  blocking collectives: 0 us -> 158 us
  starting transfers between devices: 0.3 us -> 45.8 us
  local copies, waits for them, and re-layouts: 2.41 us -> 30.3 us
  between operations: 13.1 us -> 0.45 us
  matrix products: 28.7 us -> 17 us
    all_gather x3 -> x0, waiting for transfers between devices: 549 us -> none  [the longest x1 228 us: body(): slab_all = lax.all_gather(iterate, 'row', axis=0, tiled=True)]
    psum x1 -> x0, waiting for transfers between devices: 306 us -> none  [body(): gram_panel = lax.psum(partial_value, 'col')]
    all_to_all x0 -> x5, blocking collectives: none -> 132 us  [the longest x2 48.2 us: body(): parts = lax.all_to_all(parts, AXES, 0, 0, axis_index_groups=A_GROUPS)]
    ppermute x0 -> x7, waiting for transfers between devices: none -> 40.7 us  [permute(): return lax.ppermute(value, AXES, pairs)]
    ppermute x0 -> x7, starting transfers between devices: none -> 33.1 us  [permute(): return lax.ppermute(value, AXES, pairs)]
    all_gather x0 -> x2, blocking collectives: none -> 26.2 us  [the longest x1 14.1 us: body(): right = lax.all_gather(block, 'row', axis=0, axis_index_groups=X_GROUPS)]
    dynamic_update_slice x0 -> x4, local copies, waits for them, and re-layouts: none -> 16.9 us  [body(): lax.dynamic_update_slice_in_dim(left, shifted[s][None], (b + 4 - s) % 4, 0)]
    all_to_all x0 -> x1, waiting for transfers between devices: none -> 14.4 us  [body(): parts = lax.all_to_all(parts, 'row', 0, 0, axis_index_groups=X_GROUPS)]
  transfers between devices with their start and end apart: 4 -> 8, of which waited for: 4 -> 6; matrix products, arithmetic and copies ran while one was open for 0% -> 3% of each run, Pallas kernels for 0% -> 0%
where the time goes in v2:
time: 315 us
  blocking collectives  158 us (50%)
  waiting for transfers between devices  55.1 us (17%)
  starting transfers between devices  45.8 us (15%)
  local copies, waits for them, and re-layouts  30.3 us (10%)
  matrix products  17 us (5%)
  other arithmetic  8.21 us (3%)
    all_to_all x2, blocking collectives, body(): parts = lax.all_to_all(parts, AXES, 0, 0, axis_index_groups=A_GROUPS)  48.2 us
    all_to_all x1, blocking collectives, body(): parts = lax.all_to_all(parts, 'row', 0, 0, axis_index_groups=B_GROUPS)  40.7 us
    ppermute x7, waiting for transfers between devices, permute(): return lax.ppermute(value, AXES, pairs)  40.7 us
    ppermute x7, starting transfers between devices, permute(): return lax.ppermute(value, AXES, pairs)  33.1 us
    all_to_all x1, blocking collectives, body(): lax.all_to_all(total.reshape(4, chunk, size), 'col', 0, 0, axis_index_gro...  24.5 us
    all_to_all x1, blocking collectives, body(): parts = lax.all_to_all(parts, 'col', 0, 0, axis_index_groups=Y_GROUPS)  18.2 us
    dot_general x3, matrix products, dot(): lax.dot_general(left, right, (dims, ((), ())), precision=PREC, preferred_...  17 us
    dynamic_update_slice x4, local copies, waits for them, and re-layouts, body(): lax.dynamic_update_slice_in_dim(left, shifted[s][None], (b + 4 - s) % 4, 0)  16.9 us
  transfers between devices with their start and end apart: 8, of which 6 were waited for; matrix products, arithmetic and copies ran while one was open for 3% of the time, Pallas kernels for 0%

profile of v2, /device:TPU:1, one launch (start us, length us, event | category | flops | bytes accessed | tf_op | source)
XLA Modules:
  0.0 314.6 jit_solution(733847305591531241)
XLA Ops:
  1.0 9.7 %collective-permute-start = (f32[288,112]{0,1:T(8,128)S(1)}, f32[288,112]{0,1:T(8,128)S(1)}, u32[]{:S(2)}, u32[]{:S(2)}) collective-permute-start(f32[288,112]{0,1:T(8,128)S(1)} %dynamic-slice_bitcast_fusion), channel_id=1, source_target_pairs={{0,256},{1,257},{64,320},{65,321},{128,384},{129,385},{192,448},{1... | collective-permute-start | bytes 387080 | tf_op jit(solution)/shard_map/swap_columns/ppermute | solution.py:37
  10.8 14.3 %collective-permute-done = f32[288,112]{0,1:T(8,128)S(1)} collective-permute-done((f32[288,112]{0,1:T(8,128)S(1)}, f32[288,112]{0,1:T(8,128)S(1)}, u32[]{:S(2)}, u32[]{:S(2)}) %collective-permute-start) | collective-permute-done | bytes 129056 | tf_op jit(solution)/shard_map/swap_columns/ppermute | solution.py:37
  26.4 5.6 %collective-permute-start.3 = (f32[288,224]{0,1:T(8,128)S(1)}, f32[288,224]{0,1:T(8,128)S(1)}, u32[]{:S(2)}, u32[]{:S(2)}) collective-permute-start(f32[288,224]{0,1:T(8,128)S(1)} %get-tuple-element.11), channel_id=1, source_target_pairs={{0,192},{1,193},{64,0},{65,1},{128,64},{129,65},{192,128},{193,129... | collective-permute-start | bytes 774152 | tf_op jit(solution)/shard_map/faces/ppermute | solution.py:37
  36.3 14.1 %all-gather = f32[1152,224]{1,0:T(8,128)S(1)} all-gather(f32[288,224]{1,0:T(8,128)S(1)} %copy.28), channel_id=2, replica_groups={{0,16,32,48},{64,80,96,112},{128,144,160,176},{192,208,224,240},{256,27..., dimensions={0}, use_global_device_ids=true | all-gather | bytes 1290240 | tf_op jit(solution)/shard_map/faces/all_gather | solution.py:80
  53.0 4.2 %dynamic_update_slice.12 = f32[4,288,224]{2,0,1:T(4,128)S(1)} dynamic-update-slice(f32[4,288,224]{2,0,1:T(4,128)S(1)} %broadcast_in_dim.19, f32[1,288,224]{2,0,1:T(1,128)S(1)} %copy.30, s32[]{:T(128)S(6)} %select_n.116, s32[]{:T(128)} %constant.87.clone.1, s32[]{:T(128)} %constant.87.clone.1) | dynamic-update-slice | bytes 516100 | tf_op jit(solution)/shard_map/faces/dynamic_update_slice | solution.py:84
  58.8 4.2 %dynamic_update_slice.13 = f32[4,288,224]{2,0,1:T(4,128)S(1)} dynamic-update-slice(f32[4,288,224]{2,0,1:T(4,128)S(1)} %dynamic_update_slice.12, f32[1,288,224]{2,0,1:T(1,128)S(1)} %copy.31, s32[]{:T(128)S(6)} %select_n.118, s32[]{:T(128)} %constant.87.clone.1, s32[]{:T(128)} %constant.87.clone.1) | dynamic-update-slice | bytes 516100 | tf_op jit(solution)/shard_map/faces/dynamic_update_slice | solution.py:84
  63.0 4.2 %dynamic_update_slice.14 = f32[4,288,224]{2,0,1:T(4,128)S(1)} dynamic-update-slice(f32[4,288,224]{2,0,1:T(4,128)S(1)} %dynamic_update_slice.13, f32[1,288,224]{2,0,1:T(1,128)S(1)} %copy.32, s32[]{:T(128)S(6)} %select_n.120, s32[]{:T(128)} %constant.87.clone.1, s32[]{:T(128)} %constant.87.clone.1) | dynamic-update-slice | bytes 516100 | tf_op jit(solution)/shard_map/faces/dynamic_update_slice | solution.py:84
  67.3 4.2 %dynamic_update_slice.15 = f32[4,288,224]{2,0,1:T(4,128)S(1)} dynamic-update-slice(f32[4,288,224]{2,0,1:T(4,128)S(1)} %dynamic_update_slice.14, f32[1,288,224]{2,0,1:T(1,128)S(1)} %copy.33, s32[]{:T(128)S(6)} %select_n.122, s32[]{:T(128)} %constant.87.clone.1, s32[]{:T(128)} %constant.87.clone.1) | dynamic-update-slice | bytes 516100 | tf_op jit(solution)/shard_map/faces/dynamic_update_slice | solution.py:84
  74.3 7.1 %fusion.9 = f32[896,896]{1,0:T(8,128)S(1)} fusion(f32[288,896]{1,0:T(8,128)} %reshape.25, f32[288,896]{1,0:T(8,128)} %reshape.24), kind=kOutput, calls=%fused_computation.25 | convolution fusion | flops 2774532096 | bytes 5275648 | tf_op jit(solution)/shard_map/gram/dot_general | solution.py:53
  82.6 3.5 %collective-permute-start.4 = (f32[448,896]{1,0:T(8,128)}, f32[448,896]{1,0:T(8,128)}, u32[]{:S(2)}, u32[]{:S(2)}) collective-permute-start(f32[448,896]{1,0:T(8,128)} %constant_dynamic-slice_fusion), channel_id=1, source_target_pairs={{0,1},{1,0},{64,65},{65,64},{128,129},{129,128},{192,193},{193,192... | collective-permute-start | bytes 4816904 | tf_op jit(solution)/shard_map/gram/ppermute | solution.py:37
  86.2 3.4 %collective-permute-done.4 = f32[448,896]{1,0:T(8,128)} collective-permute-done((f32[448,896]{1,0:T(8,128)}, f32[448,896]{1,0:T(8,128)}, u32[]{:S(2)}, u32[]{:S(2)}) %collective-permute-start.4) | collective-permute-done | bytes 1605664 | tf_op jit(solution)/shard_map/gram/ppermute | solution.py:37
  91.2 24.5 %all_to_all.30 = f32[4,112,896]{2,1,0:T(8,128)S(1)} all-to-all(f32[4,112,896]{2,1,0:T(8,128)S(1)} %bitcast.36), channel_id=1, replica_groups={{0,4,8,12},{1,5,9,13},{2,6,10,14},{3,7,11,15},{16,20,24,28},{17,21,25,2..., dimensions={0} | all-to-all | bytes 3211264 | tf_op jit(solution)/shard_map/reduce_y/all_to_all | solution.py:95
  115.8 28.0 %all_to_all.31 = f32[4,28,896]{2,1,0:T(8,128)S(1)} all-to-all(f32[4,28,896]{2,1,0:T(8,128)S(1)} %reshape.27), channel_id=1, replica_groups={{0,256,2,258},{1,257,3,259},{64,320,66,322},{65,321,67,323},{128,384,13..., dimensions={0} | all-to-all | bytes 802816 | tf_op jit(solution)/shard_map/reduce_a/all_to_all | solution.py:101
  143.9 20.2 %all_to_all.32 = f32[4,28,896]{2,1,0:T(8,128)S(1)} all-to-all(f32[4,28,896]{2,1,0:T(8,128)S(1)} %broadcast_in_dim.23), channel_id=1, replica_groups={{0,256,2,258},{1,257,3,259},{64,320,66,322},{65,321,67,323},{128,384,13..., dimensions={0} | all-to-all | bytes 802816 | tf_op jit(solution)/shard_map/gather_a/all_to_all | solution.py:105
  164.3 18.2 %all_to_all.33 = f32[4,112,896]{2,1,0:T(8,128)S(1)} all-to-all(f32[4,112,896]{2,1,0:T(8,128)S(1)} %broadcast_in_dim.24), channel_id=1, replica_groups={{0,4,8,12},{1,5,9,13},{2,6,10,14},{3,7,11,15},{16,20,24,28},{17,21,25,2..., dimensions={0} | all-to-all | bytes 3211264 | tf_op jit(solution)/shard_map/gather_y/all_to_all | solution.py:109
  182.4 8.3 %collective-permute-start.5 = (f32[448,896]{1,0:T(8,128)S(1)}, f32[448,896]{1,0:T(8,128)}, u32[]{:S(2)}, u32[]{:S(2)}) collective-permute-start(f32[448,896]{1,0:T(8,128)S(1)} %bitcast.37), channel_id=1, source_target_pairs={{0,1},{1,0},{64,65},{65,64},{128,129},{129,128},{192,193},{193,192... | collective-permute-start | bytes 4816904 | tf_op jit(solution)/shard_map/gather_core/ppermute | solution.py:37
  196.1 5.0 %fusion = f32[4,72,896]{2,1,0:T(8,128)} fusion(f32[4,72,896]{2,1,0:T(8,128)S(1)} %copy-done.3, f32[448,896]{1,0:T(8,128)S(1)} %get-tuple-element.6, f32[448,896]{1,0:T(8,128)S(1)} %get-tuple-element.5), kind=kOutput, calls=%fused_computation.1 | convolution fusion | flops 2775334912 | bytes 5275648 | tf_op jit(solution)/shard_map/first_product/dot_general | solution.py:53
  201.0 12.7 %all-to-all-start.4 = ((f32[4,72,896]{2,1,0:T(8,128)}), f32[4,72,896]{2,1,0:T(8,128)}, u32[]{:S(2)}, u32[]{:S(2)}) async-start(f32[4,72,896]{2,1,0:T(8,128)} %fusion), calls=%async_computation.4 | async-start | bytes 2064384 | tf_op jit(solution)/shard_map/first_product/all_to_all | solution.py:117
  213.7 14.4 %all-to-all-done.4 = f32[4,72,896]{2,1,0:T(8,128)} async-done(((f32[4,72,896]{2,1,0:T(8,128)}), f32[4,72,896]{2,1,0:T(8,128)}, u32[]{:S(2)}, u32[]{:S(2)}) %all-to-all-start.4) | async-done | bytes 1032224 | tf_op jit(solution)/shard_map/first_product/all_to_all | solution.py:117
  230.4 12.1 %all_gather.11 = f32[288,896]{1,0:T(8,128)S(1)} all-gather(f32[72,896]{1,0:T(8,128)S(1)} %multiply_add_fusion), channel_id=1, replica_groups={{0,16,32,48},{64,80,96,112},{128,144,160,176},{192,208,224,240},{256,27..., dimensions={0}, use_global_device_ids=true | all-gather | bytes 1290240 | tf_op jit(solution)/shard_map/first_product/all_gather | solution.py:120
  242.5 5.0 %fusion.2 = f32[288,896]{1,0:T(8,128)} fusion(f32[288,896]{1,0:T(8,128)S(1)} %all_gather.11, f32[448,896]{1,0:T(8,128)S(1)} %get-tuple-element.6, f32[448,896]{1,0:T(8,128)S(1)} %get-tuple-element.5), kind=kOutput, calls=%fused_computation.3 | convolution fusion | flops 2775334912 | bytes 5275648 | tf_op jit(solution)/shard_map/second_product/dot_general | solution.py:53
  247.5 2.3 reshape.30
  250.1 40.7 %all_to_all.34 = f32[4,288,224]{2,1,0:T(8,128)S(1)} all-to-all(f32[4,288,224]{2,1,0:T(8,128)S(1)} %bitcast.39), channel_id=1, replica_groups={{0,64,128,192},{16,80,144,208},{32,96,160,224},{48,112,176,240},{256,32..., dimensions={0} | all-to-all | bytes 2064384 | tf_op jit(solution)/shard_map/second_product/all_to_all | solution.py:124
  293.2 20.5 %collective-permute-done.6 = f32[288,112]{0,1:T(8,128)S(1)} collective-permute-done((f32[288,112]{0,1:T(8,128)S(1)}, f32[288,112]{0,1:T(8,128)S(1)}, u32[]{:S(2)}, u32[]{:S(2)}) %collective-permute-start.6) | collective-permute-done | bytes 129056 | tf_op jit(solution)/shard_map/swap_back/ppermute | solution.py:37
  (49 shorter events, 27.7 us)
Async XLA Ops:
  1.0 24.1 %collective-permute-start = (f32[288,112]{0,1:T(8,128)S(1)}, f32[288,112]{0,1:T(8,128)S(1)}, u32[]{:S(2)}, u32[]{:S(2)}) collective-permute-start(f32[288,112]{0,1:T(8,128)S(1)} %dynamic-slice_bitcast_fusion), channel_id=1, source_target_pairs={{0,256},{1,257},{64,320},{65,321},{128,384},{129,385},{192,448},{1... | collective-permute-start | bytes 387080 | tf_op jit(solution)/shard_map/swap_columns/ppermute | solution.py:37
  26.4 30.8 %collective-permute-start.3 = (f32[288,224]{0,1:T(8,128)S(1)}, f32[288,224]{0,1:T(8,128)S(1)}, u32[]{:S(2)}, u32[]{:S(2)}) collective-permute-start(f32[288,224]{0,1:T(8,128)S(1)} %get-tuple-element.11), channel_id=1, source_target_pairs={{0,192},{1,193},{64,0},{65,1},{128,64},{129,65},{192,128},{193,129... | collective-permute-start | bytes 774152 | tf_op jit(solution)/shard_map/faces/ppermute | solution.py:37
  32.0 26.4 %collective-permute-start.2 = (f32[288,224]{0,1:T(8,128)S(1)}, f32[288,224]{0,1:T(8,128)S(1)}, u32[]{:S(2)}, u32[]{:S(2)}) collective-permute-start(f32[288,224]{0,1:T(8,128)S(1)} %get-tuple-element.11), channel_id=1, source_target_pairs={{0,128},{1,129},{64,192},{65,193},{128,0},{129,1},{192,64},{193,65... | collective-permute-start | bytes 774152 | tf_op jit(solution)/shard_map/faces/ppermute | solution.py:37
  33.9 24.7 %collective-permute-start.1 = (f32[288,224]{0,1:T(8,128)S(1)}, f32[288,224]{0,1:T(8,128)S(1)}, u32[]{:S(2)}, u32[]{:S(2)}) collective-permute-start(f32[288,224]{0,1:T(8,128)S(1)} %get-tuple-element.11), channel_id=1, source_target_pairs={{0,64},{1,65},{64,128},{65,129},{128,192},{129,193},{192,0},{193,1... | collective-permute-start | bytes 774152 | tf_op jit(solution)/shard_map/faces/ppermute | solution.py:37
  71.5 1.0 copy-start
  82.6 6.9 %collective-permute-start.4 = (f32[448,896]{1,0:T(8,128)}, f32[448,896]{1,0:T(8,128)}, u32[]{:S(2)}, u32[]{:S(2)}) collective-permute-start(f32[448,896]{1,0:T(8,128)} %constant_dynamic-slice_fusion), channel_id=1, source_target_pairs={{0,1},{1,0},{64,65},{65,64},{128,129},{129,128},{192,193},{193,192... | collective-permute-start | bytes 4816904 | tf_op jit(solution)/shard_map/gram/ppermute | solution.py:37
  164.3 26.5 %copy-start.1 = (f32[4,288,224]{2,0,1:T(4,128)S(1)}, f32[4,288,224]{2,0,1:T(4,128)}, u32[]{:S(2)}) copy-start(f32[4,288,224]{2,0,1:T(4,128)} %copy-done) | copy-start | bytes 3096580
  182.4 10.1 %copy-start.2 = (f32[4,112,896]{2,1,0:T(8,128)}, f32[4,112,896]{2,1,0:T(8,128)S(1)}, u32[]{:S(2)}) copy-start(f32[4,112,896]{2,1,0:T(8,128)S(1)} %all_to_all.33) | copy-start | bytes 4816900
  182.4 11.5 %collective-permute-start.5 = (f32[448,896]{1,0:T(8,128)S(1)}, f32[448,896]{1,0:T(8,128)}, u32[]{:S(2)}, u32[]{:S(2)}) collective-permute-start(f32[448,896]{1,0:T(8,128)S(1)} %bitcast.37), channel_id=1, source_target_pairs={{0,1},{1,0},{64,65},{65,64},{128,129},{129,128},{192,193},{193,192... | collective-permute-start | bytes 4816904 | tf_op jit(solution)/shard_map/gather_core/ppermute | solution.py:37
  192.5 3.5 %copy-start.3 = (f32[4,72,896]{2,1,0:T(8,128)S(1)}, f32[4,72,896]{2,1,0:T(8,128)}, u32[]{:S(2)}) copy-start(f32[4,72,896]{2,1,0:T(8,128)} %dot_general.11) | copy-start | bytes 3096580
  201.0 27.1 %all-to-all-start.4 = ((f32[4,72,896]{2,1,0:T(8,128)}), f32[4,72,896]{2,1,0:T(8,128)}, u32[]{:S(2)}, u32[]{:S(2)}) async-start(f32[4,72,896]{2,1,0:T(8,128)} %fusion), calls=%async_computation.4 | async-start | bytes 2064384 | tf_op jit(solution)/shard_map/first_product/all_to_all | solution.py:117
  290.9 22.9 %copy-start.4 = (f32[112,576]{1,0:T(8,128)S(1)}, f32[112,576]{1,0:T(8,128)}, u32[]{:S(2)}) copy-start(f32[112,576]{1,0:T(8,128)} %param.1) | copy-start | bytes 774148
  291.3 22.5 %collective-permute-start.6 = (f32[288,112]{0,1:T(8,128)S(1)}, f32[288,112]{0,1:T(8,128)S(1)}, u32[]{:S(2)}, u32[]{:S(2)}) collective-permute-start(f32[288,112]{0,1:T(8,128)S(1)} %broadcast_select_fusion.4), channel_id=1, source_target_pairs={{0,256},{1,257},{64,320},{65,321},{128,384},{129,385},{192,448},{1... | collective-permute-start | bytes 387080 | tf_op jit(solution)/shard_map/swap_back/ppermute | solution.py:37

commit v3 on v2

--- a/solution.py
+++ b/solution.py
@@ -3,6 +3,7 @@
 import jax
 import jax.numpy as jnp
 from jax import lax
+from jax.experimental.layout import Layout, with_layout_constraint
 from jax.sharding import PartitionSpec as P
 
 M = 3584
@@ -15,7 +16,6 @@
 AXES = ("row", "col")
 
 X_GROUPS = [[zl * 4 + x for x in range(4)] for zl in range(8)]
-B_GROUPS = [[(q * 4 + b) * 4 + x for b in range(4)] for q in range(2) for x in range(4)]
 Y_GROUPS = [[y * 4 + k for y in range(4)] for k in range(4)]
 
 
@@ -59,6 +59,10 @@
     return lax.dynamic_slice_in_dim(value, start, size, 0)
 
 
+def in_rows(value):
+    return with_layout_constraint(value, Layout(major_to_minor=(0, 1)))
+
+
 def ordered(index, own, other):
     return jnp.where(index == 0, own, other), jnp.where(index == 0, other, own)
 
@@ -68,29 +72,32 @@
     depth = cols // 2
     row, col = lax.axis_index("row"), lax.axis_index("col")
     core = col % 2
-    x, b, q = row % 4, row // 4 % 4, row // 16
+    x, q = row % 4, row // 16
 
     with jax.named_scope("swap_columns"):
-        flipped = iterate.T
-        own = rows_at(flipped, q * depth, depth)
-        other = swap_q(rows_at(flipped, (1 - q) * depth, depth))
-        block = jnp.concatenate(ordered(q, own, other), 1)
+        flipped = in_rows(iterate.T)
+        own = in_rows(rows_at(flipped, q * depth, depth))
+        other = in_rows(swap_q(in_rows(rows_at(flipped, (1 - q) * depth, depth))))
     with jax.named_scope("faces"):
-        shifted = [block] + [b_shift(block, s) for s in (1, 2, 3)]
-        right = lax.all_gather(block, "row", axis=0, axis_index_groups=X_GROUPS)
+        lefts = []
+        for s in range(4):
+            parts = (own, other) if s == 0 else (b_shift(own, s), b_shift(other, s))
+            lefts.append(jnp.concatenate(ordered(q, *parts), 1))
+        near = jnp.concatenate(lefts[:2], 1)
+        far = jnp.concatenate(lefts[2:], 1)
+        kept, given = ordered(core, near, far)
+        right = [
+            lax.all_gather(part, "row", axis=0, axis_index_groups=X_GROUPS)
+            for part in (own, other)
+        ]
+        right = jnp.concatenate(ordered(q, *right), 0)
         right = right.transpose(1, 0, 2).reshape(depth, 8 * rows)
-        left = jnp.zeros((4,) + block.shape, jnp.float32)
-        for s in range(4):
-            left = lax.dynamic_update_slice_in_dim(left, shifted[s][None], (b + 4 - s) % 4, 0)
-        left = left.transpose(1, 0, 2).reshape(depth, 8 * rows)
     size = 8 * rows
     half, chunk = size // 2, size // 8
 
     with jax.named_scope("gram"):
-        partial = dot(left, right, ((0,), (0,)))
-        total = rows_at(partial, core * half, half) + swap_core(
-            rows_at(partial, (1 - core) * half, half)
-        )
+        partial = swap_core(dot(given, right, ((0,), (0,))))
+        total = dot(kept, right, ((0,), (0,))) + partial
     with jax.named_scope("reduce_y"):
         parts = lax.all_to_all(
             total.reshape(4, chunk, size), "col", 0, 0, axis_index_groups=Y_GROUPS
@@ -107,26 +114,33 @@
     with jax.named_scope("gather_y"):
         parts = jnp.broadcast_to(near, (4,) + near.shape)
         parts = lax.all_to_all(parts, "col", 0, 0, axis_index_groups=Y_GROUPS)
-        total = parts.reshape(half, size)
+        gram_kept = parts.reshape(half, size)
     with jax.named_scope("gather_core"):
-        gram = jnp.concatenate(ordered(core, total, swap_core(total)), 0)
+        gram_given = swap_core(gram_kept)
 
     with jax.named_scope("first_product"):
-        product = dot(left, gram, ((1,), (0,)))
+        product = dot(kept, gram_kept, ((1,), (0,))) + dot(given, gram_given, ((1,), (0,)))
         parts = product.reshape(4, depth // 4, size)
         parts = lax.all_to_all(parts, "row", 0, 0, axis_index_groups=X_GROUPS)
         mine = rows_at(right, x * (depth // 4), depth // 4)
         inner = COEF_B * mine + COEF_C * jnp.sum(parts, 0)
         inner = lax.all_gather(inner, "row", axis=0, tiled=True, axis_index_groups=X_GROUPS)
     with jax.named_scope("second_product"):
-        product = dot(inner, gram, ((1,), (1,)))
-        parts = product.reshape(depth, 4, 2 * rows).transpose(1, 0, 2)
-        parts = lax.all_to_all(parts, "row", 0, 0, axis_index_groups=B_GROUPS)
-        applied = jnp.sum(parts, 0)
+        near, far = ordered(
+            core,
+            in_rows(dot(inner, gram_kept, ((1,), (1,)))),
+            in_rows(dot(inner, gram_given, ((1,), (1,)))),
+        )
+        sums = []
+        for part in (1 - q, q):
+            blocks = []
+            for s in range(4):
+                value = (near, far)[s // 2][:, s % 2 * 2 * rows :][:, : 2 * rows]
+                block = in_rows(jnp.where(part == 0, value[:, :rows], value[:, rows:]))
+                blocks.append(b_shift(block, -s) if s else block)
+            sums.append(blocks[0] + blocks[1] + blocks[2] + blocks[3])
     with jax.named_scope("swap_back"):
-        first, second = applied[:, :rows], applied[:, rows:]
-        own, other = ordered(q, first, second)
-        applied = jnp.concatenate(ordered(q, own, swap_q(other)), 0).T
+        applied = jnp.concatenate(ordered(q, sums[1], swap_q(sums[0])), 0).T
     return (COEF_A * iterate + applied) * (0.2 * math.sqrt(max(M, N)))
 
 

time: 315 us -> 308 us (0.978)
  the two profiles are of different devices: /device:TPU:1 before, /device:TPU:32 now
where the time goes in v3:
time: 308 us; the launch traced here: 307 us
  blocking collectives  161 us (52%)
  starting transfers between devices  67.7 us (22%)
  waiting for transfers between devices  52.2 us (17%)
  matrix products  17 us (6%)
  local copies, waits for them, and re-layouts  5.54 us (2%)
  other arithmetic  3.36 us (1%)
    all_to_all x2, blocking collectives, body(): parts = lax.all_to_all(parts, AXES, 0, 0, axis_index_groups=A_GROUPS)  73.9 us
    ppermute x16, starting transfers between devices, permute(): return lax.ppermute(value, AXES, pairs)  63.4 us
    ppermute x16, waiting for transfers between devices, permute(): return lax.ppermute(value, AXES, pairs)  36.7 us
    all_gather x2, blocking collectives, body(): lax.all_gather(part, 'row', axis=0, axis_index_groups=X_GROUPS)  26.4 us
    all_to_all x1, blocking collectives, body(): lax.all_to_all(total.reshape(4, chunk, size), 'col', 0, 0, axis_index_gro...  25.6 us
    all_to_all x1, blocking collectives, body(): parts = lax.all_to_all(parts, 'col', 0, 0, axis_index_groups=Y_GROUPS)  19.6 us
    dot_general x6, matrix products, dot(): lax.dot_general(left, right, (dims, ((), ())), precision=PREC, preferred_...  17 us
    all_to_all x1, waiting for transfers between devices, body(): parts = lax.all_to_all(parts, 'row', 0, 0, axis_index_groups=X_GROUPS)  15.5 us
  transfers between devices with their start and end apart: 17, of which 9 were waited for; matrix products, arithmetic and copies ran while one was open for 1% of the time, Pallas kernels for 0%

profile of v3, /device:TPU:32, one launch (start us, length us, event | category | flops | bytes accessed | tf_op | source)
XLA Modules:
  0.0 306.9 jit_solution(8502859501655106560)
XLA Ops:
  1.1 9.1 %collective-permute-start = (f32[288,112]{1,0:T(8,128)S(1)}, f32[288,112]{1,0:T(8,128)S(1)}, u32[]{:S(2)}, u32[]{:S(2)}) collective-permute-start(f32[288,112]{1,0:T(8,128)S(1)} %constant_dynamic-slice_fusion), channel_id=1, source_target_pairs={{0,256},{1,257},{64,320},{65,321},{128,384},{129,385},{192,448},{1... | collective-permute-start | bytes 387080 | tf_op jit(solution)/shard_map/swap_columns/ppermute | solution.py:37
  10.3 10.2 %collective-permute-done = f32[288,112]{1,0:T(8,128)S(1)} collective-permute-done((f32[288,112]{1,0:T(8,128)S(1)}, f32[288,112]{1,0:T(8,128)S(1)}, u32[]{:S(2)}, u32[]{:S(2)}) %collective-permute-start) | collective-permute-done | bytes 129056 | tf_op jit(solution)/shard_map/swap_columns/ppermute | solution.py:37
  22.7 7.2 %collective-permute-start.3 = (f32[288,112]{1,0:T(8,128)S(1)}, f32[288,112]{1,0:T(8,128)S(1)}, u32[]{:S(2)}, u32[]{:S(2)}) collective-permute-start(f32[288,112]{1,0:T(8,128)S(1)} %get-tuple-element.8), channel_id=1, source_target_pairs={{0,128},{1,129},{64,192},{65,193},{128,0},{129,1},{192,64},{193,65... | collective-permute-start | bytes 387080 | tf_op jit(solution)/shard_map/faces/ppermute | solution.py:37
  32.5 13.5 %all-gather = f32[1152,112]{1,0:T(8,128)S(1)} all-gather(f32[288,112]{1,0:T(8,128)S(1)} %get-tuple-element.8), channel_id=2, replica_groups={{0,16,32,48},{64,80,96,112},{128,144,160,176},{192,208,224,240},{256,27..., dimensions={0}, use_global_device_ids=true | all-gather | bytes 645120 | tf_op jit(solution)/shard_map/faces/all_gather | solution.py:90
  46.0 12.9 %all-gather.1 = f32[1152,112]{1,0:T(8,128)S(1)} all-gather(f32[288,112]{1,0:T(8,128)S(1)} %collective-permute-done), channel_id=3, replica_groups={{0,16,32,48},{64,80,96,112},{128,144,160,176},{192,208,224,240},{256,27..., dimensions={0}, use_global_device_ids=true | all-gather | bytes 645120 | tf_op jit(solution)/shard_map/faces/all_gather | solution.py:90
  62.4 4.6 %collective-permute-start.2 = (f32[288,112]{1,0:T(8,128)S(1)}, f32[288,112]{1,0:T(8,128)S(1)}, u32[]{:S(2)}, u32[]{:S(2)}) collective-permute-start(f32[288,112]{1,0:T(8,128)S(1)} %collective-permute-done), channel_id=1, source_target_pairs={{0,64},{1,65},{64,128},{65,129},{128,192},{129,193},{192,0},{193,1... | collective-permute-start | bytes 387080 | tf_op jit(solution)/shard_map/faces/ppermute | solution.py:37
  67.0 5.6 %collective-permute-done.2 = f32[288,112]{1,0:T(8,128)S(1)} collective-permute-done((f32[288,112]{1,0:T(8,128)S(1)}, f32[288,112]{1,0:T(8,128)S(1)}, u32[]{:S(2)}, u32[]{:S(2)}) %collective-permute-start.2) | collective-permute-done | bytes 129056 | tf_op jit(solution)/shard_map/faces/ppermute | solution.py:37
  72.6 4.4 %collective-permute-start.6 = (f32[288,112]{1,0:T(8,128)S(1)}, f32[288,112]{1,0:T(8,128)S(1)}, u32[]{:S(2)}, u32[]{:S(2)}) collective-permute-start(f32[288,112]{1,0:T(8,128)S(1)} %collective-permute-done), channel_id=1, source_target_pairs={{0,192},{1,193},{64,0},{65,1},{128,64},{129,65},{192,128},{193,129... | collective-permute-start | bytes 387080 | tf_op jit(solution)/shard_map/faces/ppermute | solution.py:37
  79.7 3.6 %fusion.8 = f32[448,896]{1,0:T(8,128)S(1)} fusion(f32[288,896]{1,0:T(8,128)S(1)} %reshape.18, f32[288,112]{1,0:T(8,128)S(1)} %get-tuple-element.24, f32[288,112]{1,0:T(8,128)S(1)} %get-tuple-element.23, f32[288,112]{1,0:T(8,128)S(1)} %get-tuple-element.22, f32[288,112]{1,0:T(8,128)S(1)} %get-tuple-element.21, f32[288,112]{1,0:T(8,128)S(1)} %get-tuple-element.20, ...), kind=kOutput, calls=%fused_computation.36 | convolution fusion | flops 1388169216 | bytes 3670017 | tf_op jit(solution)/shard_map/gram/dot_general | solution.py:53
  85.2 3.4 %collective-permute-done.7 = f32[448,896]{1,0:T(8,128)S(1)} collective-permute-done((f32[448,896]{1,0:T(8,128)S(1)}, f32[448,896]{1,0:T(8,128)S(1)}, u32[]{:S(2)}, u32[]{:S(2)}) %collective-permute-start.7) | collective-permute-done | bytes 1605664 | tf_op jit(solution)/shard_map/gram/ppermute | solution.py:37
  88.6 3.6 %convolution_add_fusion = f32[448,896]{1,0:T(8,128)S(1)} fusion(f32[448,896]{1,0:T(8,128)S(1)} %collective-permute-done.7, f32[288,896]{1,0:T(8,128)S(1)} %reshape.18, f32[288,112]{1,0:T(8,128)S(1)} %get-tuple-element.24, f32[288,112]{1,0:T(8,128)S(1)} %get-tuple-element.23, f32[288,112]{1,0:T(8,128)S(1)} %get-tuple-element.22, ...), kind=kOutput, calls=%fused_computation | convolution fusion | flops 1388570624 | bytes 5275649 | tf_op jit(solution)/shard_map/gram/dot_general | solution.py:53
  92.2 25.6 %all_to_all.25 = f32[4,112,896]{2,1,0:T(8,128)S(1)} all-to-all(f32[4,112,896]{2,1,0:T(8,128)S(1)} %bitcast.25), channel_id=1, replica_groups={{0,4,8,12},{1,5,9,13},{2,6,10,14},{3,7,11,15},{16,20,24,28},{17,21,25,2..., dimensions={0} | all-to-all | bytes 3211264 | tf_op jit(solution)/shard_map/reduce_y/all_to_all | solution.py:102
  119.7 42.6 %all_to_all.26 = f32[4,28,896]{2,1,0:T(8,128)S(1)} all-to-all(f32[4,28,896]{2,1,0:T(8,128)S(1)} %reshape.20), channel_id=1, replica_groups={{0,256,2,258},{1,257,3,259},{64,320,66,322},{65,321,67,323},{128,384,13..., dimensions={0} | all-to-all | bytes 802816 | tf_op jit(solution)/shard_map/reduce_a/all_to_all | solution.py:108
  162.4 31.3 %all_to_all.27 = f32[4,28,896]{2,1,0:T(8,128)S(1)} all-to-all(f32[4,28,896]{2,1,0:T(8,128)S(1)} %broadcast_in_dim.6), channel_id=1, replica_groups={{0,256,2,258},{1,257,3,259},{64,320,66,322},{65,321,67,323},{128,384,13..., dimensions={0} | all-to-all | bytes 802816 | tf_op jit(solution)/shard_map/gather_a/all_to_all | solution.py:112
  193.9 19.6 %all_to_all.28 = f32[4,112,896]{2,1,0:T(8,128)S(1)} all-to-all(f32[4,112,896]{2,1,0:T(8,128)S(1)} %broadcast_in_dim.7), channel_id=1, replica_groups={{0,4,8,12},{1,5,9,13},{2,6,10,14},{3,7,11,15},{16,20,24,28},{17,21,25,2..., dimensions={0} | all-to-all | bytes 3211264 | tf_op jit(solution)/shard_map/gather_y/all_to_all | solution.py:116
  222.4 3.4 %convolution_add_fusion.1 = f32[288,896]{1,0:T(8,128)} fusion(f32[288,896]{1,0:T(8,128)S(1)} %fusion.6, f32[448,896]{1,0:T(8,128)S(1)} %bitcast.23, f32[288,112]{1,0:T(8,128)S(1)} %copy-done.5, f32[288,112]{1,0:T(8,128)S(1)} %copy-done.3, f32[288,112]{1,0:T(8,128)S(1)} %get-tuple-element.22, f32[288,112]{1,0:T(8,128)S(1)} %get-tuple-element.21, ...), kind=kOutput, calls=%fused_computation.1 | convolution fusion | flops 1388427264 | bytes 4702209 | tf_op jit(solution)/shard_map/first_product/dot_general | solution.py:53
  225.7 4.3 %all-to-all-start.4 = ((f32[4,72,896]{2,1,0:T(8,128)}), f32[4,72,896]{2,1,0:T(8,128)}, u32[]{:S(2)}, u32[]{:S(2)}) async-start(f32[4,72,896]{2,1,0:T(8,128)} %bitcast.26), calls=%async_computation.4 | async-start | bytes 2064384 | tf_op jit(solution)/shard_map/first_product/all_to_all | solution.py:124
  230.0 15.5 %all-to-all-done.4 = f32[4,72,896]{2,1,0:T(8,128)} async-done(((f32[4,72,896]{2,1,0:T(8,128)}), f32[4,72,896]{2,1,0:T(8,128)}, u32[]{:S(2)}, u32[]{:S(2)}) %all-to-all-start.4) | async-done | bytes 1032224 | tf_op jit(solution)/shard_map/first_product/all_to_all | solution.py:124
  246.9 15.1 %all_gather.19 = f32[288,896]{1,0:T(8,128)S(1)} all-gather(f32[72,896]{1,0:T(8,128)S(1)} %multiply_add_fusion), channel_id=1, replica_groups={{0,16,32,48},{64,80,96,112},{128,144,160,176},{192,208,224,240},{256,27..., dimensions={0}, use_global_device_ids=true | all-gather | bytes 1290240 | tf_op jit(solution)/shard_map/first_product/all_gather | solution.py:127
  266.4 3.4 %collective-permute-start.14 = (f32[288,112]{1,0:T(8,128)S(1)}, f32[288,112]{1,0:T(8,128)S(1)}, u32[]{:S(2)}, u32[]{:S(2)}) collective-permute-start(f32[288,112]{1,0:T(8,128)S(1)} %get-tuple-element.17), channel_id=1, source_target_pairs={{0,64},{1,65},{64,128},{65,129},{128,192},{129,193},{192,0},{193,1... | collective-permute-start | bytes 387080 | tf_op jit(solution)/shard_map/second_product/ppermute | solution.py:37
  269.8 3.7 %collective-permute-start.13 = (f32[288,112]{1,0:T(8,128)S(1)}, f32[288,112]{1,0:T(8,128)S(1)}, u32[]{:S(2)}, u32[]{:S(2)}) collective-permute-start(f32[288,112]{1,0:T(8,128)S(1)} %get-tuple-element.18), channel_id=1, source_target_pairs={{0,128},{1,129},{64,192},{65,193},{128,0},{129,1},{192,64},{193,65... | collective-permute-start | bytes 387080 | tf_op jit(solution)/shard_map/second_product/ppermute | solution.py:37
  279.3 4.2 %collective-permute-start.11 = (f32[288,112]{1,0:T(8,128)S(1)}, f32[288,112]{1,0:T(8,128)S(1)}, u32[]{:S(2)}, u32[]{:S(2)}) collective-permute-start(f32[288,112]{1,0:T(8,128)S(1)} %get-tuple-element.16), channel_id=1, source_target_pairs={{0,64},{1,65},{64,128},{65,129},{128,192},{129,193},{192,0},{193,1... | collective-permute-start | bytes 387080 | tf_op jit(solution)/shard_map/second_product/ppermute | solution.py:37
  290.2 8.7 %collective-permute-start.15 = (f32[288,112]{1,0:T(8,128)S(1)}, f32[288,112]{1,0:T(8,128)S(1)}, u32[]{:S(2)}, u32[]{:S(2)}) collective-permute-start(f32[288,112]{1,0:T(8,128)S(1)} %add_add_fusion), channel_id=1, source_target_pairs={{0,256},{1,257},{64,320},{65,321},{128,384},{129,385},{192,448},{1... | collective-permute-start | bytes 387080 | tf_op jit(solution)/shard_map/swap_back/ppermute | solution.py:37
  298.8 7.0 %collective-permute-done.15 = f32[288,112]{1,0:T(8,128)S(1)} collective-permute-done((f32[288,112]{1,0:T(8,128)S(1)}, f32[288,112]{1,0:T(8,128)S(1)}, u32[]{:S(2)}, u32[]{:S(2)}) %collective-permute-start.15) | collective-permute-done | bytes 129056 | tf_op jit(solution)/shard_map/swap_back/ppermute | solution.py:37
  (66 shorter events, 44.0 us)
Async XLA Ops:
  1.1 57.9 %copy-start.6 = (f32[112,576]{0,1:T(8,128)}, f32[112,576]{0,1:T(8,128)S(1)}, u32[]{:S(2)}) copy-start(f32[112,576]{0,1:T(8,128)S(1)} %copy.10) | copy-start | bytes 774148
  1.1 19.4 %collective-permute-start = (f32[288,112]{1,0:T(8,128)S(1)}, f32[288,112]{1,0:T(8,128)S(1)}, u32[]{:S(2)}, u32[]{:S(2)}) collective-permute-start(f32[288,112]{1,0:T(8,128)S(1)} %constant_dynamic-slice_fusion), channel_id=1, source_target_pairs={{0,256},{1,257},{64,320},{65,321},{128,384},{129,385},{192,448},{1... | collective-permute-start | bytes 387080 | tf_op jit(solution)/shard_map/swap_columns/ppermute | solution.py:37
  20.5 56.5 %collective-permute-start.1 = (f32[288,112]{1,0:T(8,128)S(1)}, f32[288,112]{1,0:T(8,128)S(1)}, u32[]{:S(2)}, u32[]{:S(2)}) collective-permute-start(f32[288,112]{1,0:T(8,128)S(1)} %get-tuple-element.8), channel_id=1, source_target_pairs={{0,64},{1,65},{64,128},{65,129},{128,192},{129,193},{192,0},{193,1... | collective-permute-start | bytes 387080 | tf_op jit(solution)/shard_map/faces/ppermute | solution.py:37
  22.7 54.4 %collective-permute-start.3 = (f32[288,112]{1,0:T(8,128)S(1)}, f32[288,112]{1,0:T(8,128)S(1)}, u32[]{:S(2)}, u32[]{:S(2)}) collective-permute-start(f32[288,112]{1,0:T(8,128)S(1)} %get-tuple-element.8), channel_id=1, source_target_pairs={{0,128},{1,129},{64,192},{65,193},{128,0},{129,1},{192,64},{193,65... | collective-permute-start | bytes 387080 | tf_op jit(solution)/shard_map/faces/ppermute | solution.py:37
  29.9 49.8 %collective-permute-start.5 = (f32[288,112]{1,0:T(8,128)S(1)}, f32[288,112]{1,0:T(8,128)S(1)}, u32[]{:S(2)}, u32[]{:S(2)}) collective-permute-start(f32[288,112]{1,0:T(8,128)S(1)} %get-tuple-element.8), channel_id=1, source_target_pairs={{0,192},{1,193},{64,0},{65,1},{128,64},{129,65},{192,128},{193,129... | collective-permute-start | bytes 387080 | tf_op jit(solution)/shard_map/faces/ppermute | solution.py:37
  60.5 16.6 %collective-permute-start.4 = (f32[288,112]{1,0:T(8,128)S(1)}, f32[288,112]{1,0:T(8,128)S(1)}, u32[]{:S(2)}, u32[]{:S(2)}) collective-permute-start(f32[288,112]{1,0:T(8,128)S(1)} %collective-permute-done), channel_id=1, source_target_pairs={{0,128},{1,129},{64,192},{65,193},{128,0},{129,1},{192,64},{193,65... | collective-permute-start | bytes 387080 | tf_op jit(solution)/shard_map/faces/ppermute | solution.py:37
  62.4 10.2 %collective-permute-start.2 = (f32[288,112]{1,0:T(8,128)S(1)}, f32[288,112]{1,0:T(8,128)S(1)}, u32[]{:S(2)}, u32[]{:S(2)}) collective-permute-start(f32[288,112]{1,0:T(8,128)S(1)} %collective-permute-done), channel_id=1, source_target_pairs={{0,64},{1,65},{64,128},{65,129},{128,192},{129,193},{192,0},{193,1... | collective-permute-start | bytes 387080 | tf_op jit(solution)/shard_map/faces/ppermute | solution.py:37
  72.6 7.0 %collective-permute-start.6 = (f32[288,112]{1,0:T(8,128)S(1)}, f32[288,112]{1,0:T(8,128)S(1)}, u32[]{:S(2)}, u32[]{:S(2)}) collective-permute-start(f32[288,112]{1,0:T(8,128)S(1)} %collective-permute-done), channel_id=1, source_target_pairs={{0,192},{1,193},{64,0},{65,1},{128,64},{129,65},{192,128},{193,129... | collective-permute-start | bytes 387080 | tf_op jit(solution)/shard_map/faces/ppermute | solution.py:37
  79.7 8.9 %copy-start.2 = (f32[288,112]{1,0:T(8,128)}, f32[288,112]{1,0:T(8,128)S(1)}, u32[]{:S(2)}) copy-start(f32[288,112]{1,0:T(8,128)S(1)} %get-tuple-element.23) | copy-start | bytes 387076
  79.7 8.9 %copy-start.4 = (f32[288,112]{1,0:T(8,128)}, f32[288,112]{1,0:T(8,128)S(1)}, u32[]{:S(2)}) copy-start(f32[288,112]{1,0:T(8,128)S(1)} %get-tuple-element.24) | copy-start | bytes 387076
  83.3 5.4 %collective-permute-start.7 = (f32[448,896]{1,0:T(8,128)S(1)}, f32[448,896]{1,0:T(8,128)S(1)}, u32[]{:S(2)}, u32[]{:S(2)}) collective-permute-start(f32[448,896]{1,0:T(8,128)S(1)} %fusion.8), channel_id=1, source_target_pairs={{0,1},{1,0},{64,65},{65,64},{128,129},{129,128},{192,193},{193,192... | collective-permute-start | bytes 4816904 | tf_op jit(solution)/shard_map/gram/ppermute | solution.py:37
  193.9 26.1 %copy-start.3 = (f32[288,112]{1,0:T(8,128)S(1)}, f32[288,112]{1,0:T(8,128)}, u32[]{:S(2)}) copy-start(f32[288,112]{1,0:T(8,128)} %copy-done.2) | copy-start | bytes 387076
  193.9 26.1 %copy-start.5 = (f32[288,112]{1,0:T(8,128)S(1)}, f32[288,112]{1,0:T(8,128)}, u32[]{:S(2)}) copy-start(f32[288,112]{1,0:T(8,128)} %copy-done.4) | copy-start | bytes 387076
  213.5 5.3 %collective-permute-start.8 = (f32[448,896]{1,0:T(8,128)S(1)}, f32[448,896]{1,0:T(8,128)S(1)}, u32[]{:S(2)}, u32[]{:S(2)}) collective-permute-start(f32[448,896]{1,0:T(8,128)S(1)} %bitcast.22), channel_id=1, source_target_pairs={{0,1},{1,0},{64,65},{65,64},{128,129},{129,128},{192,193},{193,192... | collective-permute-start | bytes 4816904 | tf_op jit(solution)/shard_map/gather_core/ppermute | solution.py:37
  225.7 19.8 %all-to-all-start.4 = ((f32[4,72,896]{2,1,0:T(8,128)}), f32[4,72,896]{2,1,0:T(8,128)}, u32[]{:S(2)}, u32[]{:S(2)}) async-start(f32[4,72,896]{2,1,0:T(8,128)} %bitcast.26), calls=%async_computation.4 | async-start | bytes 2064384 | tf_op jit(solution)/shard_map/first_product/all_to_all | solution.py:124
  262.0 2.1 copy-start.1
  266.4 39.6 %copy-start.7 = (f32[112,576]{0,1:T(8,128)S(1)}, f32[112,576]{0,1:T(8,128)}, u32[]{:S(2)}) copy-start(f32[112,576]{0,1:T(8,128)} %copy-done.6) | copy-start | bytes 774148
  266.4 17.1 %collective-permute-start.14 = (f32[288,112]{1,0:T(8,128)S(1)}, f32[288,112]{1,0:T(8,128)S(1)}, u32[]{:S(2)}, u32[]{:S(2)}) collective-permute-start(f32[288,112]{1,0:T(8,128)S(1)} %get-tuple-element.17), channel_id=1, source_target_pairs={{0,64},{1,65},{64,128},{65,129},{128,192},{129,193},{192,0},{193,1... | collective-permute-start | bytes 387080 | tf_op jit(solution)/shard_map/second_product/ppermute | solution.py:37
  269.8 17.6 %collective-permute-start.13 = (f32[288,112]{1,0:T(8,128)S(1)}, f32[288,112]{1,0:T(8,128)S(1)}, u32[]{:S(2)}, u32[]{:S(2)}) collective-permute-start(f32[288,112]{1,0:T(8,128)S(1)} %get-tuple-element.18), channel_id=1, source_target_pairs={{0,128},{1,129},{64,192},{65,193},{128,0},{129,1},{192,64},{193,65... | collective-permute-start | bytes 387080 | tf_op jit(solution)/shard_map/second_product/ppermute | solution.py:37
  273.7 16.4 %collective-permute-start.12 = (f32[288,112]{1,0:T(8,128)S(1)}, f32[288,112]{1,0:T(8,128)S(1)}, u32[]{:S(2)}, u32[]{:S(2)}) collective-permute-start(f32[288,112]{1,0:T(8,128)S(1)} %get-tuple-element.14), channel_id=1, source_target_pairs={{0,192},{1,193},{64,0},{65,1},{128,64},{129,65},{192,128},{193,129... | collective-permute-start | bytes 387080 | tf_op jit(solution)/shard_map/second_product/ppermute | solution.py:37
  276.0 22.9 %collective-permute-start.10 = (f32[288,112]{1,0:T(8,128)S(1)}, f32[288,112]{1,0:T(8,128)S(1)}, u32[]{:S(2)}, u32[]{:S(2)}) collective-permute-start(f32[288,112]{1,0:T(8,128)S(1)} %get-tuple-element.15), channel_id=1, source_target_pairs={{0,128},{1,129},{64,192},{65,193},{128,0},{129,1},{192,64},{193,65... | collective-permute-start | bytes 387080 | tf_op jit(solution)/shard_map/second_product/ppermute | solution.py:37
  279.3 19.5 %collective-permute-start.11 = (f32[288,112]{1,0:T(8,128)S(1)}, f32[288,112]{1,0:T(8,128)S(1)}, u32[]{:S(2)}, u32[]{:S(2)}) collective-permute-start(f32[288,112]{1,0:T(8,128)S(1)} %get-tuple-element.16), channel_id=1, source_target_pairs={{0,64},{1,65},{64,128},{65,129},{128,192},{129,193},{192,0},{193,1... | collective-permute-start | bytes 387080 | tf_op jit(solution)/shard_map/second_product/ppermute | solution.py:37
  283.5 15.3 %collective-permute-start.9 = (f32[288,112]{1,0:T(8,128)S(1)}, f32[288,112]{1,0:T(8,128)S(1)}, u32[]{:S(2)}, u32[]{:S(2)}) collective-permute-start(f32[288,112]{1,0:T(8,128)S(1)} %get-tuple-element.13), channel_id=1, source_target_pairs={{0,192},{1,193},{64,0},{65,1},{128,64},{129,65},{192,128},{193,129... | collective-permute-start | bytes 387080 | tf_op jit(solution)/shard_map/second_product/ppermute | solution.py:37
  290.2 15.7 %collective-permute-start.15 = (f32[288,112]{1,0:T(8,128)S(1)}, f32[288,112]{1,0:T(8,128)S(1)}, u32[]{:S(2)}, u32[]{:S(2)}) collective-permute-start(f32[288,112]{1,0:T(8,128)S(1)} %add_add_fusion), channel_id=1, source_target_pairs={{0,256},{1,257},{64,320},{65,321},{128,384},{129,385},{192,448},{1... | collective-permute-start | bytes 387080 | tf_op jit(solution)/shard_map/swap_back/ppermute | solution.py:37
  (1 other events, 1.2 us)

commit v4 on v3

--- a/solution.py
+++ b/solution.py
@@ -16,6 +16,7 @@
 AXES = ("row", "col")
 
 X_GROUPS = [[zl * 4 + x for x in range(4)] for zl in range(8)]
+B_GROUPS = [[(q * 4 + b) * 4 + x for b in range(4)] for q in range(2) for x in range(4)]
 Y_GROUPS = [[y * 4 + k for y in range(4)] for k in range(4)]
 
 
@@ -67,37 +68,40 @@
     return jnp.where(index == 0, own, other), jnp.where(index == 0, other, own)
 
 
+def joined(blocks, part, rows):
+    blocks = blocks.reshape(4, part, 4, 2 * rows).transpose(2, 1, 0, 3)
+    return blocks.reshape(4 * part, 8 * rows)
+
+
 def body(iterate):
     rows, cols = iterate.shape
     depth = cols // 2
     row, col = lax.axis_index("row"), lax.axis_index("col")
     core = col % 2
-    x, q = row % 4, row // 16
+    x, b, q = row % 4, row // 4 % 4, row // 16
 
     with jax.named_scope("swap_columns"):
         flipped = in_rows(iterate.T)
         own = in_rows(rows_at(flipped, q * depth, depth))
         other = in_rows(swap_q(in_rows(rows_at(flipped, (1 - q) * depth, depth))))
     with jax.named_scope("faces"):
-        lefts = []
-        for s in range(4):
-            parts = (own, other) if s == 0 else (b_shift(own, s), b_shift(other, s))
-            lefts.append(jnp.concatenate(ordered(q, *parts), 1))
-        near = jnp.concatenate(lefts[:2], 1)
-        far = jnp.concatenate(lefts[2:], 1)
-        kept, given = ordered(core, near, far)
-        right = [
-            lax.all_gather(part, "row", axis=0, axis_index_groups=X_GROUPS)
-            for part in (own, other)
-        ]
-        right = jnp.concatenate(ordered(q, *right), 0)
-        right = right.transpose(1, 0, 2).reshape(depth, 8 * rows)
+        block = jnp.concatenate(ordered(q, own, other), 1)
+        part = depth // 4
+        block = block.reshape(4, part, 2 * rows).transpose(1, 0, 2).reshape(part, 8 * rows)
+        blocks = jnp.broadcast_to(block, (4,) + block.shape)
+        right = lax.all_to_all(blocks, "row", 0, 0, axis_index_groups=X_GROUPS)
+        right = joined(right, part, rows)
+        left = lax.all_gather(block, "row", axis=0, axis_index_groups=B_GROUPS)
+        left = rows_at(jnp.concatenate([left, left], 0), b, 4)
+        left = joined(left, part, rows)
     size = 8 * rows
     half, chunk = size // 2, size // 8
 
     with jax.named_scope("gram"):
+        kept, given = ordered(core, left[:, :half], left[:, half:])
         partial = swap_core(dot(given, right, ((0,), (0,))))
-        total = dot(kept, right, ((0,), (0,))) + partial
+        total = lax.optimization_barrier(dot(kept, right, ((0,), (0,))))
+        total = total + partial
     with jax.named_scope("reduce_y"):
         parts = lax.all_to_all(
             total.reshape(4, chunk, size), "col", 0, 0, axis_index_groups=Y_GROUPS
@@ -108,8 +112,7 @@
         parts = lax.all_to_all(parts, AXES, 0, 0, axis_index_groups=A_GROUPS)
         piece = jnp.sum(parts, 0)
     with jax.named_scope("gather_a"):
-        parts = jnp.broadcast_to(piece, (4,) + piece.shape)
-        parts = lax.all_to_all(parts, AXES, 0, 0, axis_index_groups=A_GROUPS)
+        parts = lax.all_gather(piece, AXES, axis=0, axis_index_groups=A_GROUPS)
         near = parts.reshape(chunk, size)
     with jax.named_scope("gather_y"):
         parts = jnp.broadcast_to(near, (4,) + near.shape)
@@ -119,7 +122,8 @@
         gram_given = swap_core(gram_kept)
 
     with jax.named_scope("first_product"):
-        product = dot(kept, gram_kept, ((1,), (0,))) + dot(given, gram_given, ((1,), (0,)))
+        product = lax.optimization_barrier(dot(kept, gram_kept, ((1,), (0,))))
+        product = product + dot(given, gram_given, ((1,), (0,)))
         parts = product.reshape(4, depth // 4, size)
         parts = lax.all_to_all(parts, "row", 0, 0, axis_index_groups=X_GROUPS)
         mine = rows_at(right, x * (depth // 4), depth // 4)
@@ -137,7 +141,7 @@
             for s in range(4):
                 value = (near, far)[s // 2][:, s % 2 * 2 * rows :][:, : 2 * rows]
                 block = in_rows(jnp.where(part == 0, value[:, :rows], value[:, rows:]))
-                blocks.append(b_shift(block, -s) if s else block)
+                blocks.append(b_shift(block, s) if s else block)
             sums.append(blocks[0] + blocks[1] + blocks[2] + blocks[3])
     with jax.named_scope("swap_back"):
         applied = jnp.concatenate(ordered(q, sums[1], swap_q(sums[0])), 0).T

time: 308 us -> 267 us (0.87)
  the two profiles are of different devices: /device:TPU:32 before, /device:TPU:8 now
where the time goes in v4:
time: 267 us; the launch traced here: 266 us
  blocking collectives  146 us (55%)
  waiting for transfers between devices  49.5 us (19%)
  starting transfers between devices  43.5 us (16%)
  matrix products  15.8 us (6%)
  local copies, waits for them, and re-layouts  8.57 us (3%)
    all_to_all x1, blocking collectives, body(): parts = lax.all_to_all(parts, AXES, 0, 0, axis_index_groups=A_GROUPS)  40.4 us
    ppermute x10, waiting for transfers between devices, permute(): return lax.ppermute(value, AXES, pairs)  34.3 us
    ppermute x10, starting transfers between devices, permute(): return lax.ppermute(value, AXES, pairs)  33.6 us
    all_to_all x1, blocking collectives, body(): lax.all_to_all(total.reshape(4, chunk, size), 'col', 0, 0, axis_index_gro...  25 us
    all_to_all x1, blocking collectives, body(): parts = lax.all_to_all(parts, 'col', 0, 0, axis_index_groups=Y_GROUPS)  22.3 us
    all_gather x1, blocking collectives, body(): parts = lax.all_gather(piece, AXES, axis=0, axis_index_groups=A_GROUPS)  21.5 us
    all_gather x1, blocking collectives, body(): left = lax.all_gather(block, 'row', axis=0, axis_index_groups=B_GROUPS)  21.5 us
    dot_general x6, matrix products, dot(): lax.dot_general(left, right, (dims, ((), ())), precision=PREC, preferred_...  15.8 us
  transfers between devices with their start and end apart: 12, of which 6 were waited for; matrix products, arithmetic and copies ran while one was open for 3% of the time, Pallas kernels for 0%

profile of v4, /device:TPU:8, one launch (start us, length us, event | category | flops | bytes accessed | tf_op | source)
XLA Modules:
  0.0 266.2 jit_solution(2111609822459811916)
XLA Ops:
  1.1 9.1 %collective-permute-start = (f32[288,112]{1,0:T(8,128)S(1)}, f32[288,112]{1,0:T(8,128)S(1)}, u32[]{:S(2)}, u32[]{:S(2)}) collective-permute-start(f32[288,112]{1,0:T(8,128)S(1)} %constant_dynamic-slice_fusion), channel_id=1, source_target_pairs={{0,256},{1,257},{64,320},{65,321},{128,384},{129,385},{192,448},{1... | collective-permute-start | bytes 387080 | tf_op jit(solution)/shard_map/swap_columns/ppermute | solution.py:38
  10.3 13.3 %collective-permute-done = f32[288,112]{1,0:T(8,128)S(1)} collective-permute-done((f32[288,112]{1,0:T(8,128)S(1)}, f32[288,112]{1,0:T(8,128)S(1)}, u32[]{:S(2)}, u32[]{:S(2)}) %collective-permute-start) | collective-permute-done | bytes 129056 | tf_op jit(solution)/shard_map/swap_columns/ppermute | solution.py:38
  25.1 4.3 %all-to-all-start = ((f32[4,72,896]{2,1,0:T(8,128)}), f32[4,72,896]{2,1,0:T(8,128)S(1)}, u32[]{:S(2)}, u32[]{:S(2)}) async-start(f32[4,72,896]{2,1,0:T(8,128)} %broadcast_in_dim.6), calls=%async_computation | async-start | bytes 2064384 | tf_op jit(solution)/shard_map/faces/all_to_all | solution.py:92
  29.6 21.5 %all_gather.12 = f32[4,72,896]{2,1,0:T(8,128)S(1)} all-gather(f32[1,72,896]{2,1,0:T(8,128)S(1)} %reshape.40), channel_id=1, replica_groups={{0,64,128,192},{16,80,144,208},{32,96,160,224},{48,112,176,240},{256,32..., dimensions={0}, use_global_device_ids=true | all-gather | bytes 1290240 | tf_op jit(solution)/shard_map/faces/all_gather | solution.py:94
  56.1 3.2 %fusion.5 = f32[448,896]{1,0:T(8,128)S(1)} fusion(f32[288,896]{1,0:T(8,128)S(1)} %reshape.39, f32[288,896]{1,0:T(8,128)S(1)} %reshape.42, pred[]{:T(512)S(6)} %eq.11), kind=kOutput, calls=%fused_computation.16 | convolution fusion | flops 1387395072 | bytes 3817473 | tf_op jit(solution)/shard_map/gram/dot_general | solution.py:54
  59.4 2.1 collective-permute-start.1
  61.5 3.2 %fusion.4 = f32[448,896]{1,0:T(8,128)S(1)} fusion(f32[288,896]{1,0:T(8,128)S(1)} %reshape.39, f32[288,896]{1,0:T(8,128)S(1)} %reshape.42, pred[]{:T(512)S(6)} %eq.11), kind=kOutput, calls=%fused_computation.15 | convolution fusion | flops 1387395072 | bytes 3817473 | tf_op jit(solution)/shard_map/gram/dot_general | solution.py:54
  64.9 25.0 %all_to_all.25 = f32[4,112,896]{2,1,0:T(8,128)S(1)} all-to-all(f32[4,112,896]{2,1,0:T(8,128)S(1)} %bitcast.28), channel_id=1, replica_groups={{0,4,8,12},{1,5,9,13},{2,6,10,14},{3,7,11,15},{16,20,24,28},{17,21,25,2..., dimensions={0} | all-to-all | bytes 3211264 | tf_op jit(solution)/shard_map/reduce_y/all_to_all | solution.py:106
  90.1 40.4 %all_to_all.26 = f32[4,28,896]{2,1,0:T(8,128)S(1)} all-to-all(f32[4,28,896]{2,1,0:T(8,128)S(1)} %reshape.44), channel_id=1, replica_groups={{0,256,2,258},{1,257,3,259},{64,320,66,322},{65,321,67,323},{128,384,13..., dimensions={0} | all-to-all | bytes 802816 | tf_op jit(solution)/shard_map/reduce_a/all_to_all | solution.py:112
  130.5 21.5 %all-gather.1 = f32[4,28,896]{2,1,0:T(8,128)S(1)} all-gather(f32[1,28,896]{2,1,0:T(8,128)S(1)} %bitcast.37), channel_id=2, replica_groups={{0,256,2,258},{1,257,3,259},{64,320,66,322},{65,321,67,323},{128,384,13..., dimensions={0}, use_global_device_ids=true | all-gather | bytes 501760 | tf_op jit(solution)/shard_map/gather_a/all_gather | solution.py:115
  152.2 22.3 %all_to_all.27 = f32[4,112,896]{2,1,0:T(8,128)S(1)} all-to-all(f32[4,112,896]{2,1,0:T(8,128)S(1)} %broadcast_in_dim.7), channel_id=1, replica_groups={{0,4,8,12},{1,5,9,13},{2,6,10,14},{3,7,11,15},{16,20,24,28},{17,21,25,2..., dimensions={0} | all-to-all | bytes 3211264 | tf_op jit(solution)/shard_map/gather_y/all_to_all | solution.py:119
  176.4 2.1 fusion.3
  179.9 3.1 %convolution_add_fusion = f32[288,896]{1,0:T(8,128)} fusion(f32[288,896]{1,0:T(8,128)S(1)} %fusion.3, f32[448,896]{1,0:T(8,128)S(1)} %collective-permute-done.2, f32[288,896]{1,0:T(8,128)S(1)} %reshape.42, pred[]{:T(512)S(6)} %eq.11), kind=kOutput, calls=%fused_computation.2 | convolution fusion | flops 1387653120 | bytes 4849665 | tf_op jit(solution)/shard_map/first_product/dot_general | solution.py:54
  183.0 5.6 %all-to-all-start.4 = ((f32[4,72,896]{2,1,0:T(8,128)}), f32[4,72,896]{2,1,0:T(8,128)S(1)}, u32[]{:S(2)}, u32[]{:S(2)}) async-start(f32[4,72,896]{2,1,0:T(8,128)} %bitcast.31), calls=%async_computation.4 | async-start | bytes 2064384 | tf_op jit(solution)/shard_map/first_product/all_to_all | solution.py:128
  188.6 15.2 %all-to-all-done.4 = f32[4,72,896]{2,1,0:T(8,128)S(1)} async-done(((f32[4,72,896]{2,1,0:T(8,128)}), f32[4,72,896]{2,1,0:T(8,128)S(1)}, u32[]{:S(2)}, u32[]{:S(2)}) %all-to-all-start.4) | async-done | bytes 1032224 | tf_op jit(solution)/shard_map/first_product/all_to_all | solution.py:128
  204.8 15.4 %all_gather.15 = f32[288,896]{1,0:T(8,128)S(1)} all-gather(f32[72,896]{1,0:T(8,128)S(1)} %multiply_add_fusion), channel_id=1, replica_groups={{0,16,32,48},{64,80,96,112},{128,144,160,176},{192,208,224,240},{256,27..., dimensions={0}, use_global_device_ids=true | all-gather | bytes 1290240 | tf_op jit(solution)/shard_map/first_product/all_gather | solution.py:131
  224.6 2.9 %collective-permute-start.8 = (f32[288,112]{1,0:T(8,128)S(1)}, f32[288,112]{1,0:T(8,128)S(1)}, u32[]{:S(2)}, u32[]{:S(2)}) collective-permute-start(f32[288,112]{1,0:T(8,128)S(1)} %get-tuple-element.13), channel_id=1, source_target_pairs={{0,192},{1,193},{64,0},{65,1},{128,64},{129,65},{192,128},{193,129... | collective-permute-start | bytes 387080 | tf_op jit(solution)/shard_map/second_product/ppermute | solution.py:38
  227.5 2.3 collective-permute-start.7
  230.0 3.5 %collective-permute-start.6 = (f32[288,112]{1,0:T(8,128)S(1)}, f32[288,112]{1,0:T(8,128)S(1)}, u32[]{:S(2)}, u32[]{:S(2)}) collective-permute-start(f32[288,112]{1,0:T(8,128)S(1)} %get-tuple-element.10), channel_id=1, source_target_pairs={{0,64},{1,65},{64,128},{65,129},{128,192},{129,193},{192,0},{193,1... | collective-permute-start | bytes 387080 | tf_op jit(solution)/shard_map/second_product/ppermute | solution.py:38
  233.5 3.9 %collective-permute-start.4 = (f32[288,112]{1,0:T(8,128)S(1)}, f32[288,112]{1,0:T(8,128)S(1)}, u32[]{:S(2)}, u32[]{:S(2)}) collective-permute-start(f32[288,112]{1,0:T(8,128)S(1)} %get-tuple-element.11), channel_id=1, source_target_pairs={{0,128},{1,129},{64,192},{65,193},{128,0},{129,1},{192,64},{193,65... | collective-permute-start | bytes 387080 | tf_op jit(solution)/shard_map/second_product/ppermute | solution.py:38
  237.5 3.7 %collective-permute-start.5 = (f32[288,112]{1,0:T(8,128)S(1)}, f32[288,112]{1,0:T(8,128)S(1)}, u32[]{:S(2)}, u32[]{:S(2)}) collective-permute-start(f32[288,112]{1,0:T(8,128)S(1)} %get-tuple-element.12), channel_id=1, source_target_pairs={{0,192},{1,193},{64,0},{65,1},{128,64},{129,65},{192,128},{193,129... | collective-permute-start | bytes 387080 | tf_op jit(solution)/shard_map/second_product/ppermute | solution.py:38
  241.2 2.1 collective-permute-start.3
  243.3 6.8 %collective-permute-done.7 = f32[288,112]{1,0:T(8,128)S(1)} collective-permute-done((f32[288,112]{1,0:T(8,128)S(1)}, f32[288,112]{1,0:T(8,128)S(1)}, u32[]{:S(2)}, u32[]{:S(2)}) %collective-permute-start.7) | collective-permute-done | bytes 129056 | tf_op jit(solution)/shard_map/second_product/ppermute | solution.py:38
  252.8 12.3 %collective-permute-done.9 = f32[288,112]{1,0:T(8,128)S(1)} collective-permute-done((f32[288,112]{1,0:T(8,128)S(1)}, f32[288,112]{1,0:T(8,128)S(1)}, u32[]{:S(2)}, u32[]{:S(2)}) %collective-permute-start.9) | collective-permute-done | bytes 129056 | tf_op jit(solution)/shard_map/swap_back/ppermute | solution.py:38
  (52 shorter events, 20.7 us)
Async XLA Ops:
  1.1 24.0 %copy-start.3 = (f32[112,576]{0,1:T(8,128)}, f32[112,576]{0,1:T(8,128)S(1)}, u32[]{:S(2)}) copy-start(f32[112,576]{0,1:T(8,128)S(1)} %copy.22) | copy-start | bytes 774148
  1.1 22.4 %collective-permute-start = (f32[288,112]{1,0:T(8,128)S(1)}, f32[288,112]{1,0:T(8,128)S(1)}, u32[]{:S(2)}, u32[]{:S(2)}) collective-permute-start(f32[288,112]{1,0:T(8,128)S(1)} %constant_dynamic-slice_fusion), channel_id=1, source_target_pairs={{0,256},{1,257},{64,320},{65,321},{128,384},{129,385},{192,448},{1... | collective-permute-start | bytes 387080 | tf_op jit(solution)/shard_map/swap_columns/ppermute | solution.py:38
  25.1 28.6 %all-to-all-start = ((f32[4,72,896]{2,1,0:T(8,128)}), f32[4,72,896]{2,1,0:T(8,128)S(1)}, u32[]{:S(2)}, u32[]{:S(2)}) async-start(f32[4,72,896]{2,1,0:T(8,128)} %broadcast_in_dim.6), calls=%async_computation | async-start | bytes 2064384 | tf_op jit(solution)/shard_map/faces/all_to_all | solution.py:92
  56.1 5.4 %copy-start = (f32[288,896]{1,0:T(8,128)}, f32[288,896]{1,0:T(8,128)S(1)}, u32[]{:S(2)}) copy-start(f32[288,896]{1,0:T(8,128)S(1)} %reshape.39) | copy-start | bytes 3096580
  59.4 5.4 %collective-permute-start.1 = (f32[448,896]{1,0:T(8,128)S(1)}, f32[448,896]{1,0:T(8,128)S(1)}, u32[]{:S(2)}, u32[]{:S(2)}) collective-permute-start(f32[448,896]{1,0:T(8,128)S(1)} %fusion.5), channel_id=1, source_target_pairs={{0,1},{1,0},{64,65},{65,64},{128,129},{129,128},{192,193},{193,192... | collective-permute-start | bytes 4816904 | tf_op jit(solution)/shard_map/gram/ppermute | solution.py:38
  174.5 5.3 %collective-permute-start.2 = (f32[448,896]{1,0:T(8,128)S(1)}, f32[448,896]{1,0:T(8,128)S(1)}, u32[]{:S(2)}, u32[]{:S(2)}) collective-permute-start(f32[448,896]{1,0:T(8,128)S(1)} %bitcast.25), channel_id=1, source_target_pairs={{0,1},{1,0},{64,65},{65,64},{128,129},{129,128},{192,193},{193,192... | collective-permute-start | bytes 4816904 | tf_op jit(solution)/shard_map/gather_core/ppermute | solution.py:38
  179.9 3.1 %copy-start.1 = (f32[448,896]{1,0:T(8,128)}, f32[448,896]{1,0:T(8,128)S(1)}, u32[]{:S(2)}) copy-start(f32[448,896]{1,0:T(8,128)S(1)} %collective-permute-done.2) | copy-start | bytes 4816900
  183.0 20.8 %all-to-all-start.4 = ((f32[4,72,896]{2,1,0:T(8,128)}), f32[4,72,896]{2,1,0:T(8,128)S(1)}, u32[]{:S(2)}, u32[]{:S(2)}) async-start(f32[4,72,896]{2,1,0:T(8,128)} %bitcast.31), calls=%async_computation.4 | async-start | bytes 2064384 | tf_op jit(solution)/shard_map/first_product/all_to_all | solution.py:128
  220.2 2.1 copy-start.2
  224.6 40.7 %copy-start.4 = (f32[112,576]{0,1:T(8,128)S(1)}, f32[112,576]{0,1:T(8,128)}, u32[]{:S(2)}) copy-start(f32[112,576]{0,1:T(8,128)} %copy-done.3) | copy-start | bytes 774148
  224.6 16.6 %collective-permute-start.8 = (f32[288,112]{1,0:T(8,128)S(1)}, f32[288,112]{1,0:T(8,128)S(1)}, u32[]{:S(2)}, u32[]{:S(2)}) collective-permute-start(f32[288,112]{1,0:T(8,128)S(1)} %get-tuple-element.13), channel_id=1, source_target_pairs={{0,192},{1,193},{64,0},{65,1},{128,64},{129,65},{192,128},{193,129... | collective-permute-start | bytes 387080 | tf_op jit(solution)/shard_map/second_product/ppermute | solution.py:38
  227.5 22.6 %collective-permute-start.7 = (f32[288,112]{1,0:T(8,128)S(1)}, f32[288,112]{1,0:T(8,128)S(1)}, u32[]{:S(2)}, u32[]{:S(2)}) collective-permute-start(f32[288,112]{1,0:T(8,128)S(1)} %get-tuple-element.14), channel_id=1, source_target_pairs={{0,128},{1,129},{64,192},{65,193},{128,0},{129,1},{192,64},{193,65... | collective-permute-start | bytes 387080 | tf_op jit(solution)/shard_map/second_product/ppermute | solution.py:38
  230.0 20.1 %collective-permute-start.6 = (f32[288,112]{1,0:T(8,128)S(1)}, f32[288,112]{1,0:T(8,128)S(1)}, u32[]{:S(2)}, u32[]{:S(2)}) collective-permute-start(f32[288,112]{1,0:T(8,128)S(1)} %get-tuple-element.10), channel_id=1, source_target_pairs={{0,64},{1,65},{64,128},{65,129},{128,192},{129,193},{192,0},{193,1... | collective-permute-start | bytes 387080 | tf_op jit(solution)/shard_map/second_product/ppermute | solution.py:38
  233.5 19.2 %collective-permute-start.4 = (f32[288,112]{1,0:T(8,128)S(1)}, f32[288,112]{1,0:T(8,128)S(1)}, u32[]{:S(2)}, u32[]{:S(2)}) collective-permute-start(f32[288,112]{1,0:T(8,128)S(1)} %get-tuple-element.11), channel_id=1, source_target_pairs={{0,128},{1,129},{64,192},{65,193},{128,0},{129,1},{192,64},{193,65... | collective-permute-start | bytes 387080 | tf_op jit(solution)/shard_map/second_product/ppermute | solution.py:38
  237.5 15.3 %collective-permute-start.5 = (f32[288,112]{1,0:T(8,128)S(1)}, f32[288,112]{1,0:T(8,128)S(1)}, u32[]{:S(2)}, u32[]{:S(2)}) collective-permute-start(f32[288,112]{1,0:T(8,128)S(1)} %get-tuple-element.12), channel_id=1, source_target_pairs={{0,192},{1,193},{64,0},{65,1},{128,64},{129,65},{192,128},{193,129... | collective-permute-start | bytes 387080 | tf_op jit(solution)/shard_map/second_product/ppermute | solution.py:38
  241.2 11.6 %collective-permute-start.3 = (f32[288,112]{1,0:T(8,128)S(1)}, f32[288,112]{1,0:T(8,128)S(1)}, u32[]{:S(2)}, u32[]{:S(2)}) collective-permute-start(f32[288,112]{1,0:T(8,128)S(1)} %get-tuple-element.9), channel_id=1, source_target_pairs={{0,64},{1,65},{64,128},{65,129},{128,192},{129,193},{192,0},{193,1... | collective-permute-start | bytes 387080 | tf_op jit(solution)/shard_map/second_product/ppermute | solution.py:38
  250.3 14.8 %collective-permute-start.9 = (f32[288,112]{1,0:T(8,128)S(1)}, f32[288,112]{1,0:T(8,128)S(1)}, u32[]{:S(2)}, u32[]{:S(2)}) collective-permute-start(f32[288,112]{1,0:T(8,128)S(1)} %add_add_fusion), channel_id=1, source_target_pairs={{0,256},{1,257},{64,320},{65,321},{128,384},{129,385},{192,448},{1... | collective-permute-start | bytes 387080 | tf_op jit(solution)/shard_map/swap_back/ppermute | solution.py:38

commit v5 on v4

--- a/solution.py
+++ b/solution.py
@@ -73,11 +73,28 @@
     return blocks.reshape(4 * part, 8 * rows)
 
 
+def tiles(value):
+    rows, lanes = value.shape
+    value = value.reshape(rows // 8, 8, lanes // 128, 128).transpose(0, 2, 1, 3)
+    value = value.reshape(-1, 8, 128)
+    each = -(-value.shape[0] // 4)
+    value = jnp.pad(value, ((0, 4 * each - value.shape[0]), (0, 0), (0, 0)))
+    return value.reshape(4, each, 8, 128)
+
+
+def from_tiles(pieces, shape):
+    rows, lanes = shape
+    value = pieces.reshape(-1, 8, 128)[: rows // 8 * (lanes // 128)]
+    value = value.reshape(rows // 8, lanes // 128, 8, 128).transpose(0, 2, 1, 3)
+    return value.reshape(rows, lanes)
+
+
 def body(iterate):
     rows, cols = iterate.shape
     depth = cols // 2
     row, col = lax.axis_index("row"), lax.axis_index("col")
     core = col % 2
+    a = col // 2 % 2 * 2 + row // 16
     x, b, q = row % 4, row // 4 % 4, row // 16
 
     with jax.named_scope("swap_columns"):
@@ -108,12 +125,14 @@
         )
         near = jnp.sum(parts, 0)
     with jax.named_scope("reduce_a"):
-        parts = near.reshape(4, chunk // 4, size)
-        parts = lax.all_to_all(parts, AXES, 0, 0, axis_index_groups=A_GROUPS)
-        piece = jnp.sum(parts, 0)
+        pieces = tiles(near)
+        piece = lax.dynamic_index_in_dim(pieces, a, 0, False)
+        for step in (2, 1, 3):
+            sent = lax.dynamic_index_in_dim(pieces, (a + step) % 4, 0, False)
+            piece = piece + permute(sent, lambda x, y, z, c: (x, y, (z + 4 * step) % 16, c))
     with jax.named_scope("gather_a"):
-        parts = lax.all_gather(piece, AXES, axis=0, axis_index_groups=A_GROUPS)
-        near = parts.reshape(chunk, size)
+        pieces = lax.all_gather(piece, AXES, axis=0, axis_index_groups=A_GROUPS)
+        near = from_tiles(pieces, near.shape)
     with jax.named_scope("gather_y"):
         parts = jnp.broadcast_to(near, (4,) + near.shape)
         parts = lax.all_to_all(parts, "col", 0, 0, axis_index_groups=Y_GROUPS)

time: 267 us -> 259 us (0.970)
  the two profiles are of different devices: /device:TPU:8 before, /device:TPU:2 now
where the time goes in v5:
time: 259 us; the launch traced here: 258 us
  blocking collectives  83.2 us (32%)
  starting transfers between devices  74.3 us (29%)
  waiting for transfers between devices  72.5 us (28%)
  matrix products  15.8 us (6%)
  local copies, waits for them, and re-layouts  8.59 us (3%)
  other arithmetic  3.53 us (1%)
    ppermute x13, starting transfers between devices, permute(): return lax.ppermute(value, AXES, pairs)  60.5 us
    ppermute x13, waiting for transfers between devices, permute(): return lax.ppermute(value, AXES, pairs)  37.1 us
    all_gather x1, blocking collectives, body(): pieces = lax.all_gather(piece, AXES, axis=0, axis_index_groups=A_GROUPS)  23.9 us
    all_to_all x1, blocking collectives, body(): parts = lax.all_to_all(parts, 'col', 0, 0, axis_index_groups=Y_GROUPS)  23.7 us
    all_to_all x1, waiting for transfers between devices, body(): lax.all_to_all(total.reshape(4, chunk, size), 'col', 0, 0, axis_index_gro...  21.7 us
    all_gather x1, blocking collectives, body(): left = lax.all_gather(block, 'row', axis=0, axis_index_groups=B_GROUPS)  21.5 us
    dot_general x6, matrix products, dot(): lax.dot_general(left, right, (dims, ((), ())), precision=PREC, preferred_...  15.8 us
    all_gather x1, blocking collectives, body(): lax.all_gather(inner, 'row', axis=0, tiled=True, axis_index_groups=X_GROUPS)  14.1 us
  transfers between devices with their start and end apart: 16, of which 7 were waited for; matrix products, arithmetic and copies ran while one was open for 3% of the time, Pallas kernels for 0%

profile of v5, /device:TPU:2, one launch (start us, length us, event | category | flops | bytes accessed | tf_op | source)
XLA Modules:
  0.0 258.4 jit_solution(6319326752601867312)
XLA Ops:
  1.1 9.1 %collective-permute-start = (f32[288,112]{1,0:T(8,128)S(1)}, f32[288,112]{1,0:T(8,128)S(1)}, u32[]{:S(2)}, u32[]{:S(2)}) collective-permute-start(f32[288,112]{1,0:T(8,128)S(1)} %constant_dynamic-slice_fusion), channel_id=1, source_target_pairs={{0,256},{1,257},{64,320},{65,321},{128,384},{129,385},{192,448},{1... | collective-permute-start | bytes 387080 | tf_op jit(solution)/shard_map/swap_columns/ppermute | solution.py:38
  10.3 13.3 %collective-permute-done = f32[288,112]{1,0:T(8,128)S(1)} collective-permute-done((f32[288,112]{1,0:T(8,128)S(1)}, f32[288,112]{1,0:T(8,128)S(1)}, u32[]{:S(2)}, u32[]{:S(2)}) %collective-permute-start) | collective-permute-done | bytes 129056 | tf_op jit(solution)/shard_map/swap_columns/ppermute | solution.py:38
  25.1 4.8 %all-to-all-start = ((f32[4,72,896]{2,1,0:T(8,128)}), f32[4,72,896]{2,1,0:T(8,128)S(1)}, u32[]{:S(2)}, u32[]{:S(2)}) async-start(f32[4,72,896]{2,1,0:T(8,128)} %broadcast_in_dim.6), calls=%async_computation | async-start | bytes 2064384 | tf_op jit(solution)/shard_map/faces/all_to_all | solution.py:109
  30.1 21.5 %all_gather.12 = f32[4,72,896]{2,1,0:T(8,128)S(1)} all-gather(f32[1,72,896]{2,1,0:T(8,128)S(1)} %reshape.52), channel_id=1, replica_groups={{0,64,128,192},{16,80,144,208},{32,96,160,224},{48,112,176,240},{256,32..., dimensions={0}, use_global_device_ids=true | all-gather | bytes 1290240 | tf_op jit(solution)/shard_map/faces/all_gather | solution.py:111
  56.7 3.2 %fusion.5 = f32[448,896]{1,0:T(8,128)S(1)} fusion(f32[288,896]{1,0:T(8,128)S(1)} %reshape.51, f32[288,896]{1,0:T(8,128)S(1)} %reshape.54, pred[]{:T(512)S(6)} %eq.15), kind=kOutput, calls=%fused_computation.16 | convolution fusion | flops 1387395072 | bytes 3817473 | tf_op jit(solution)/shard_map/gram/dot_general | solution.py:54
  62.0 3.2 %fusion.4 = f32[448,896]{1,0:T(8,128)S(1)} fusion(f32[288,896]{1,0:T(8,128)S(1)} %reshape.51, f32[288,896]{1,0:T(8,128)S(1)} %reshape.54, pred[]{:T(512)S(6)} %eq.15), kind=kOutput, calls=%fused_computation.15 | convolution fusion | flops 1387395072 | bytes 3817473 | tf_op jit(solution)/shard_map/gram/dot_general | solution.py:54
  66.7 4.5 %all-to-all-start.1 = ((f32[4,112,896]{2,1,0:T(8,128)}), f32[4,112,896]{2,1,0:T(8,128)S(1)}, u32[]{:S(2)}, u32[]{:S(2)}) async-start(f32[4,112,896]{2,1,0:T(8,128)} %bitcast.50), calls=%async_computation.1 | async-start | bytes 3211264 | tf_op jit(solution)/shard_map/reduce_y/all_to_all | solution.py:123
  71.1 21.7 %all-to-all-done.1 = f32[4,112,896]{2,1,0:T(8,128)S(1)} async-done(((f32[4,112,896]{2,1,0:T(8,128)}), f32[4,112,896]{2,1,0:T(8,128)S(1)}, u32[]{:S(2)}, u32[]{:S(2)}) %all-to-all-start.1) | async-done | bytes 1605664 | tf_op jit(solution)/shard_map/reduce_y/all_to_all | solution.py:123
  93.0 12.9 %collective-permute-start.2 = (f32[25,8,128]{2,1,0:T(8,128)S(1)}, f32[25,8,128]{2,1,0:T(8,128)S(1)}, u32[]{:S(2)}, u32[]{:S(2)}) collective-permute-start(f32[25,8,128]{2,1,0:T(8,128)S(1)} %get-tuple-element.17), channel_id=1, source_target_pairs={{0,2},{1,3},{64,66},{65,67},{128,130},{129,131},{192,194},{193,195... | collective-permute-start | bytes 307208 | tf_op jit(solution)/shard_map/reduce_a/ppermute | solution.py:38
  106.0 2.7 %collective-permute-start.4 = (f32[25,8,128]{2,1,0:T(8,128)S(1)}, f32[25,8,128]{2,1,0:T(8,128)S(1)}, u32[]{:S(2)}, u32[]{:S(2)}) collective-permute-start(f32[25,8,128]{2,1,0:T(8,128)S(1)} %get-tuple-element.18), channel_id=1, source_target_pairs={{0,258},{1,259},{64,322},{65,323},{128,386},{129,387},{192,450},{1... | collective-permute-start | bytes 307208 | tf_op jit(solution)/shard_map/reduce_a/ppermute | solution.py:38
  108.6 7.1 %collective-permute-start.3 = (f32[25,8,128]{2,1,0:T(8,128)S(1)}, f32[25,8,128]{2,1,0:T(8,128)S(1)}, u32[]{:S(2)}, u32[]{:S(2)}) collective-permute-start(f32[25,8,128]{2,1,0:T(8,128)S(1)} %get-tuple-element.19), channel_id=1, source_target_pairs={{0,256},{1,257},{64,320},{65,321},{128,384},{129,385},{192,448},{1... | collective-permute-start | bytes 307208 | tf_op jit(solution)/shard_map/reduce_a/ppermute | solution.py:38
  115.7 7.9 %collective-permute-done.4 = f32[25,8,128]{2,1,0:T(8,128)S(1)} collective-permute-done((f32[25,8,128]{2,1,0:T(8,128)S(1)}, f32[25,8,128]{2,1,0:T(8,128)S(1)}, u32[]{:S(2)}, u32[]{:S(2)}) %collective-permute-start.4) | collective-permute-done | bytes 102432 | tf_op jit(solution)/shard_map/reduce_a/ppermute | solution.py:38
  123.7 23.9 %all-gather = f32[100,8,128]{2,1,0:T(8,128)S(1)} all-gather(f32[25,8,128]{2,1,0:T(8,128)S(1)} %fusion.7), channel_id=2, replica_groups={{0,256,2,258},{1,257,3,259},{64,320,66,322},{65,321,67,323},{128,384,13..., dimensions={0}, use_global_device_ids=true | all-gather | bytes 512000 | tf_op jit(solution)/shard_map/gather_a/all_gather | solution.py:134
  147.8 23.7 %all_to_all.20 = f32[4,112,896]{2,1,0:T(8,128)S(1)} all-to-all(f32[4,112,896]{2,1,0:T(8,128)S(1)} %broadcast_in_dim.7), channel_id=1, replica_groups={{0,4,8,12},{1,5,9,13},{2,6,10,14},{3,7,11,15},{16,20,24,28},{17,21,25,2..., dimensions={0} | all-to-all | bytes 3211264 | tf_op jit(solution)/shard_map/gather_y/all_to_all | solution.py:138
  176.8 3.1 %convolution_add_fusion = f32[288,896]{1,0:T(8,128)} fusion(f32[288,896]{1,0:T(8,128)S(1)} %fusion.3, f32[448,896]{1,0:T(8,128)S(1)} %collective-permute-done.5, f32[288,896]{1,0:T(8,128)S(1)} %reshape.54, pred[]{:T(512)S(6)} %eq.15), kind=kOutput, calls=%fused_computation.2 | convolution fusion | flops 1387653120 | bytes 4849665 | tf_op jit(solution)/shard_map/first_product/dot_general | solution.py:54
  179.9 4.5 %all-to-all-start.3 = ((f32[4,72,896]{2,1,0:T(8,128)}), f32[4,72,896]{2,1,0:T(8,128)S(1)}, u32[]{:S(2)}, u32[]{:S(2)}) async-start(f32[4,72,896]{2,1,0:T(8,128)} %bitcast.53), calls=%async_computation.3 | async-start | bytes 2064384 | tf_op jit(solution)/shard_map/first_product/all_to_all | solution.py:147
  184.4 13.8 %all-to-all-done.3 = f32[4,72,896]{2,1,0:T(8,128)S(1)} async-done(((f32[4,72,896]{2,1,0:T(8,128)}), f32[4,72,896]{2,1,0:T(8,128)S(1)}, u32[]{:S(2)}, u32[]{:S(2)}) %all-to-all-start.3) | async-done | bytes 1032224 | tf_op jit(solution)/shard_map/first_product/all_to_all | solution.py:147
  199.3 14.1 %all_gather.15 = f32[288,896]{1,0:T(8,128)S(1)} all-gather(f32[72,896]{1,0:T(8,128)S(1)} %multiply_add_fusion), channel_id=1, replica_groups={{0,16,32,48},{64,80,96,112},{128,144,160,176},{192,208,224,240},{256,27..., dimensions={0}, use_global_device_ids=true | all-gather | bytes 1290240 | tf_op jit(solution)/shard_map/first_product/all_gather | solution.py:150
  221.8 3.9 %collective-permute-start.9 = (f32[288,112]{1,0:T(8,128)S(1)}, f32[288,112]{1,0:T(8,128)S(1)}, u32[]{:S(2)}, u32[]{:S(2)}) collective-permute-start(f32[288,112]{1,0:T(8,128)S(1)} %get-tuple-element.10), channel_id=1, source_target_pairs={{0,64},{1,65},{64,128},{65,129},{128,192},{129,193},{192,0},{193,1... | collective-permute-start | bytes 387080 | tf_op jit(solution)/shard_map/second_product/ppermute | solution.py:38
  225.8 4.8 %collective-permute-start.7 = (f32[288,112]{1,0:T(8,128)S(1)}, f32[288,112]{1,0:T(8,128)S(1)}, u32[]{:S(2)}, u32[]{:S(2)}) collective-permute-start(f32[288,112]{1,0:T(8,128)S(1)} %get-tuple-element.11), channel_id=1, source_target_pairs={{0,128},{1,129},{64,192},{65,193},{128,0},{129,1},{192,64},{193,65... | collective-permute-start | bytes 387080 | tf_op jit(solution)/shard_map/second_product/ppermute | solution.py:38
  230.6 2.8 %collective-permute-start.8 = (f32[288,112]{1,0:T(8,128)S(1)}, f32[288,112]{1,0:T(8,128)S(1)}, u32[]{:S(2)}, u32[]{:S(2)}) collective-permute-start(f32[288,112]{1,0:T(8,128)S(1)} %get-tuple-element.12), channel_id=1, source_target_pairs={{0,192},{1,193},{64,0},{65,1},{128,64},{129,65},{192,128},{193,129... | collective-permute-start | bytes 387080 | tf_op jit(solution)/shard_map/second_product/ppermute | solution.py:38
  233.4 3.0 %collective-permute-start.6 = (f32[288,112]{1,0:T(8,128)S(1)}, f32[288,112]{1,0:T(8,128)S(1)}, u32[]{:S(2)}, u32[]{:S(2)}) collective-permute-start(f32[288,112]{1,0:T(8,128)S(1)} %get-tuple-element.9), channel_id=1, source_target_pairs={{0,64},{1,65},{64,128},{65,129},{128,192},{129,193},{192,0},{193,1... | collective-permute-start | bytes 387080 | tf_op jit(solution)/shard_map/second_product/ppermute | solution.py:38
  238.9 6.2 %collective-permute-start.12 = (f32[288,112]{1,0:T(8,128)S(1)}, f32[288,112]{1,0:T(8,128)S(1)}, u32[]{:S(2)}, u32[]{:S(2)}) collective-permute-start(f32[288,112]{1,0:T(8,128)S(1)} %add_add_fusion), channel_id=1, source_target_pairs={{0,256},{1,257},{64,320},{65,321},{128,384},{129,385},{192,448},{1... | collective-permute-start | bytes 387080 | tf_op jit(solution)/shard_map/swap_back/ppermute | solution.py:38
  245.1 12.2 %collective-permute-done.12 = f32[288,112]{1,0:T(8,128)S(1)} collective-permute-done((f32[288,112]{1,0:T(8,128)S(1)}, f32[288,112]{1,0:T(8,128)S(1)}, u32[]{:S(2)}, u32[]{:S(2)}) %collective-permute-start.12) | collective-permute-done | bytes 129056 | tf_op jit(solution)/shard_map/swap_back/ppermute | solution.py:38
  (59 shorter events, 30.0 us)
Async XLA Ops:
  1.1 24.0 %copy-start.3 = (f32[112,576]{0,1:T(8,128)}, f32[112,576]{0,1:T(8,128)S(1)}, u32[]{:S(2)}) copy-start(f32[112,576]{0,1:T(8,128)S(1)} %copy.22) | copy-start | bytes 774148
  1.1 22.4 %collective-permute-start = (f32[288,112]{1,0:T(8,128)S(1)}, f32[288,112]{1,0:T(8,128)S(1)}, u32[]{:S(2)}, u32[]{:S(2)}) collective-permute-start(f32[288,112]{1,0:T(8,128)S(1)} %constant_dynamic-slice_fusion), channel_id=1, source_target_pairs={{0,256},{1,257},{64,320},{65,321},{128,384},{129,385},{192,448},{1... | collective-permute-start | bytes 387080 | tf_op jit(solution)/shard_map/swap_columns/ppermute | solution.py:38
  25.1 29.2 %all-to-all-start = ((f32[4,72,896]{2,1,0:T(8,128)}), f32[4,72,896]{2,1,0:T(8,128)S(1)}, u32[]{:S(2)}, u32[]{:S(2)}) async-start(f32[4,72,896]{2,1,0:T(8,128)} %broadcast_in_dim.6), calls=%async_computation | async-start | bytes 2064384 | tf_op jit(solution)/shard_map/faces/all_to_all | solution.py:109
  56.7 5.3 %copy-start = (f32[288,896]{1,0:T(8,128)}, f32[288,896]{1,0:T(8,128)S(1)}, u32[]{:S(2)}) copy-start(f32[288,896]{1,0:T(8,128)S(1)} %reshape.51) | copy-start | bytes 3096580
  59.9 5.4 %collective-permute-start.1 = (f32[448,896]{1,0:T(8,128)S(1)}, f32[448,896]{1,0:T(8,128)S(1)}, u32[]{:S(2)}, u32[]{:S(2)}) collective-permute-start(f32[448,896]{1,0:T(8,128)S(1)} %fusion.5), channel_id=1, source_target_pairs={{0,1},{1,0},{64,65},{65,64},{128,129},{129,128},{192,193},{193,192... | collective-permute-start | bytes 4816904 | tf_op jit(solution)/shard_map/gram/ppermute | solution.py:38
  66.7 26.2 %all-to-all-start.1 = ((f32[4,112,896]{2,1,0:T(8,128)}), f32[4,112,896]{2,1,0:T(8,128)S(1)}, u32[]{:S(2)}, u32[]{:S(2)}) async-start(f32[4,112,896]{2,1,0:T(8,128)} %bitcast.50), calls=%async_computation.1 | async-start | bytes 3211264 | tf_op jit(solution)/shard_map/reduce_y/all_to_all | solution.py:123
  93.0 22.7 %collective-permute-start.2 = (f32[25,8,128]{2,1,0:T(8,128)S(1)}, f32[25,8,128]{2,1,0:T(8,128)S(1)}, u32[]{:S(2)}, u32[]{:S(2)}) collective-permute-start(f32[25,8,128]{2,1,0:T(8,128)S(1)} %get-tuple-element.17), channel_id=1, source_target_pairs={{0,2},{1,3},{64,66},{65,67},{128,130},{129,131},{192,194},{193,195... | collective-permute-start | bytes 307208 | tf_op jit(solution)/shard_map/reduce_a/ppermute | solution.py:38
  106.0 17.7 %collective-permute-start.4 = (f32[25,8,128]{2,1,0:T(8,128)S(1)}, f32[25,8,128]{2,1,0:T(8,128)S(1)}, u32[]{:S(2)}, u32[]{:S(2)}) collective-permute-start(f32[25,8,128]{2,1,0:T(8,128)S(1)} %get-tuple-element.18), channel_id=1, source_target_pairs={{0,258},{1,259},{64,322},{65,323},{128,386},{129,387},{192,450},{1... | collective-permute-start | bytes 307208 | tf_op jit(solution)/shard_map/reduce_a/ppermute | solution.py:38
  108.6 15.0 %collective-permute-start.3 = (f32[25,8,128]{2,1,0:T(8,128)S(1)}, f32[25,8,128]{2,1,0:T(8,128)S(1)}, u32[]{:S(2)}, u32[]{:S(2)}) collective-permute-start(f32[25,8,128]{2,1,0:T(8,128)S(1)} %get-tuple-element.19), channel_id=1, source_target_pairs={{0,256},{1,257},{64,320},{65,321},{128,384},{129,385},{192,448},{1... | collective-permute-start | bytes 307208 | tf_op jit(solution)/shard_map/reduce_a/ppermute | solution.py:38
  171.5 5.3 %collective-permute-start.5 = (f32[448,896]{1,0:T(8,128)S(1)}, f32[448,896]{1,0:T(8,128)S(1)}, u32[]{:S(2)}, u32[]{:S(2)}) collective-permute-start(f32[448,896]{1,0:T(8,128)S(1)} %bitcast.47), channel_id=1, source_target_pairs={{0,1},{1,0},{64,65},{65,64},{128,129},{129,128},{192,193},{193,192... | collective-permute-start | bytes 4816904 | tf_op jit(solution)/shard_map/gather_core/ppermute | solution.py:38
  176.8 3.1 %copy-start.1 = (f32[448,896]{1,0:T(8,128)}, f32[448,896]{1,0:T(8,128)S(1)}, u32[]{:S(2)}) copy-start(f32[448,896]{1,0:T(8,128)S(1)} %collective-permute-done.5) | copy-start | bytes 4816900
  179.9 18.3 %all-to-all-start.3 = ((f32[4,72,896]{2,1,0:T(8,128)}), f32[4,72,896]{2,1,0:T(8,128)S(1)}, u32[]{:S(2)}, u32[]{:S(2)}) async-start(f32[4,72,896]{2,1,0:T(8,128)} %bitcast.53), calls=%async_computation.3 | async-start | bytes 2064384 | tf_op jit(solution)/shard_map/first_product/all_to_all | solution.py:147
  213.3 2.1 copy-start.2
  217.7 39.8 %copy-start.4 = (f32[112,576]{0,1:T(8,128)S(1)}, f32[112,576]{0,1:T(8,128)}, u32[]{:S(2)}) copy-start(f32[112,576]{0,1:T(8,128)} %copy-done.3) | copy-start | bytes 774148
  217.7 15.7 %collective-permute-start.11 = (f32[288,112]{1,0:T(8,128)S(1)}, f32[288,112]{1,0:T(8,128)S(1)}, u32[]{:S(2)}, u32[]{:S(2)}) collective-permute-start(f32[288,112]{1,0:T(8,128)S(1)} %get-tuple-element.13), channel_id=1, source_target_pairs={{0,192},{1,193},{64,0},{65,1},{128,64},{129,65},{192,128},{193,129... | collective-permute-start | bytes 387080 | tf_op jit(solution)/shard_map/second_product/ppermute | solution.py:38
  219.8 19.0 %collective-permute-start.10 = (f32[288,112]{1,0:T(8,128)S(1)}, f32[288,112]{1,0:T(8,128)S(1)}, u32[]{:S(2)}, u32[]{:S(2)}) collective-permute-start(f32[288,112]{1,0:T(8,128)S(1)} %get-tuple-element.14), channel_id=1, source_target_pairs={{0,128},{1,129},{64,192},{65,193},{128,0},{129,1},{192,64},{193,65... | collective-permute-start | bytes 387080 | tf_op jit(solution)/shard_map/second_product/ppermute | solution.py:38
  221.8 16.9 %collective-permute-start.9 = (f32[288,112]{1,0:T(8,128)S(1)}, f32[288,112]{1,0:T(8,128)S(1)}, u32[]{:S(2)}, u32[]{:S(2)}) collective-permute-start(f32[288,112]{1,0:T(8,128)S(1)} %get-tuple-element.10), channel_id=1, source_target_pairs={{0,64},{1,65},{64,128},{65,129},{128,192},{129,193},{192,0},{193,1... | collective-permute-start | bytes 387080 | tf_op jit(solution)/shard_map/second_product/ppermute | solution.py:38
  225.8 19.3 %collective-permute-start.7 = (f32[288,112]{1,0:T(8,128)S(1)}, f32[288,112]{1,0:T(8,128)S(1)}, u32[]{:S(2)}, u32[]{:S(2)}) collective-permute-start(f32[288,112]{1,0:T(8,128)S(1)} %get-tuple-element.11), channel_id=1, source_target_pairs={{0,128},{1,129},{64,192},{65,193},{128,0},{129,1},{192,64},{193,65... | collective-permute-start | bytes 387080 | tf_op jit(solution)/shard_map/second_product/ppermute | solution.py:38
  230.6 14.5 %collective-permute-start.8 = (f32[288,112]{1,0:T(8,128)S(1)}, f32[288,112]{1,0:T(8,128)S(1)}, u32[]{:S(2)}, u32[]{:S(2)}) collective-permute-start(f32[288,112]{1,0:T(8,128)S(1)} %get-tuple-element.12), channel_id=1, source_target_pairs={{0,192},{1,193},{64,0},{65,1},{128,64},{129,65},{192,128},{193,129... | collective-permute-start | bytes 387080 | tf_op jit(solution)/shard_map/second_product/ppermute | solution.py:38
  233.4 11.7 %collective-permute-start.6 = (f32[288,112]{1,0:T(8,128)S(1)}, f32[288,112]{1,0:T(8,128)S(1)}, u32[]{:S(2)}, u32[]{:S(2)}) collective-permute-start(f32[288,112]{1,0:T(8,128)S(1)} %get-tuple-element.9), channel_id=1, source_target_pairs={{0,64},{1,65},{64,128},{65,129},{128,192},{129,193},{192,0},{193,1... | collective-permute-start | bytes 387080 | tf_op jit(solution)/shard_map/second_product/ppermute | solution.py:38
  238.9 18.5 %collective-permute-start.12 = (f32[288,112]{1,0:T(8,128)S(1)}, f32[288,112]{1,0:T(8,128)S(1)}, u32[]{:S(2)}, u32[]{:S(2)}) collective-permute-start(f32[288,112]{1,0:T(8,128)S(1)} %add_add_fusion), channel_id=1, source_target_pairs={{0,256},{1,257},{64,320},{65,321},{128,384},{129,385},{192,448},{1... | collective-permute-start | bytes 387080 | tf_op jit(solution)/shard_map/swap_back/ppermute | solution.py:38

commit v6 on v5

--- a/solution.py
+++ b/solution.py
@@ -3,7 +3,8 @@
 import jax
 import jax.numpy as jnp
 from jax import lax
-from jax.experimental.layout import Layout, with_layout_constraint
+from jax.experimental import pallas as pl
+from jax.experimental.pallas import tpu as pltpu
 from jax.sharding import PartitionSpec as P
 
 M = 3584
@@ -56,21 +57,106 @@
     )
 
 
-def rows_at(value, start, size):
-    return lax.dynamic_slice_in_dim(value, start, size, 0)
-
-
-def in_rows(value):
-    return with_layout_constraint(value, Layout(major_to_minor=(0, 1)))
-
-
-def ordered(index, own, other):
-    return jnp.where(index == 0, own, other), jnp.where(index == 0, other, own)
-
-
-def joined(blocks, part, rows):
-    blocks = blocks.reshape(4, part, 4, 2 * rows).transpose(2, 1, 0, 3)
-    return blocks.reshape(4 * part, 8 * rows)
+def local(kernel, shapes, index, *arrays, scratch=()):
+    vmem = pl.BlockSpec(memory_space=pltpu.VMEM)
+    return pl.pallas_call(
+        kernel,
+        out_shape=[jax.ShapeDtypeStruct(shape, jnp.float32) for shape in shapes],
+        in_specs=[pl.BlockSpec(memory_space=pltpu.SMEM)] + [vmem] * len(arrays),
+        out_specs=[vmem] * len(shapes),
+        scratch_shapes=[pltpu.VMEM(shape, jnp.float32) for shape in scratch],
+        compiler_params=pltpu.CompilerParams(vmem_limit_bytes=24 * 2**20),
+    )(jnp.stack(index).astype(jnp.int32), *arrays)
+
+
+ROWS, DEPTH = 112, 288
+PACKED = (256, 128)
+
+
+def pack(packed, value):
+    packed[0:ROWS, :] = value[:, 0:128]
+    packed[ROWS : 2 * ROWS, :] = value[:, 128:256]
+    packed[240:256, :] = jnp.zeros((16, 128), jnp.float32)
+    for g in range(4):
+        n = min(32, ROWS - 32 * g)
+        packed[224 : 224 + n, 32 * g : 32 * g + 32] = value[32 * g : 32 * g + n, 256:DEPTH]
+
+
+def unpack(value, packed, at):
+    value[0:ROWS, at : at + 128] = packed[0:ROWS, :]
+    value[0:ROWS, at + 128 : at + 256] = packed[ROWS : 2 * ROWS, :]
+    for g in range(4):
+        n = min(32, ROWS - 32 * g)
+        value[32 * g : 32 * g + n, at + 256 : at + DEPTH] = packed[
+            224 : 224 + n, 32 * g : 32 * g + 32
+        ]
+
+
+def send_kernel(index, iterate, sent):
+    for q in range(2):
+
+        @pl.when(index[0] == q)
+        def _():
+            pack(sent, iterate[:, DEPTH * (1 - q) : DEPTH * (2 - q)])
+
+
+def block_kernel(index, iterate, other, block, blocks, wide):
+    part = DEPTH // 4
+
+    def place(q):
+        flipped = wide[...].T
+        for k in range(4):
+            at = k * 2 * ROWS + q * ROWS
+            value = flipped[k * part : (k + 1) * part, 0:ROWS]
+            block[:, at : at + ROWS] = value
+            for n in range(4):
+                blocks[n, :, at : at + ROWS] = value
+
+    for q in range(2):
+
+        @pl.when(index[0] == q)
+        def _():
+            wide[0:ROWS, 0:DEPTH] = iterate[:, DEPTH * q : DEPTH * (q + 1)]
+            place(q)
+            unpack(wide, other, 0)
+            place(1 - q)
+
+
+def faces_kernel(index, from_x, from_b, right, kept, given, mine):
+    b, core, x = index[0], index[1], index[2]
+    part, wide = DEPTH // 4, 2 * ROWS
+    for n in range(4):
+        for k in range(4):
+            rows, lanes = pl.ds(k * part, part), pl.ds(k * wide, wide)
+            right[rows, n * wide : (n + 1) * wide] = from_x[n, :, lanes]
+            face = (kept, given)[n // 2]
+            source = lax.rem(b + 2 * core + n, 4)
+            face[rows, n % 2 * wide : (n % 2 + 1) * wide] = from_b[source, :, lanes]
+    mine[...] = COEF_B * right[pl.ds(pl.multiple_of(x * part, 8), part), :]
+
+
+def tail_kernel(index, kept, given, *packed):
+    core, q = index[0], index[1]
+    for c in range(2):
+
+        @pl.when(core == c)
+        def _():
+            for s in range(4):
+                source = (kept, given)[(s // 2 + c) % 2]
+                for n, part in enumerate((1 - q, q)):
+                    at = pl.multiple_of(s % 2 * 2 * ROWS + part * ROWS, 8)
+                    pack(packed[4 * n + s], source[pl.ds(at, ROWS), :])
+
+
+def final_kernel(index, iterate, own, other, update):
+    for q in range(2):
+
+        @pl.when(index[0] == q)
+        def _():
+            unpack(update, own, DEPTH * q)
+            unpack(update, other, DEPTH * (1 - q))
+
+    update[...] = (COEF_A * iterate[...] + update[...]) * (0.2 * math.sqrt(max(M, N)))
 
 
 def tiles(value):
@@ -90,32 +176,31 @@
 
 
 def body(iterate):
-    rows, cols = iterate.shape
-    depth = cols // 2
+    part, size = DEPTH // 4, 8 * ROWS
+    half, chunk = size // 2, size // 8
     row, col = lax.axis_index("row"), lax.axis_index("col")
     core = col % 2
     a = col // 2 % 2 * 2 + row // 16
     x, b, q = row % 4, row // 4 % 4, row // 16
 
     with jax.named_scope("swap_columns"):
-        flipped = in_rows(iterate.T)
-        own = in_rows(rows_at(flipped, q * depth, depth))
-        other = in_rows(swap_q(in_rows(rows_at(flipped, (1 - q) * depth, depth))))
+        (sent,) = local(send_kernel, [PACKED], [q], iterate)
+        other = swap_q(sent)
     with jax.named_scope("faces"):
-        block = jnp.concatenate(ordered(q, own, other), 1)
-        part = depth // 4
-        block = block.reshape(4, part, 2 * rows).transpose(1, 0, 2).reshape(part, 8 * rows)
-        blocks = jnp.broadcast_to(block, (4,) + block.shape)
-        right = lax.all_to_all(blocks, "row", 0, 0, axis_index_groups=X_GROUPS)
-        right = joined(right, part, rows)
-        left = lax.all_gather(block, "row", axis=0, axis_index_groups=B_GROUPS)
-        left = rows_at(jnp.concatenate([left, left], 0), b, 4)
-        left = joined(left, part, rows)
-    size = 8 * rows
-    half, chunk = size // 2, size // 8
+        block, blocks = local(
+            block_kernel, [(part, size), (4, part, size)], [q], iterate, other, scratch=[(128, 384)]
+        )
+        from_x = lax.all_to_all(blocks, "row", 0, 0, axis_index_groups=X_GROUPS)
+        from_b = lax.all_gather(block, "row", axis=0, axis_index_groups=B_GROUPS)
+        right, kept, given, mine = local(
+            faces_kernel,
+            [(DEPTH, size), (DEPTH, half), (DEPTH, half), (part, size)],
+            [b, core, x],
+            from_x,
+            from_b,
+        )
 
     with jax.named_scope("gram"):
-        kept, given = ordered(core, left[:, :half], left[:, half:])
         partial = swap_core(dot(given, right, ((0,), (0,))))
         total = lax.optimization_barrier(dot(kept, right, ((0,), (0,))))
         total = total + partial
@@ -143,28 +228,25 @@
     with jax.named_scope("first_product"):
         product = lax.optimization_barrier(dot(kept, gram_kept, ((1,), (0,))))
         product = product + dot(given, gram_given, ((1,), (0,)))
-        parts = product.reshape(4, depth // 4, size)
+        parts = product.reshape(4, part, size)
         parts = lax.all_to_all(parts, "row", 0, 0, axis_index_groups=X_GROUPS)
-        mine = rows_at(right, x * (depth // 4), depth // 4)
-        inner = COEF_B * mine + COEF_C * jnp.sum(parts, 0)
+        inner = mine + COEF_C * jnp.sum(parts, 0)
         inner = lax.all_gather(inner, "row", axis=0, tiled=True, axis_index_groups=X_GROUPS)
     with jax.named_scope("second_product"):
-        near, far = ordered(
-            core,
-            in_rows(dot(inner, gram_kept, ((1,), (1,)))),
-            in_rows(dot(inner, gram_given, ((1,), (1,)))),
+        packed = local(
+            tail_kernel,
+            [PACKED] * 8,
+            [core, q],
+            dot(gram_kept, inner, ((1,), (1,))),
+            dot(gram_given, inner, ((1,), (1,))),
         )
         sums = []
-        for part in (1 - q, q):
-            blocks = []
-            for s in range(4):
-                value = (near, far)[s // 2][:, s % 2 * 2 * rows :][:, : 2 * rows]
-                block = in_rows(jnp.where(part == 0, value[:, :rows], value[:, rows:]))
-                blocks.append(b_shift(block, s) if s else block)
+        for blocks in (packed[:4], packed[4:]):
+            blocks = [b_shift(block, s) if s else block for s, block in enumerate(blocks)]
             sums.append(blocks[0] + blocks[1] + blocks[2] + blocks[3])
     with jax.named_scope("swap_back"):
-        applied = jnp.concatenate(ordered(q, sums[1], swap_q(sums[0])), 0).T
-    return (COEF_A * iterate + applied) * (0.2 * math.sqrt(max(M, N)))
+        other = swap_q(sums[0])
+        return local(final_kernel, [iterate.shape], [q], iterate, sums[1], other)[0]
 
 
 def solution(mesh):

time: 259 us -> 249 us (0.961)
  the two profiles are of different devices: /device:TPU:2 before, /device:TPU:8 now
where the time goes in v6:
time: 249 us; the launch traced here: 248 us
  blocking collectives  80.7 us (32%)
  starting transfers between devices  74.9 us (30%)
  waiting for transfers between devices  68.2 us (27%)
  matrix products  17.1 us (7%)
  Pallas kernels  4.3 us (2%)
    ppermute x13, starting transfers between devices, permute(): return lax.ppermute(value, AXES, pairs)  60.8 us
    ppermute x13, waiting for transfers between devices, permute(): return lax.ppermute(value, AXES, pairs)  33.2 us
    all_gather x1, blocking collectives, body(): pieces = lax.all_gather(piece, AXES, axis=0, axis_index_groups=A_GROUPS)  22.9 us
    all_gather x1, blocking collectives, body(): from_b = lax.all_gather(block, 'row', axis=0, axis_index_groups=B_GROUPS)  21.5 us
    all_to_all x1, blocking collectives, body(): parts = lax.all_to_all(parts, 'col', 0, 0, axis_index_groups=Y_GROUPS)  21.2 us
    all_to_all x1, waiting for transfers between devices, body(): lax.all_to_all(total.reshape(4, chunk, size), 'col', 0, 0, axis_index_gro...  19.9 us
    dot_general x6, matrix products, dot(): lax.dot_general(left, right, (dims, ((), ())), precision=PREC, preferred_...  17.1 us
    all_gather x1, blocking collectives, body(): lax.all_gather(inner, 'row', axis=0, tiled=True, axis_index_groups=X_GROUPS)  15.2 us
  transfers between devices with their start and end apart: 16, of which 10 were waited for; matrix products, arithmetic and copies ran while one was open for 2% of the time, Pallas kernels for 0%

profile of v6, /device:TPU:8, one launch (start us, length us, event | category | flops | bytes accessed | tf_op | source)
XLA Modules:
  0.0 248.5 jit_solution(14773259200030270467)
XLA Ops:
  1.1 9.0 %collective-permute-start = (f32[256,128]{1,0:T(8,128)S(1)}, f32[256,128]{1,0:T(8,128)S(1)}, u32[]{:S(2)}, u32[]{:S(2)}) collective-permute-start(f32[256,128]{1,0:T(8,128)S(1)} %swap_columns.1), channel_id=1, source_target_pairs={{0,256},{1,257},{64,320},{65,321},{128,384},{129,385},{192,448},{1... | collective-permute-start | bytes 393224 | tf_op jit(solution)/shard_map/swap_columns/ppermute | solution.py:39
  10.1 11.9 %collective-permute-done.other = f32[256,128]{1,0:T(8,128)S(1)} collective-permute-done((f32[256,128]{1,0:T(8,128)S(1)}, f32[256,128]{1,0:T(8,128)S(1)}, u32[]{:S(2)}, u32[]{:S(2)}) %collective-permute-start) | collective-permute-done | bytes 131104 | tf_op jit(solution)/shard_map/swap_columns/ppermute | solution.py:39
  23.4 4.3 %all-to-all-start = ((f32[4,72,896]{2,1,0:T(8,128)}), f32[4,72,896]{2,1,0:T(8,128)S(1)}, u32[]{:S(2)}, u32[]{:S(2)}) async-start(f32[4,72,896]{2,1,0:T(8,128)} %get-tuple-element.19), calls=%async_computation | async-start | bytes 2064384 | tf_op jit(solution)/shard_map/faces/all_to_all | solution.py:193
  27.8 21.5 %all-gather = f32[288,896]{1,0:T(8,128)S(1)} all-gather(f32[72,896]{1,0:T(8,128)S(1)} %get-tuple-element.20), channel_id=2, replica_groups={{0,64,128,192},{16,80,144,208},{32,96,160,224},{48,112,176,240},{256,32..., dimensions={0}, use_global_device_ids=true | all-gather | bytes 1290240 | tf_op jit(solution)/shard_map/faces/all_gather | solution.py:194
  50.5 3.0 %fusion.3 = f32[448,896]{1,0:T(8,128)S(1)} fusion(f32[288,448]{1,0:T(8,128)S(1)} %get-tuple-element.23, f32[288,896]{1,0:T(8,128)S(1)} %get-tuple-element.22), kind=kOutput, calls=%fused_computation.13 | convolution fusion | flops 1387266048 | bytes 3153920 | tf_op jit(solution)/shard_map/gram/dot_general | solution.py:55
  55.4 3.0 %fusion.2 = f32[448,896]{1,0:T(8,128)S(1)} fusion(f32[288,448]{1,0:T(8,128)S(1)} %get-tuple-element.21, f32[288,896]{1,0:T(8,128)S(1)} %get-tuple-element.22), kind=kOutput, calls=%fused_computation.12 | convolution fusion | flops 1387266048 | bytes 3153920 | tf_op jit(solution)/shard_map/gram/dot_general | solution.py:55
  60.2 4.9 %all-to-all-start.1 = ((f32[4,112,896]{2,1,0:T(8,128)}), f32[4,112,896]{2,1,0:T(8,128)S(1)}, u32[]{:S(2)}, u32[]{:S(2)}) async-start(f32[4,112,896]{2,1,0:T(8,128)} %bitcast.47), calls=%async_computation.1 | async-start | bytes 3211264 | tf_op jit(solution)/shard_map/reduce_y/all_to_all | solution.py:208
  65.1 19.9 %all-to-all-done.1 = f32[4,112,896]{2,1,0:T(8,128)S(1)} async-done(((f32[4,112,896]{2,1,0:T(8,128)}), f32[4,112,896]{2,1,0:T(8,128)S(1)}, u32[]{:S(2)}, u32[]{:S(2)}) %all-to-all-start.1) | async-done | bytes 1605664 | tf_op jit(solution)/shard_map/reduce_y/all_to_all | solution.py:208
  85.2 13.3 %collective-permute-start.2 = (f32[25,8,128]{2,1,0:T(8,128)S(1)}, f32[25,8,128]{2,1,0:T(8,128)S(1)}, u32[]{:S(2)}, u32[]{:S(2)}) collective-permute-start(f32[25,8,128]{2,1,0:T(8,128)S(1)} %get-tuple-element.33), channel_id=1, source_target_pairs={{0,2},{1,3},{64,66},{65,67},{128,130},{129,131},{192,194},{193,195... | collective-permute-start | bytes 307208 | tf_op jit(solution)/shard_map/reduce_a/ppermute | solution.py:39
  98.5 4.7 %collective-permute-start.3 = (f32[25,8,128]{2,1,0:T(8,128)S(1)}, f32[25,8,128]{2,1,0:T(8,128)S(1)}, u32[]{:S(2)}, u32[]{:S(2)}) collective-permute-start(f32[25,8,128]{2,1,0:T(8,128)S(1)} %get-tuple-element.35), channel_id=1, source_target_pairs={{0,256},{1,257},{64,320},{65,321},{128,384},{129,385},{192,448},{1... | collective-permute-start | bytes 307208 | tf_op jit(solution)/shard_map/reduce_a/ppermute | solution.py:39
  103.2 5.0 %collective-permute-start.4 = (f32[25,8,128]{2,1,0:T(8,128)S(1)}, f32[25,8,128]{2,1,0:T(8,128)S(1)}, u32[]{:S(2)}, u32[]{:S(2)}) collective-permute-start(f32[25,8,128]{2,1,0:T(8,128)S(1)} %get-tuple-element.34), channel_id=1, source_target_pairs={{0,258},{1,259},{64,322},{65,323},{128,386},{129,387},{192,450},{1... | collective-permute-start | bytes 307208 | tf_op jit(solution)/shard_map/reduce_a/ppermute | solution.py:39
  108.2 5.5 %collective-permute-done.3 = f32[25,8,128]{2,1,0:T(8,128)S(1)} collective-permute-done((f32[25,8,128]{2,1,0:T(8,128)S(1)}, f32[25,8,128]{2,1,0:T(8,128)S(1)}, u32[]{:S(2)}, u32[]{:S(2)}) %collective-permute-start.3) | collective-permute-done | bytes 102432 | tf_op jit(solution)/shard_map/reduce_a/ppermute | solution.py:39
  113.8 3.0 %collective-permute-done.4 = f32[25,8,128]{2,1,0:T(8,128)S(1)} collective-permute-done((f32[25,8,128]{2,1,0:T(8,128)S(1)}, f32[25,8,128]{2,1,0:T(8,128)S(1)}, u32[]{:S(2)}, u32[]{:S(2)}) %collective-permute-start.4) | collective-permute-done | bytes 102432 | tf_op jit(solution)/shard_map/reduce_a/ppermute | solution.py:39
  116.8 22.9 %all-gather.1 = f32[100,8,128]{2,1,0:T(8,128)S(1)} all-gather(f32[25,8,128]{2,1,0:T(8,128)S(1)} %fusion.1), channel_id=3, replica_groups={{0,256,2,258},{1,257,3,259},{64,320,66,322},{65,321,67,323},{128,384,13..., dimensions={0}, use_global_device_ids=true | all-gather | bytes 512000 | tf_op jit(solution)/shard_map/gather_a/all_gather | solution.py:219
  139.8 21.2 %all_to_all.20 = f32[4,112,896]{2,1,0:T(8,128)S(1)} all-to-all(f32[4,112,896]{2,1,0:T(8,128)S(1)} %broadcast_in_dim.3), channel_id=1, replica_groups={{0,4,8,12},{1,5,9,13},{2,6,10,14},{3,7,11,15},{16,20,24,28},{17,21,25,2..., dimensions={0} | all-to-all | bytes 3211264 | tf_op jit(solution)/shard_map/gather_y/all_to_all | solution.py:223
  166.4 3.1 %convolution_add_fusion = f32[288,896]{1,0:T(8,128)} fusion(f32[288,896]{1,0:T(8,128)S(1)} %fusion.4, f32[288,448]{1,0:T(8,128)S(1)} %get-tuple-element.23, f32[448,896]{1,0:T(8,128)S(1)} %collective-permute-done.5), kind=kOutput, calls=%fused_computation | convolution fusion | flops 1387524096 | bytes 4186112 | tf_op jit(solution)/shard_map/first_product/dot_general | solution.py:55
  169.5 4.9 %all-to-all-start.3 = ((f32[4,72,896]{2,1,0:T(8,128)}), f32[4,72,896]{2,1,0:T(8,128)S(1)}, u32[]{:S(2)}, u32[]{:S(2)}) async-start(f32[4,72,896]{2,1,0:T(8,128)} %bitcast.48), calls=%async_computation.3 | async-start | bytes 2064384 | tf_op jit(solution)/shard_map/first_product/all_to_all | solution.py:232
  174.5 15.1 %all-to-all-done.3 = f32[4,72,896]{2,1,0:T(8,128)S(1)} async-done(((f32[4,72,896]{2,1,0:T(8,128)}), f32[4,72,896]{2,1,0:T(8,128)S(1)}, u32[]{:S(2)}, u32[]{:S(2)}) %all-to-all-start.3) | async-done | bytes 1032224 | tf_op jit(solution)/shard_map/first_product/all_to_all | solution.py:232
  189.7 15.2 %all_gather.19 = f32[288,896]{1,0:T(8,128)S(1)} all-gather(f32[72,896]{1,0:T(8,128)S(1)} %multiply_add_fusion), channel_id=1, replica_groups={{0,16,32,48},{64,80,96,112},{128,144,160,176},{192,208,224,240},{256,27..., dimensions={0}, use_global_device_ids=true | all-gather | bytes 1290240 | tf_op jit(solution)/shard_map/first_product/all_gather | solution.py:234
  213.5 5.7 %collective-permute-start.11 = (f32[256,128]{1,0:T(8,128)S(1)}, f32[256,128]{1,0:T(8,128)S(1)}, u32[]{:S(2)}, u32[]{:S(2)}) collective-permute-start(f32[256,128]{1,0:T(8,128)S(1)} %get-tuple-element.32), channel_id=1, source_target_pairs={{0,192},{1,193},{64,0},{65,1},{128,64},{129,65},{192,128},{193,129... | collective-permute-start | bytes 393224 | tf_op jit(solution)/shard_map/second_product/ppermute | solution.py:39
  221.7 3.9 %collective-permute-start.6 = (f32[256,128]{1,0:T(8,128)S(1)}, f32[256,128]{1,0:T(8,128)S(1)}, u32[]{:S(2)}, u32[]{:S(2)}) collective-permute-start(f32[256,128]{1,0:T(8,128)S(1)} %get-tuple-element.26), channel_id=1, source_target_pairs={{0,64},{1,65},{64,128},{65,129},{128,192},{129,193},{192,0},{193,1... | collective-permute-start | bytes 393224 | tf_op jit(solution)/shard_map/second_product/ppermute | solution.py:39
  225.6 3.7 %collective-permute-start.7 = (f32[256,128]{1,0:T(8,128)S(1)}, f32[256,128]{1,0:T(8,128)S(1)}, u32[]{:S(2)}, u32[]{:S(2)}) collective-permute-start(f32[256,128]{1,0:T(8,128)S(1)} %get-tuple-element.27), channel_id=1, source_target_pairs={{0,128},{1,129},{64,192},{65,193},{128,0},{129,1},{192,64},{193,65... | collective-permute-start | bytes 393224 | tf_op jit(solution)/shard_map/second_product/ppermute | solution.py:39
  231.9 4.5 %collective-permute-start.12 = (f32[256,128]{1,0:T(8,128)S(1)}, f32[256,128]{1,0:T(8,128)S(1)}, u32[]{:S(2)}, u32[]{:S(2)}) collective-permute-start(f32[256,128]{1,0:T(8,128)S(1)} %add_add_fusion), channel_id=1, source_target_pairs={{0,256},{1,257},{64,320},{65,321},{128,384},{129,385},{192,448},{1... | collective-permute-start | bytes 393224 | tf_op jit(solution)/shard_map/swap_back/ppermute | solution.py:39
  238.3 9.3 %collective-permute-done.12.other = f32[256,128]{1,0:T(8,128)S(1)} collective-permute-done((f32[256,128]{1,0:T(8,128)S(1)}, f32[256,128]{1,0:T(8,128)S(1)}, u32[]{:S(2)}, u32[]{:S(2)}) %collective-permute-start.12) | collective-permute-done | bytes 131104 | tf_op jit(solution)/shard_map/swap_back/ppermute | solution.py:39
  (44 shorter events, 29.5 us)
Async XLA Ops:
  0.0 1.0 copy-start
  1.1 21.0 %collective-permute-start = (f32[256,128]{1,0:T(8,128)S(1)}, f32[256,128]{1,0:T(8,128)S(1)}, u32[]{:S(2)}, u32[]{:S(2)}) collective-permute-start(f32[256,128]{1,0:T(8,128)S(1)} %swap_columns.1), channel_id=1, source_target_pairs={{0,256},{1,257},{64,320},{65,321},{128,384},{129,385},{192,448},{1... | collective-permute-start | bytes 393224 | tf_op jit(solution)/shard_map/swap_columns/ppermute | solution.py:39
  23.4 25.9 %all-to-all-start = ((f32[4,72,896]{2,1,0:T(8,128)}), f32[4,72,896]{2,1,0:T(8,128)S(1)}, u32[]{:S(2)}, u32[]{:S(2)}) async-start(f32[4,72,896]{2,1,0:T(8,128)} %get-tuple-element.19), calls=%async_computation | async-start | bytes 2064384 | tf_op jit(solution)/shard_map/faces/all_to_all | solution.py:193
  53.5 5.4 %collective-permute-start.1 = (f32[448,896]{1,0:T(8,128)S(1)}, f32[448,896]{1,0:T(8,128)S(1)}, u32[]{:S(2)}, u32[]{:S(2)}) collective-permute-start(f32[448,896]{1,0:T(8,128)S(1)} %fusion.3), channel_id=1, source_target_pairs={{0,1},{1,0},{64,65},{65,64},{128,129},{129,128},{192,193},{193,192... | collective-permute-start | bytes 4816904 | tf_op jit(solution)/shard_map/gram/ppermute | solution.py:39
  60.2 24.8 %all-to-all-start.1 = ((f32[4,112,896]{2,1,0:T(8,128)}), f32[4,112,896]{2,1,0:T(8,128)S(1)}, u32[]{:S(2)}, u32[]{:S(2)}) async-start(f32[4,112,896]{2,1,0:T(8,128)} %bitcast.47), calls=%async_computation.1 | async-start | bytes 3211264 | tf_op jit(solution)/shard_map/reduce_y/all_to_all | solution.py:208
  85.2 23.1 %collective-permute-start.2 = (f32[25,8,128]{2,1,0:T(8,128)S(1)}, f32[25,8,128]{2,1,0:T(8,128)S(1)}, u32[]{:S(2)}, u32[]{:S(2)}) collective-permute-start(f32[25,8,128]{2,1,0:T(8,128)S(1)} %get-tuple-element.33), channel_id=1, source_target_pairs={{0,2},{1,3},{64,66},{65,67},{128,130},{129,131},{192,194},{193,195... | collective-permute-start | bytes 307208 | tf_op jit(solution)/shard_map/reduce_a/ppermute | solution.py:39
  98.5 15.3 %collective-permute-start.3 = (f32[25,8,128]{2,1,0:T(8,128)S(1)}, f32[25,8,128]{2,1,0:T(8,128)S(1)}, u32[]{:S(2)}, u32[]{:S(2)}) collective-permute-start(f32[25,8,128]{2,1,0:T(8,128)S(1)} %get-tuple-element.35), channel_id=1, source_target_pairs={{0,256},{1,257},{64,320},{65,321},{128,384},{129,385},{192,448},{1... | collective-permute-start | bytes 307208 | tf_op jit(solution)/shard_map/reduce_a/ppermute | solution.py:39
  103.2 13.6 %collective-permute-start.4 = (f32[25,8,128]{2,1,0:T(8,128)S(1)}, f32[25,8,128]{2,1,0:T(8,128)S(1)}, u32[]{:S(2)}, u32[]{:S(2)}) collective-permute-start(f32[25,8,128]{2,1,0:T(8,128)S(1)} %get-tuple-element.34), channel_id=1, source_target_pairs={{0,258},{1,259},{64,322},{65,323},{128,386},{129,387},{192,450},{1... | collective-permute-start | bytes 307208 | tf_op jit(solution)/shard_map/reduce_a/ppermute | solution.py:39
  161.1 5.3 %collective-permute-start.5 = (f32[448,896]{1,0:T(8,128)S(1)}, f32[448,896]{1,0:T(8,128)S(1)}, u32[]{:S(2)}, u32[]{:S(2)}) collective-permute-start(f32[448,896]{1,0:T(8,128)S(1)} %bitcast.44), channel_id=1, source_target_pairs={{0,1},{1,0},{64,65},{65,64},{128,129},{129,128},{192,193},{193,192... | collective-permute-start | bytes 4816904 | tf_op jit(solution)/shard_map/gather_core/ppermute | solution.py:39
  166.4 3.1 %copy-start.2 = (f32[448,896]{1,0:T(8,128)}, f32[448,896]{1,0:T(8,128)S(1)}, u32[]{:S(2)}) copy-start(f32[448,896]{1,0:T(8,128)S(1)} %collective-permute-done.5) | copy-start | bytes 4816900
  169.5 20.1 %all-to-all-start.3 = ((f32[4,72,896]{2,1,0:T(8,128)}), f32[4,72,896]{2,1,0:T(8,128)S(1)}, u32[]{:S(2)}, u32[]{:S(2)}) async-start(f32[4,72,896]{2,1,0:T(8,128)} %bitcast.48), calls=%async_computation.3 | async-start | bytes 2064384 | tf_op jit(solution)/shard_map/first_product/all_to_all | solution.py:232
  204.9 3.0 %copy-start.3 = (f32[448,896]{1,0:T(8,128)S(1)}, f32[448,896]{1,0:T(8,128)}, u32[]{:S(2)}) copy-start(f32[448,896]{1,0:T(8,128)} %copy-done.2) | copy-start | bytes 4816900
  210.8 36.8 %copy-start.1 = (f32[112,576]{1,0:T(8,128)S(1)}, f32[112,576]{1,0:T(8,128)}, u32[]{:S(2)}) copy-start(f32[112,576]{1,0:T(8,128)} %iterate.5) | copy-start | bytes 774148
  211.5 17.8 %collective-permute-start.10 = (f32[256,128]{1,0:T(8,128)S(1)}, f32[256,128]{1,0:T(8,128)S(1)}, u32[]{:S(2)}, u32[]{:S(2)}) collective-permute-start(f32[256,128]{1,0:T(8,128)S(1)} %get-tuple-element.31), channel_id=1, source_target_pairs={{0,128},{1,129},{64,192},{65,193},{128,0},{129,1},{192,64},{193,65... | collective-permute-start | bytes 393224 | tf_op jit(solution)/shard_map/second_product/ppermute | solution.py:39
  213.5 18.4 %collective-permute-start.11 = (f32[256,128]{1,0:T(8,128)S(1)}, f32[256,128]{1,0:T(8,128)S(1)}, u32[]{:S(2)}, u32[]{:S(2)}) collective-permute-start(f32[256,128]{1,0:T(8,128)S(1)} %get-tuple-element.32), channel_id=1, source_target_pairs={{0,192},{1,193},{64,0},{65,1},{128,64},{129,65},{192,128},{193,129... | collective-permute-start | bytes 393224 | tf_op jit(solution)/shard_map/second_product/ppermute | solution.py:39
  219.2 12.6 %collective-permute-start.9 = (f32[256,128]{1,0:T(8,128)S(1)}, f32[256,128]{1,0:T(8,128)S(1)}, u32[]{:S(2)}, u32[]{:S(2)}) collective-permute-start(f32[256,128]{1,0:T(8,128)S(1)} %get-tuple-element.30), channel_id=1, source_target_pairs={{0,64},{1,65},{64,128},{65,129},{128,192},{129,193},{192,0},{193,1... | collective-permute-start | bytes 393224 | tf_op jit(solution)/shard_map/second_product/ppermute | solution.py:39
  221.7 14.7 %collective-permute-start.6 = (f32[256,128]{1,0:T(8,128)S(1)}, f32[256,128]{1,0:T(8,128)S(1)}, u32[]{:S(2)}, u32[]{:S(2)}) collective-permute-start(f32[256,128]{1,0:T(8,128)S(1)} %get-tuple-element.26), channel_id=1, source_target_pairs={{0,64},{1,65},{64,128},{65,129},{128,192},{129,193},{192,0},{193,1... | collective-permute-start | bytes 393224 | tf_op jit(solution)/shard_map/second_product/ppermute | solution.py:39
  225.6 11.7 %collective-permute-start.7 = (f32[256,128]{1,0:T(8,128)S(1)}, f32[256,128]{1,0:T(8,128)S(1)}, u32[]{:S(2)}, u32[]{:S(2)}) collective-permute-start(f32[256,128]{1,0:T(8,128)S(1)} %get-tuple-element.27), channel_id=1, source_target_pairs={{0,128},{1,129},{64,192},{65,193},{128,0},{129,1},{192,64},{193,65... | collective-permute-start | bytes 393224 | tf_op jit(solution)/shard_map/second_product/ppermute | solution.py:39
  229.4 8.9 %collective-permute-start.8 = (f32[256,128]{1,0:T(8,128)S(1)}, f32[256,128]{1,0:T(8,128)S(1)}, u32[]{:S(2)}, u32[]{:S(2)}) collective-permute-start(f32[256,128]{1,0:T(8,128)S(1)} %get-tuple-element.28), channel_id=1, source_target_pairs={{0,192},{1,193},{64,0},{65,1},{128,64},{129,65},{192,128},{193,129... | collective-permute-start | bytes 393224 | tf_op jit(solution)/shard_map/second_product/ppermute | solution.py:39
  231.9 15.7 %collective-permute-start.12 = (f32[256,128]{1,0:T(8,128)S(1)}, f32[256,128]{1,0:T(8,128)S(1)}, u32[]{:S(2)}, u32[]{:S(2)}) collective-permute-start(f32[256,128]{1,0:T(8,128)S(1)} %add_add_fusion), channel_id=1, source_target_pairs={{0,256},{1,257},{64,320},{65,321},{128,384},{129,385},{192,448},{1... | collective-permute-start | bytes 393224 | tf_op jit(solution)/shard_map/swap_back/ppermute | solution.py:39

commit v7 on v6

--- a/solution.py
+++ b/solution.py
@@ -65,7 +65,7 @@
         in_specs=[pl.BlockSpec(memory_space=pltpu.SMEM)] + [vmem] * len(arrays),
         out_specs=[vmem] * len(shapes),
         scratch_shapes=[pltpu.VMEM(shape, jnp.float32) for shape in scratch],
-        compiler_params=pltpu.CompilerParams(vmem_limit_bytes=24 * 2**20),
+        compiler_params=pltpu.CompilerParams(vmem_limit_bytes=16 * 2**20),
     )(jnp.stack(index).astype(jnp.int32), *arrays)
 
 
@@ -92,15 +92,16 @@
         ]
 
 
-def send_kernel(index, iterate, sent):
+def send_kernel(index, iterate, sent, own):
     for q in range(2):
 
         @pl.when(index[0] == q)
         def _():
             pack(sent, iterate[:, DEPTH * (1 - q) : DEPTH * (2 - q)])
-
-
-def block_kernel(index, iterate, other, block, blocks, wide):
+            own[...] = iterate[:, DEPTH * q : DEPTH * (q + 1)]
+
+
+def block_kernel(index, own, other, block, blocks, wide):
     part = DEPTH // 4
 
     def place(q):
@@ -109,17 +110,18 @@
             at = k * 2 * ROWS + q * ROWS
             value = flipped[k * part : (k + 1) * part, 0:ROWS]
             block[:, at : at + ROWS] = value
-            for n in range(4):
-                blocks[n, :, at : at + ROWS] = value
 
     for q in range(2):
 
         @pl.when(index[0] == q)
         def _():
-            wide[0:ROWS, 0:DEPTH] = iterate[:, DEPTH * q : DEPTH * (q + 1)]
+            wide[0:ROWS, 0:DEPTH] = own[...]
             place(q)
             unpack(wide, other, 0)
             place(1 - q)
+
+    for n in range(4):
+        blocks[n, :, :] = block[...]
 
 
 def faces_kernel(index, from_x, from_b, right, kept, given, mine):
@@ -135,28 +137,61 @@
     mine[...] = COEF_B * right[pl.ds(pl.multiple_of(x * part, 8), part), :]
 
 
-def tail_kernel(index, kept, given, *packed):
+def split(value):
+    first = value.astype(jnp.bfloat16)
+    value = value - first.astype(jnp.float32)
+    second = value.astype(jnp.bfloat16)
+    value = value - second.astype(jnp.float32)
+    return first, second, value.astype(jnp.bfloat16)
+
+
+def gram_kernel(index, left, right, product):
+    deep, dims = 256, (((0,), (0,)), ((), ()))
+    one = split(left[deep:DEPTH, :])
+    two = split(right[deep:DEPTH, :])
+    pairs = ((0, 0), (0, 1), (1, 0), (1, 1), (0, 2), (2, 0))
+    rest = lax.dot_general(
+        jnp.concatenate([one[i] for i, _ in pairs], 0),
+        jnp.concatenate([two[j] for _, j in pairs], 0),
+        dims,
+        preferred_element_type=jnp.float32,
+    )
+    product[...] = rest + dot(left[0:deep, :], right[0:deep, :], dims[0])
+
+
+def tail_kernel(index, kept, given, *refs):
     core, q = index[0], index[1]
+    packed, kept_rows, given_rows = refs[:8], refs[8], refs[9]
+    kept_rows[...] = kept[...].T
+    given_rows[...] = given[...].T
     for c in range(2):
 
         @pl.when(core == c)
         def _():
             for s in range(4):
-                source = (kept, given)[(s // 2 + c) % 2]
+                source = (kept_rows, given_rows)[(s // 2 + c) % 2]
                 for n, part in enumerate((1 - q, q)):
                     at = pl.multiple_of(s % 2 * 2 * ROWS + part * ROWS, 8)
                     pack(packed[4 * n + s], source[pl.ds(at, ROWS), :])
 
 
 def final_kernel(index, iterate, own, other, update):
+    scale = 0.2 * math.sqrt(max(M, N))
+
+    def put(rows, lanes, applied):
+        update[rows, lanes] = (COEF_A * iterate[rows, lanes] + applied) * scale
+
     for q in range(2):
 
         @pl.when(index[0] == q)
         def _():
-            unpack(update, own, DEPTH * q)
-            unpack(update, other, DEPTH * (1 - q))
-
-    update[...] = (COEF_A * iterate[...] + update[...]) * (0.2 * math.sqrt(max(M, N)))
+            for packed, at in ((own, DEPTH * q), (other, DEPTH * (1 - q))):
+                put(slice(0, ROWS), slice(at, at + 128), packed[0:ROWS, :])
+                put(slice(0, ROWS), slice(at + 128, at + 256), packed[ROWS : 2 * ROWS, :])
+                for g in range(4):
+                    n = min(32, ROWS - 32 * g)
+                    rest = packed[224 : 224 + n, 32 * g : 32 * g + 32]
+                    put(slice(32 * g, 32 * g + n), slice(at + 256, at + DEPTH), rest)
 
 
 def tiles(value):
@@ -184,11 +219,11 @@
     x, b, q = row % 4, row // 4 % 4, row // 16
 
     with jax.named_scope("swap_columns"):
-        (sent,) = local(send_kernel, [PACKED], [q], iterate)
+        sent, own = local(send_kernel, [PACKED, (ROWS, DEPTH)], [q], iterate)
         other = swap_q(sent)
     with jax.named_scope("faces"):
         block, blocks = local(
-            block_kernel, [(part, size), (4, part, size)], [q], iterate, other, scratch=[(128, 384)]
+            block_kernel, [(part, size), (4, part, size)], [q], own, other, scratch=[(128, 384)]
         )
         from_x = lax.all_to_all(blocks, "row", 0, 0, axis_index_groups=X_GROUPS)
         from_b = lax.all_gather(block, "row", axis=0, axis_index_groups=B_GROUPS)
@@ -201,8 +236,9 @@
         )
 
     with jax.named_scope("gram"):
-        partial = swap_core(dot(given, right, ((0,), (0,))))
-        total = lax.optimization_barrier(dot(kept, right, ((0,), (0,))))
+        (partial,) = local(gram_kernel, [(half, size)], [core], given, right)
+        partial = swap_core(partial)
+        (total,) = local(gram_kernel, [(half, size)], [core], kept, right)
         total = total + partial
     with jax.named_scope("reduce_y"):
         parts = lax.all_to_all(
@@ -237,8 +273,9 @@
             tail_kernel,
             [PACKED] * 8,
             [core, q],
-            dot(gram_kept, inner, ((1,), (1,))),
-            dot(gram_given, inner, ((1,), (1,))),
+            dot(inner, gram_kept, ((1,), (1,))),
+            dot(inner, gram_given, ((1,), (1,))),
+            scratch=[(half, DEPTH)] * 2,
         )
         sums = []
         for blocks in (packed[:4], packed[4:]):

time: 249 us -> 247 us (level)
  matrix products: 17.1 us -> 9.26 us
  Pallas kernels: 4.3 us -> 8.46 us
    dot_general x6 -> x4, matrix products: 17.1 us -> 9.26 us  [dot(): lax.dot_general(left, right, (dims, ((), ())), precision=PREC, preferred_...]
    pallas_call x5 -> x7, Pallas kernels: 4.3 us -> 8.46 us  [local(): pl.pallas_call(kernel, out_shape=[jax.ShapeDtypeStruct(shape, jnp.float32...]
  transfers between devices with their start and end apart: 16 -> 16, of which waited for: 10 -> 10; matrix products, arithmetic and copies ran while one was open for 2% -> 1% of each run, Pallas kernels for 0% -> 1%
where the time goes in v7:
time: 247 us; the launch traced here: 246 us
  blocking collectives  81 us (33%)
  starting transfers between devices  74.7 us (30%)
  waiting for transfers between devices  69.5 us (28%)
  matrix products  9.26 us (4%)
  Pallas kernels  8.46 us (3%)
    ppermute x13, starting transfers between devices, permute(): return lax.ppermute(value, AXES, pairs)  60.6 us
    ppermute x13, waiting for transfers between devices, permute(): return lax.ppermute(value, AXES, pairs)  34.4 us
    all_to_all x1, blocking collectives, body(): parts = lax.all_to_all(parts, 'col', 0, 0, axis_index_groups=Y_GROUPS)  23.2 us
    all_gather x1, blocking collectives, body(): from_b = lax.all_gather(block, 'row', axis=0, axis_index_groups=B_GROUPS)  21.5 us
    all_gather x1, blocking collectives, body(): pieces = lax.all_gather(piece, AXES, axis=0, axis_index_groups=A_GROUPS)  20.9 us
    all_to_all x1, waiting for transfers between devices, body(): lax.all_to_all(total.reshape(4, chunk, size), 'col', 0, 0, axis_index_gro...  19.9 us
    all_gather x1, blocking collectives, body(): lax.all_gather(inner, 'row', axis=0, tiled=True, axis_index_groups=X_GROUPS)  15.3 us
    all_to_all x1, waiting for transfers between devices, body(): parts = lax.all_to_all(parts, 'row', 0, 0, axis_index_groups=X_GROUPS)  15.1 us
  transfers between devices with their start and end apart: 16, of which 10 were waited for; matrix products, arithmetic and copies ran while one was open for 1% of the time, Pallas kernels for 1%

profile of v7, /device:TPU:8, one launch (start us, length us, event | category | flops | bytes accessed | tf_op | source)
XLA Modules:
  0.0 246.0 jit_solution(3322369494555434354)
XLA Ops:
  1.1 9.1 %collective-permute-start = (f32[256,128]{1,0:T(8,128)S(1)}, f32[256,128]{1,0:T(8,128)S(1)}, u32[]{:S(2)}, u32[]{:S(2)}) collective-permute-start(f32[256,128]{1,0:T(8,128)S(1)} %get-tuple-element.22), channel_id=1, source_target_pairs={{0,256},{1,257},{64,320},{65,321},{128,384},{129,385},{192,448},{1... | collective-permute-start | bytes 393224 | tf_op jit(solution)/shard_map/swap_columns/ppermute | solution.py:39
  10.2 11.9 %collective-permute-done.other = f32[256,128]{1,0:T(8,128)S(1)} collective-permute-done((f32[256,128]{1,0:T(8,128)S(1)}, f32[256,128]{1,0:T(8,128)S(1)}, u32[]{:S(2)}, u32[]{:S(2)}) %collective-permute-start) | collective-permute-done | bytes 131104 | tf_op jit(solution)/shard_map/swap_columns/ppermute | solution.py:39
  23.5 4.3 %all-to-all-start = ((f32[4,72,896]{2,1,0:T(8,128)}), f32[4,72,896]{2,1,0:T(8,128)S(1)}, u32[]{:S(2)}, u32[]{:S(2)}) async-start(f32[4,72,896]{2,1,0:T(8,128)} %get-tuple-element.23), calls=%async_computation | async-start | bytes 2064384 | tf_op jit(solution)/shard_map/faces/all_to_all | solution.py:228
  27.9 21.5 %all-gather = f32[288,896]{1,0:T(8,128)S(1)} all-gather(f32[72,896]{1,0:T(8,128)S(1)} %get-tuple-element.24), channel_id=2, replica_groups={{0,64,128,192},{16,80,144,208},{32,96,160,224},{48,112,176,240},{256,32..., dimensions={0}, use_global_device_ids=true | all-gather | bytes 1290240 | tf_op jit(solution)/shard_map/faces/all_gather | solution.py:229
  59.1 4.9 %all-to-all-start.1 = ((f32[4,112,896]{2,1,0:T(8,128)}), f32[4,112,896]{2,1,0:T(8,128)S(1)}, u32[]{:S(2)}, u32[]{:S(2)}) async-start(f32[4,112,896]{2,1,0:T(8,128)} %bitcast.43), calls=%async_computation.1 | async-start | bytes 3211264 | tf_op jit(solution)/shard_map/reduce_y/all_to_all | solution.py:244
  64.0 19.9 %all-to-all-done.1 = f32[4,112,896]{2,1,0:T(8,128)S(1)} async-done(((f32[4,112,896]{2,1,0:T(8,128)}), f32[4,112,896]{2,1,0:T(8,128)S(1)}, u32[]{:S(2)}, u32[]{:S(2)}) %all-to-all-start.1) | async-done | bytes 1605664 | tf_op jit(solution)/shard_map/reduce_y/all_to_all | solution.py:244
  84.1 13.2 %collective-permute-start.2 = (f32[25,8,128]{2,1,0:T(8,128)S(1)}, f32[25,8,128]{2,1,0:T(8,128)S(1)}, u32[]{:S(2)}, u32[]{:S(2)}) collective-permute-start(f32[25,8,128]{2,1,0:T(8,128)S(1)} %get-tuple-element.37), channel_id=1, source_target_pairs={{0,2},{1,3},{64,66},{65,67},{128,130},{129,131},{192,194},{193,195... | collective-permute-start | bytes 307208 | tf_op jit(solution)/shard_map/reduce_a/ppermute | solution.py:39
  97.4 4.7 %collective-permute-start.3 = (f32[25,8,128]{2,1,0:T(8,128)S(1)}, f32[25,8,128]{2,1,0:T(8,128)S(1)}, u32[]{:S(2)}, u32[]{:S(2)}) collective-permute-start(f32[25,8,128]{2,1,0:T(8,128)S(1)} %get-tuple-element.39), channel_id=1, source_target_pairs={{0,256},{1,257},{64,320},{65,321},{128,384},{129,385},{192,448},{1... | collective-permute-start | bytes 307208 | tf_op jit(solution)/shard_map/reduce_a/ppermute | solution.py:39
  102.1 5.0 %collective-permute-start.4 = (f32[25,8,128]{2,1,0:T(8,128)S(1)}, f32[25,8,128]{2,1,0:T(8,128)S(1)}, u32[]{:S(2)}, u32[]{:S(2)}) collective-permute-start(f32[25,8,128]{2,1,0:T(8,128)S(1)} %get-tuple-element.38), channel_id=1, source_target_pairs={{0,258},{1,259},{64,322},{65,323},{128,386},{129,387},{192,450},{1... | collective-permute-start | bytes 307208 | tf_op jit(solution)/shard_map/reduce_a/ppermute | solution.py:39
  107.1 5.5 %collective-permute-done.3 = f32[25,8,128]{2,1,0:T(8,128)S(1)} collective-permute-done((f32[25,8,128]{2,1,0:T(8,128)S(1)}, f32[25,8,128]{2,1,0:T(8,128)S(1)}, u32[]{:S(2)}, u32[]{:S(2)}) %collective-permute-start.3) | collective-permute-done | bytes 102432 | tf_op jit(solution)/shard_map/reduce_a/ppermute | solution.py:39
  112.7 3.0 %collective-permute-done.4 = f32[25,8,128]{2,1,0:T(8,128)S(1)} collective-permute-done((f32[25,8,128]{2,1,0:T(8,128)S(1)}, f32[25,8,128]{2,1,0:T(8,128)S(1)}, u32[]{:S(2)}, u32[]{:S(2)}) %collective-permute-start.4) | collective-permute-done | bytes 102432 | tf_op jit(solution)/shard_map/reduce_a/ppermute | solution.py:39
  115.7 20.9 %all-gather.1 = f32[100,8,128]{2,1,0:T(8,128)S(1)} all-gather(f32[25,8,128]{2,1,0:T(8,128)S(1)} %fusion.1), channel_id=3, replica_groups={{0,256,2,258},{1,257,3,259},{64,320,66,322},{65,321,67,323},{128,384,13..., dimensions={0}, use_global_device_ids=true | all-gather | bytes 512000 | tf_op jit(solution)/shard_map/gather_a/all_gather | solution.py:255
  136.8 23.2 %all_to_all.20 = f32[4,112,896]{2,1,0:T(8,128)S(1)} all-to-all(f32[4,112,896]{2,1,0:T(8,128)S(1)} %broadcast_in_dim.3), channel_id=1, replica_groups={{0,4,8,12},{1,5,9,13},{2,6,10,14},{3,7,11,15},{16,20,24,28},{17,21,25,2..., dimensions={0} | all-to-all | bytes 3211264 | tf_op jit(solution)/shard_map/gather_y/all_to_all | solution.py:259
  165.3 3.1 %convolution_add_fusion = f32[288,896]{1,0:T(8,128)} fusion(f32[288,896]{1,0:T(8,128)S(1)} %fusion.2, f32[288,448]{1,0:T(8,128)S(1)} %get-tuple-element.28.left, f32[448,896]{1,0:T(8,128)S(1)} %collective-permute-done.5), kind=kOutput, calls=%fused_computation | convolution fusion | flops 1387524096 | bytes 4186112 | tf_op jit(solution)/shard_map/first_product/dot_general | solution.py:55
  168.4 4.9 %all-to-all-start.3 = ((f32[4,72,896]{2,1,0:T(8,128)}), f32[4,72,896]{2,1,0:T(8,128)S(1)}, u32[]{:S(2)}, u32[]{:S(2)}) async-start(f32[4,72,896]{2,1,0:T(8,128)} %bitcast.44), calls=%async_computation.3 | async-start | bytes 2064384 | tf_op jit(solution)/shard_map/first_product/all_to_all | solution.py:268
  173.4 15.1 %all-to-all-done.3 = f32[4,72,896]{2,1,0:T(8,128)S(1)} async-done(((f32[4,72,896]{2,1,0:T(8,128)}), f32[4,72,896]{2,1,0:T(8,128)S(1)}, u32[]{:S(2)}, u32[]{:S(2)}) %all-to-all-start.3) | async-done | bytes 1032224 | tf_op jit(solution)/shard_map/first_product/all_to_all | solution.py:268
  188.6 15.3 %all_gather.19 = f32[288,896]{1,0:T(8,128)S(1)} all-gather(f32[72,896]{1,0:T(8,128)S(1)} %multiply_add_fusion), channel_id=1, replica_groups={{0,16,32,48},{64,80,96,112},{128,144,160,176},{192,208,224,240},{256,27..., dimensions={0}, use_global_device_ids=true | all-gather | bytes 1290240 | tf_op jit(solution)/shard_map/first_product/all_gather | solution.py:270
  211.2 5.5 %collective-permute-start.11 = (f32[256,128]{1,0:T(8,128)S(1)}, f32[256,128]{1,0:T(8,128)S(1)}, u32[]{:S(2)}, u32[]{:S(2)}) collective-permute-start(f32[256,128]{1,0:T(8,128)S(1)} %get-tuple-element.36), channel_id=1, source_target_pairs={{0,192},{1,193},{64,0},{65,1},{128,64},{129,65},{192,128},{193,129... | collective-permute-start | bytes 393224 | tf_op jit(solution)/shard_map/second_product/ppermute | solution.py:39
  216.8 2.5 %collective-permute-start.9 = (f32[256,128]{1,0:T(8,128)S(1)}, f32[256,128]{1,0:T(8,128)S(1)}, u32[]{:S(2)}, u32[]{:S(2)}) collective-permute-start(f32[256,128]{1,0:T(8,128)S(1)} %get-tuple-element.34), channel_id=1, source_target_pairs={{0,64},{1,65},{64,128},{65,129},{128,192},{129,193},{192,0},{193,1... | collective-permute-start | bytes 393224 | tf_op jit(solution)/shard_map/second_product/ppermute | solution.py:39
  219.2 3.9 %collective-permute-start.6 = (f32[256,128]{1,0:T(8,128)S(1)}, f32[256,128]{1,0:T(8,128)S(1)}, u32[]{:S(2)}, u32[]{:S(2)}) collective-permute-start(f32[256,128]{1,0:T(8,128)S(1)} %get-tuple-element.30), channel_id=1, source_target_pairs={{0,64},{1,65},{64,128},{65,129},{128,192},{129,193},{192,0},{193,1... | collective-permute-start | bytes 393224 | tf_op jit(solution)/shard_map/second_product/ppermute | solution.py:39
  223.2 3.7 %collective-permute-start.7 = (f32[256,128]{1,0:T(8,128)S(1)}, f32[256,128]{1,0:T(8,128)S(1)}, u32[]{:S(2)}, u32[]{:S(2)}) collective-permute-start(f32[256,128]{1,0:T(8,128)S(1)} %get-tuple-element.31), channel_id=1, source_target_pairs={{0,128},{1,129},{64,192},{65,193},{128,0},{129,1},{192,64},{193,65... | collective-permute-start | bytes 393224 | tf_op jit(solution)/shard_map/second_product/ppermute | solution.py:39
  226.9 2.5 %collective-permute-start.8 = (f32[256,128]{1,0:T(8,128)S(1)}, f32[256,128]{1,0:T(8,128)S(1)}, u32[]{:S(2)}, u32[]{:S(2)}) collective-permute-start(f32[256,128]{1,0:T(8,128)S(1)} %get-tuple-element.32), channel_id=1, source_target_pairs={{0,192},{1,193},{64,0},{65,1},{128,64},{129,65},{192,128},{193,129... | collective-permute-start | bytes 393224 | tf_op jit(solution)/shard_map/second_product/ppermute | solution.py:39
  229.5 4.6 %collective-permute-start.12 = (f32[256,128]{1,0:T(8,128)S(1)}, f32[256,128]{1,0:T(8,128)S(1)}, u32[]{:S(2)}, u32[]{:S(2)}) collective-permute-start(f32[256,128]{1,0:T(8,128)S(1)} %add_add_fusion), channel_id=1, source_target_pairs={{0,256},{1,257},{64,320},{65,321},{128,384},{129,385},{192,448},{1... | collective-permute-start | bytes 393224 | tf_op jit(solution)/shard_map/swap_back/ppermute | solution.py:39
  235.9 9.3 %collective-permute-done.12.other = f32[256,128]{1,0:T(8,128)S(1)} collective-permute-done((f32[256,128]{1,0:T(8,128)S(1)}, f32[256,128]{1,0:T(8,128)S(1)}, u32[]{:S(2)}, u32[]{:S(2)}) %collective-permute-start.12) | collective-permute-done | bytes 131104 | tf_op jit(solution)/shard_map/swap_back/ppermute | solution.py:39
  (44 shorter events, 28.0 us)
Async XLA Ops:
  0.0 1.0 copy-start
  1.1 21.0 %collective-permute-start = (f32[256,128]{1,0:T(8,128)S(1)}, f32[256,128]{1,0:T(8,128)S(1)}, u32[]{:S(2)}, u32[]{:S(2)}) collective-permute-start(f32[256,128]{1,0:T(8,128)S(1)} %get-tuple-element.22), channel_id=1, source_target_pairs={{0,256},{1,257},{64,320},{65,321},{128,384},{129,385},{192,448},{1... | collective-permute-start | bytes 393224 | tf_op jit(solution)/shard_map/swap_columns/ppermute | solution.py:39
  23.5 25.9 %all-to-all-start = ((f32[4,72,896]{2,1,0:T(8,128)}), f32[4,72,896]{2,1,0:T(8,128)S(1)}, u32[]{:S(2)}, u32[]{:S(2)}) async-start(f32[4,72,896]{2,1,0:T(8,128)} %get-tuple-element.23), calls=%async_computation | async-start | bytes 2064384 | tf_op jit(solution)/shard_map/faces/all_to_all | solution.py:228
  52.4 5.4 %collective-permute-start.1 = (f32[448,896]{1,0:T(8,128)S(1)}, f32[448,896]{1,0:T(8,128)S(1)}, u32[]{:S(2)}, u32[]{:S(2)}) collective-permute-start(f32[448,896]{1,0:T(8,128)S(1)} %gram.3), channel_id=1, source_target_pairs={{0,1},{1,0},{64,65},{65,64},{128,129},{129,128},{192,193},{193,192... | collective-permute-start | bytes 4816904 | tf_op jit(solution)/shard_map/gram/ppermute | solution.py:39
  59.1 24.8 %all-to-all-start.1 = ((f32[4,112,896]{2,1,0:T(8,128)}), f32[4,112,896]{2,1,0:T(8,128)S(1)}, u32[]{:S(2)}, u32[]{:S(2)}) async-start(f32[4,112,896]{2,1,0:T(8,128)} %bitcast.43), calls=%async_computation.1 | async-start | bytes 3211264 | tf_op jit(solution)/shard_map/reduce_y/all_to_all | solution.py:244
  84.1 23.0 %collective-permute-start.2 = (f32[25,8,128]{2,1,0:T(8,128)S(1)}, f32[25,8,128]{2,1,0:T(8,128)S(1)}, u32[]{:S(2)}, u32[]{:S(2)}) collective-permute-start(f32[25,8,128]{2,1,0:T(8,128)S(1)} %get-tuple-element.37), channel_id=1, source_target_pairs={{0,2},{1,3},{64,66},{65,67},{128,130},{129,131},{192,194},{193,195... | collective-permute-start | bytes 307208 | tf_op jit(solution)/shard_map/reduce_a/ppermute | solution.py:39
  97.4 15.3 %collective-permute-start.3 = (f32[25,8,128]{2,1,0:T(8,128)S(1)}, f32[25,8,128]{2,1,0:T(8,128)S(1)}, u32[]{:S(2)}, u32[]{:S(2)}) collective-permute-start(f32[25,8,128]{2,1,0:T(8,128)S(1)} %get-tuple-element.39), channel_id=1, source_target_pairs={{0,256},{1,257},{64,320},{65,321},{128,384},{129,385},{192,448},{1... | collective-permute-start | bytes 307208 | tf_op jit(solution)/shard_map/reduce_a/ppermute | solution.py:39
  102.1 13.6 %collective-permute-start.4 = (f32[25,8,128]{2,1,0:T(8,128)S(1)}, f32[25,8,128]{2,1,0:T(8,128)S(1)}, u32[]{:S(2)}, u32[]{:S(2)}) collective-permute-start(f32[25,8,128]{2,1,0:T(8,128)S(1)} %get-tuple-element.38), channel_id=1, source_target_pairs={{0,258},{1,259},{64,322},{65,323},{128,386},{129,387},{192,450},{1... | collective-permute-start | bytes 307208 | tf_op jit(solution)/shard_map/reduce_a/ppermute | solution.py:39
  160.0 5.3 %collective-permute-start.5 = (f32[448,896]{1,0:T(8,128)S(1)}, f32[448,896]{1,0:T(8,128)S(1)}, u32[]{:S(2)}, u32[]{:S(2)}) collective-permute-start(f32[448,896]{1,0:T(8,128)S(1)} %bitcast.40), channel_id=1, source_target_pairs={{0,1},{1,0},{64,65},{65,64},{128,129},{129,128},{192,193},{193,192... | collective-permute-start | bytes 4816904 | tf_op jit(solution)/shard_map/gather_core/ppermute | solution.py:39
  165.3 3.1 %copy-start.2 = (f32[448,896]{1,0:T(8,128)}, f32[448,896]{1,0:T(8,128)S(1)}, u32[]{:S(2)}) copy-start(f32[448,896]{1,0:T(8,128)S(1)} %collective-permute-done.5) | copy-start | bytes 4816900
  168.4 20.1 %all-to-all-start.3 = ((f32[4,72,896]{2,1,0:T(8,128)}), f32[4,72,896]{2,1,0:T(8,128)S(1)}, u32[]{:S(2)}, u32[]{:S(2)}) async-start(f32[4,72,896]{2,1,0:T(8,128)} %bitcast.44), calls=%async_computation.3 | async-start | bytes 2064384 | tf_op jit(solution)/shard_map/first_product/all_to_all | solution.py:268
  204.0 2.1 copy-start.3
  208.1 37.1 %copy-start.1 = (f32[112,576]{1,0:T(8,128)S(1)}, f32[112,576]{1,0:T(8,128)}, u32[]{:S(2)}) copy-start(f32[112,576]{1,0:T(8,128)} %iterate.3) | copy-start | bytes 774148
  209.3 17.6 %collective-permute-start.10 = (f32[256,128]{1,0:T(8,128)S(1)}, f32[256,128]{1,0:T(8,128)S(1)}, u32[]{:S(2)}, u32[]{:S(2)}) collective-permute-start(f32[256,128]{1,0:T(8,128)S(1)} %get-tuple-element.35), channel_id=1, source_target_pairs={{0,128},{1,129},{64,192},{65,193},{128,0},{129,1},{192,64},{193,65... | collective-permute-start | bytes 393224 | tf_op jit(solution)/shard_map/second_product/ppermute | solution.py:39
  211.2 18.2 %collective-permute-start.11 = (f32[256,128]{1,0:T(8,128)S(1)}, f32[256,128]{1,0:T(8,128)S(1)}, u32[]{:S(2)}, u32[]{:S(2)}) collective-permute-start(f32[256,128]{1,0:T(8,128)S(1)} %get-tuple-element.36), channel_id=1, source_target_pairs={{0,192},{1,193},{64,0},{65,1},{128,64},{129,65},{192,128},{193,129... | collective-permute-start | bytes 393224 | tf_op jit(solution)/shard_map/second_product/ppermute | solution.py:39
  216.8 12.6 %collective-permute-start.9 = (f32[256,128]{1,0:T(8,128)S(1)}, f32[256,128]{1,0:T(8,128)S(1)}, u32[]{:S(2)}, u32[]{:S(2)}) collective-permute-start(f32[256,128]{1,0:T(8,128)S(1)} %get-tuple-element.34), channel_id=1, source_target_pairs={{0,64},{1,65},{64,128},{65,129},{128,192},{129,193},{192,0},{193,1... | collective-permute-start | bytes 393224 | tf_op jit(solution)/shard_map/second_product/ppermute | solution.py:39
  219.2 14.8 %collective-permute-start.6 = (f32[256,128]{1,0:T(8,128)S(1)}, f32[256,128]{1,0:T(8,128)S(1)}, u32[]{:S(2)}, u32[]{:S(2)}) collective-permute-start(f32[256,128]{1,0:T(8,128)S(1)} %get-tuple-element.30), channel_id=1, source_target_pairs={{0,64},{1,65},{64,128},{65,129},{128,192},{129,193},{192,0},{193,1... | collective-permute-start | bytes 393224 | tf_op jit(solution)/shard_map/second_product/ppermute | solution.py:39
  223.2 11.6 %collective-permute-start.7 = (f32[256,128]{1,0:T(8,128)S(1)}, f32[256,128]{1,0:T(8,128)S(1)}, u32[]{:S(2)}, u32[]{:S(2)}) collective-permute-start(f32[256,128]{1,0:T(8,128)S(1)} %get-tuple-element.31), channel_id=1, source_target_pairs={{0,128},{1,129},{64,192},{65,193},{128,0},{129,1},{192,64},{193,65... | collective-permute-start | bytes 393224 | tf_op jit(solution)/shard_map/second_product/ppermute | solution.py:39
  226.9 8.9 %collective-permute-start.8 = (f32[256,128]{1,0:T(8,128)S(1)}, f32[256,128]{1,0:T(8,128)S(1)}, u32[]{:S(2)}, u32[]{:S(2)}) collective-permute-start(f32[256,128]{1,0:T(8,128)S(1)} %get-tuple-element.32), channel_id=1, source_target_pairs={{0,192},{1,193},{64,0},{65,1},{128,64},{129,65},{192,128},{193,129... | collective-permute-start | bytes 393224 | tf_op jit(solution)/shard_map/second_product/ppermute | solution.py:39
  229.5 15.7 %collective-permute-start.12 = (f32[256,128]{1,0:T(8,128)S(1)}, f32[256,128]{1,0:T(8,128)S(1)}, u32[]{:S(2)}, u32[]{:S(2)}) collective-permute-start(f32[256,128]{1,0:T(8,128)S(1)} %add_add_fusion), channel_id=1, source_target_pairs={{0,256},{1,257},{64,320},{65,321},{128,384},{129,385},{192,448},{1... | collective-permute-start | bytes 393224 | tf_op jit(solution)/shard_map/swap_back/ppermute | solution.py:39

commit v8 on v7

--- a/solution.py
+++ b/solution.py
@@ -101,24 +101,32 @@
             own[...] = iterate[:, DEPTH * q : DEPTH * (q + 1)]
 
 
+def place(block, wide, q):
+    part = DEPTH // 4
+    flipped = wide[...].T
+    for k in range(4):
+        at = k * 2 * ROWS + q * ROWS
+        block[:, at : at + ROWS] = flipped[k * part : (k + 1) * part, 0:ROWS]
+
+
+def own_kernel(index, own, block, wide):
+    wide[0:ROWS, 0:DEPTH] = own[...]
+    block[...] = jnp.zeros(block.shape, jnp.float32)
+    for q in range(2):
+
+        @pl.when(index[0] == q)
+        def _():
+            place(block, wide, q)
+
+
 def block_kernel(index, own, other, block, blocks, wide):
-    part = DEPTH // 4
-
-    def place(q):
-        flipped = wide[...].T
-        for k in range(4):
-            at = k * 2 * ROWS + q * ROWS
-            value = flipped[k * part : (k + 1) * part, 0:ROWS]
-            block[:, at : at + ROWS] = value
-
+    block[...] = own[...]
+    unpack(wide, other, 0)
     for q in range(2):
 
         @pl.when(index[0] == q)
         def _():
-            wide[0:ROWS, 0:DEPTH] = own[...]
-            place(q)
-            unpack(wide, other, 0)
-            place(1 - q)
+            place(block, wide, 1 - q)
 
     for n in range(4):
         blocks[n, :, :] = block[...]
@@ -221,6 +229,7 @@
     with jax.named_scope("swap_columns"):
         sent, own = local(send_kernel, [PACKED, (ROWS, DEPTH)], [q], iterate)
         other = swap_q(sent)
+        (own,) = local(own_kernel, [(part, size)], [q], own, scratch=[(128, 384)])
     with jax.named_scope("faces"):
         block, blocks = local(
             block_kernel, [(part, size), (4, part, size)], [q], own, other, scratch=[(128, 384)]
@@ -248,7 +257,7 @@
     with jax.named_scope("reduce_a"):
         pieces = tiles(near)
         piece = lax.dynamic_index_in_dim(pieces, a, 0, False)
-        for step in (2, 1, 3):
+        for step in (2, 3, 1):
             sent = lax.dynamic_index_in_dim(pieces, (a + step) % 4, 0, False)
             piece = piece + permute(sent, lambda x, y, z, c: (x, y, (z + 4 * step) % 16, c))
     with jax.named_scope("gather_a"):

time: 247 us -> 247 us (level)
    all_to_all x1, starting transfers between devices: 4.89 us -> 7.65 us  [body(): parts = lax.all_to_all(parts, 'row', 0, 0, axis_index_groups=X_GROUPS)]
    pallas_call x7 -> x8, Pallas kernels: 8.46 us -> 8.57 us  [local(): pl.pallas_call(kernel, out_shape=[jax.ShapeDtypeStruct(shape, jnp.float32...]
  transfers between devices with their start and end apart: 16 -> 16, of which waited for: 10 -> 7; matrix products, arithmetic and copies ran while one was open for 1% -> 1% of each run, Pallas kernels for 1% -> 1%
where the time goes in v8:
time: 247 us; the launch traced here: 246 us
  blocking collectives  81 us (33%)
  starting transfers between devices  76.6 us (31%)
  waiting for transfers between devices  67.6 us (27%)
  matrix products  9.26 us (4%)
  Pallas kernels  8.57 us (3%)
    ppermute x13, starting transfers between devices, permute(): return lax.ppermute(value, AXES, pairs)  59.7 us
    ppermute x13, waiting for transfers between devices, permute(): return lax.ppermute(value, AXES, pairs)  32.6 us
    all_gather x1, blocking collectives, body(): pieces = lax.all_gather(piece, AXES, axis=0, axis_index_groups=A_GROUPS)  23.3 us
    all_gather x1, blocking collectives, body(): from_b = lax.all_gather(block, 'row', axis=0, axis_index_groups=B_GROUPS)  21.5 us
    all_to_all x1, blocking collectives, body(): parts = lax.all_to_all(parts, 'col', 0, 0, axis_index_groups=Y_GROUPS)  21 us
    all_to_all x1, waiting for transfers between devices, body(): lax.all_to_all(total.reshape(4, chunk, size), 'col', 0, 0, axis_index_gro...  19.9 us
    all_gather x1, blocking collectives, body(): lax.all_gather(inner, 'row', axis=0, tiled=True, axis_index_groups=X_GROUPS)  15.3 us
    all_to_all x1, waiting for transfers between devices, body(): parts = lax.all_to_all(parts, 'row', 0, 0, axis_index_groups=X_GROUPS)  15.1 us
  transfers between devices with their start and end apart: 16, of which 7 were waited for; matrix products, arithmetic and copies ran while one was open for 1% of the time, Pallas kernels for 1%

profile of v8, /device:TPU:8, one launch (start us, length us, event | category | flops | bytes accessed | tf_op | source)
XLA Modules:
  0.0 246.3 jit_solution(7541132732743084392)
XLA Ops:
  1.1 9.1 %collective-permute-start = (f32[256,128]{1,0:T(8,128)S(1)}, f32[256,128]{1,0:T(8,128)S(1)}, u32[]{:S(2)}, u32[]{:S(2)}) collective-permute-start(f32[256,128]{1,0:T(8,128)S(1)} %get-tuple-element.22), channel_id=1, source_target_pairs={{0,256},{1,257},{64,320},{65,321},{128,384},{129,385},{192,448},{1... | collective-permute-start | bytes 393224 | tf_op jit(solution)/shard_map/swap_columns/ppermute | solution.py:39
  10.4 11.7 %collective-permute-done.other = f32[256,128]{1,0:T(8,128)S(1)} collective-permute-done((f32[256,128]{1,0:T(8,128)S(1)}, f32[256,128]{1,0:T(8,128)S(1)}, u32[]{:S(2)}, u32[]{:S(2)}) %collective-permute-start) | collective-permute-done | bytes 131104 | tf_op jit(solution)/shard_map/swap_columns/ppermute | solution.py:39
  23.4 4.3 %all-to-all-start = ((f32[4,72,896]{2,1,0:T(8,128)}), f32[4,72,896]{2,1,0:T(8,128)S(1)}, u32[]{:S(2)}, u32[]{:S(2)}) async-start(f32[4,72,896]{2,1,0:T(8,128)} %get-tuple-element.23), calls=%async_computation | async-start | bytes 2064384 | tf_op jit(solution)/shard_map/faces/all_to_all | solution.py:237
  27.7 21.5 %all-gather = f32[288,896]{1,0:T(8,128)S(1)} all-gather(f32[72,896]{1,0:T(8,128)S(1)} %get-tuple-element.24), channel_id=2, replica_groups={{0,64,128,192},{16,80,144,208},{32,96,160,224},{48,112,176,240},{256,32..., dimensions={0}, use_global_device_ids=true | all-gather | bytes 1290240 | tf_op jit(solution)/shard_map/faces/all_gather | solution.py:238
  59.0 4.9 %all-to-all-start.1 = ((f32[4,112,896]{2,1,0:T(8,128)}), f32[4,112,896]{2,1,0:T(8,128)S(1)}, u32[]{:S(2)}, u32[]{:S(2)}) async-start(f32[4,112,896]{2,1,0:T(8,128)} %bitcast.43), calls=%async_computation.1 | async-start | bytes 3211264 | tf_op jit(solution)/shard_map/reduce_y/all_to_all | solution.py:253
  63.9 19.9 %all-to-all-done.1 = f32[4,112,896]{2,1,0:T(8,128)S(1)} async-done(((f32[4,112,896]{2,1,0:T(8,128)}), f32[4,112,896]{2,1,0:T(8,128)S(1)}, u32[]{:S(2)}, u32[]{:S(2)}) %all-to-all-start.1) | async-done | bytes 1605664 | tf_op jit(solution)/shard_map/reduce_y/all_to_all | solution.py:253
  84.0 13.2 %collective-permute-start.2 = (f32[25,8,128]{2,1,0:T(8,128)S(1)}, f32[25,8,128]{2,1,0:T(8,128)S(1)}, u32[]{:S(2)}, u32[]{:S(2)}) collective-permute-start(f32[25,8,128]{2,1,0:T(8,128)S(1)} %get-tuple-element.37), channel_id=1, source_target_pairs={{0,2},{1,3},{64,66},{65,67},{128,130},{129,131},{192,194},{193,195... | collective-permute-start | bytes 307208 | tf_op jit(solution)/shard_map/reduce_a/ppermute | solution.py:39
  97.2 2.4 collective-permute-start.3
  99.6 7.3 %collective-permute-start.4 = (f32[25,8,128]{2,1,0:T(8,128)S(1)}, f32[25,8,128]{2,1,0:T(8,128)S(1)}, u32[]{:S(2)}, u32[]{:S(2)}) collective-permute-start(f32[25,8,128]{2,1,0:T(8,128)S(1)} %get-tuple-element.38), channel_id=1, source_target_pairs={{0,256},{1,257},{64,320},{65,321},{128,384},{129,385},{192,448},{1... | collective-permute-start | bytes 307208 | tf_op jit(solution)/shard_map/reduce_a/ppermute | solution.py:39
  107.0 7.6 %collective-permute-done.3 = f32[25,8,128]{2,1,0:T(8,128)S(1)} collective-permute-done((f32[25,8,128]{2,1,0:T(8,128)S(1)}, f32[25,8,128]{2,1,0:T(8,128)S(1)}, u32[]{:S(2)}, u32[]{:S(2)}) %collective-permute-start.3) | collective-permute-done | bytes 102432 | tf_op jit(solution)/shard_map/reduce_a/ppermute | solution.py:39
  114.7 23.3 %all-gather.1 = f32[100,8,128]{2,1,0:T(8,128)S(1)} all-gather(f32[25,8,128]{2,1,0:T(8,128)S(1)} %fusion.1), channel_id=3, replica_groups={{0,256,2,258},{1,257,3,259},{64,320,66,322},{65,321,67,323},{128,384,13..., dimensions={0}, use_global_device_ids=true | all-gather | bytes 512000 | tf_op jit(solution)/shard_map/gather_a/all_gather | solution.py:264
  138.1 21.0 %all_to_all.20 = f32[4,112,896]{2,1,0:T(8,128)S(1)} all-to-all(f32[4,112,896]{2,1,0:T(8,128)S(1)} %broadcast_in_dim.3), channel_id=1, replica_groups={{0,4,8,12},{1,5,9,13},{2,6,10,14},{3,7,11,15},{16,20,24,28},{17,21,25,2..., dimensions={0} | all-to-all | bytes 3211264 | tf_op jit(solution)/shard_map/gather_y/all_to_all | solution.py:268
  161.0 2.1 fusion.2
  164.4 3.1 %convolution_add_fusion = f32[288,896]{1,0:T(8,128)} fusion(f32[288,896]{1,0:T(8,128)S(1)} %fusion.2, f32[288,448]{1,0:T(8,128)S(1)} %get-tuple-element.28.left, f32[448,896]{1,0:T(8,128)S(1)} %collective-permute-done.5), kind=kOutput, calls=%fused_computation | convolution fusion | flops 1387524096 | bytes 4186112 | tf_op jit(solution)/shard_map/first_product/dot_general | solution.py:55
  167.5 7.7 %all-to-all-start.3 = ((f32[4,72,896]{2,1,0:T(8,128)}), f32[4,72,896]{2,1,0:T(8,128)S(1)}, u32[]{:S(2)}, u32[]{:S(2)}) async-start(f32[4,72,896]{2,1,0:T(8,128)} %bitcast.44), calls=%async_computation.3 | async-start | bytes 2064384 | tf_op jit(solution)/shard_map/first_product/all_to_all | solution.py:277
  175.2 15.1 %all-to-all-done.3 = f32[4,72,896]{2,1,0:T(8,128)S(1)} async-done(((f32[4,72,896]{2,1,0:T(8,128)}), f32[4,72,896]{2,1,0:T(8,128)S(1)}, u32[]{:S(2)}, u32[]{:S(2)}) %all-to-all-start.3) | async-done | bytes 1032224 | tf_op jit(solution)/shard_map/first_product/all_to_all | solution.py:277
  190.4 15.3 %all_gather.19 = f32[288,896]{1,0:T(8,128)S(1)} all-gather(f32[72,896]{1,0:T(8,128)S(1)} %multiply_add_fusion), channel_id=1, replica_groups={{0,16,32,48},{64,80,96,112},{128,144,160,176},{192,208,224,240},{256,27..., dimensions={0}, use_global_device_ids=true | all-gather | bytes 1290240 | tf_op jit(solution)/shard_map/first_product/all_gather | solution.py:279
  213.0 2.7 %collective-permute-start.11 = (f32[256,128]{1,0:T(8,128)S(1)}, f32[256,128]{1,0:T(8,128)S(1)}, u32[]{:S(2)}, u32[]{:S(2)}) collective-permute-start(f32[256,128]{1,0:T(8,128)S(1)} %get-tuple-element.36), channel_id=1, source_target_pairs={{0,192},{1,193},{64,0},{65,1},{128,64},{129,65},{192,128},{193,129... | collective-permute-start | bytes 393224 | tf_op jit(solution)/shard_map/second_product/ppermute | solution.py:39
  215.7 3.2 %collective-permute-start.9 = (f32[256,128]{1,0:T(8,128)S(1)}, f32[256,128]{1,0:T(8,128)S(1)}, u32[]{:S(2)}, u32[]{:S(2)}) collective-permute-start(f32[256,128]{1,0:T(8,128)S(1)} %get-tuple-element.34), channel_id=1, source_target_pairs={{0,64},{1,65},{64,128},{65,129},{128,192},{129,193},{192,0},{193,1... | collective-permute-start | bytes 393224 | tf_op jit(solution)/shard_map/second_product/ppermute | solution.py:39
  218.9 3.4 %collective-permute-start.6 = (f32[256,128]{1,0:T(8,128)S(1)}, f32[256,128]{1,0:T(8,128)S(1)}, u32[]{:S(2)}, u32[]{:S(2)}) collective-permute-start(f32[256,128]{1,0:T(8,128)S(1)} %get-tuple-element.30), channel_id=1, source_target_pairs={{0,64},{1,65},{64,128},{65,129},{128,192},{129,193},{192,0},{193,1... | collective-permute-start | bytes 393224 | tf_op jit(solution)/shard_map/second_product/ppermute | solution.py:39
  222.3 3.6 %collective-permute-start.7 = (f32[256,128]{1,0:T(8,128)S(1)}, f32[256,128]{1,0:T(8,128)S(1)}, u32[]{:S(2)}, u32[]{:S(2)}) collective-permute-start(f32[256,128]{1,0:T(8,128)S(1)} %get-tuple-element.31), channel_id=1, source_target_pairs={{0,128},{1,129},{64,192},{65,193},{128,0},{129,1},{192,64},{193,65... | collective-permute-start | bytes 393224 | tf_op jit(solution)/shard_map/second_product/ppermute | solution.py:39
  225.9 4.6 %collective-permute-start.8 = (f32[256,128]{1,0:T(8,128)S(1)}, f32[256,128]{1,0:T(8,128)S(1)}, u32[]{:S(2)}, u32[]{:S(2)}) collective-permute-start(f32[256,128]{1,0:T(8,128)S(1)} %get-tuple-element.32), channel_id=1, source_target_pairs={{0,192},{1,193},{64,0},{65,1},{128,64},{129,65},{192,128},{193,129... | collective-permute-start | bytes 393224 | tf_op jit(solution)/shard_map/second_product/ppermute | solution.py:39
  230.5 4.5 %collective-permute-start.12 = (f32[256,128]{1,0:T(8,128)S(1)}, f32[256,128]{1,0:T(8,128)S(1)}, u32[]{:S(2)}, u32[]{:S(2)}) collective-permute-start(f32[256,128]{1,0:T(8,128)S(1)} %add_add_fusion), channel_id=1, source_target_pairs={{0,256},{1,257},{64,320},{65,321},{128,384},{129,385},{192,448},{1... | collective-permute-start | bytes 393224 | tf_op jit(solution)/shard_map/swap_back/ppermute | solution.py:39
  235.1 10.4 %collective-permute-done.12.other = f32[256,128]{1,0:T(8,128)S(1)} collective-permute-done((f32[256,128]{1,0:T(8,128)S(1)}, f32[256,128]{1,0:T(8,128)S(1)}, u32[]{:S(2)}, u32[]{:S(2)}) %collective-permute-start.12) | collective-permute-done | bytes 131104 | tf_op jit(solution)/shard_map/swap_back/ppermute | solution.py:39
  (45 shorter events, 24.3 us)
Async XLA Ops:
  0.0 1.0 copy-start
  1.1 21.0 %collective-permute-start = (f32[256,128]{1,0:T(8,128)S(1)}, f32[256,128]{1,0:T(8,128)S(1)}, u32[]{:S(2)}, u32[]{:S(2)}) collective-permute-start(f32[256,128]{1,0:T(8,128)S(1)} %get-tuple-element.22), channel_id=1, source_target_pairs={{0,256},{1,257},{64,320},{65,321},{128,384},{129,385},{192,448},{1... | collective-permute-start | bytes 393224 | tf_op jit(solution)/shard_map/swap_columns/ppermute | solution.py:39
  23.4 25.9 %all-to-all-start = ((f32[4,72,896]{2,1,0:T(8,128)}), f32[4,72,896]{2,1,0:T(8,128)S(1)}, u32[]{:S(2)}, u32[]{:S(2)}) async-start(f32[4,72,896]{2,1,0:T(8,128)} %get-tuple-element.23), calls=%async_computation | async-start | bytes 2064384 | tf_op jit(solution)/shard_map/faces/all_to_all | solution.py:237
  52.3 5.4 %collective-permute-start.1 = (f32[448,896]{1,0:T(8,128)S(1)}, f32[448,896]{1,0:T(8,128)S(1)}, u32[]{:S(2)}, u32[]{:S(2)}) collective-permute-start(f32[448,896]{1,0:T(8,128)S(1)} %gram.3), channel_id=1, source_target_pairs={{0,1},{1,0},{64,65},{65,64},{128,129},{129,128},{192,193},{193,192... | collective-permute-start | bytes 4816904 | tf_op jit(solution)/shard_map/gram/ppermute | solution.py:39
  59.0 24.8 %all-to-all-start.1 = ((f32[4,112,896]{2,1,0:T(8,128)}), f32[4,112,896]{2,1,0:T(8,128)S(1)}, u32[]{:S(2)}, u32[]{:S(2)}) async-start(f32[4,112,896]{2,1,0:T(8,128)} %bitcast.43), calls=%async_computation.1 | async-start | bytes 3211264 | tf_op jit(solution)/shard_map/reduce_y/all_to_all | solution.py:253
  84.0 23.0 %collective-permute-start.2 = (f32[25,8,128]{2,1,0:T(8,128)S(1)}, f32[25,8,128]{2,1,0:T(8,128)S(1)}, u32[]{:S(2)}, u32[]{:S(2)}) collective-permute-start(f32[25,8,128]{2,1,0:T(8,128)S(1)} %get-tuple-element.37), channel_id=1, source_target_pairs={{0,2},{1,3},{64,66},{65,67},{128,130},{129,131},{192,194},{193,195... | collective-permute-start | bytes 307208 | tf_op jit(solution)/shard_map/reduce_a/ppermute | solution.py:39
  97.2 17.4 %collective-permute-start.3 = (f32[25,8,128]{2,1,0:T(8,128)S(1)}, f32[25,8,128]{2,1,0:T(8,128)S(1)}, u32[]{:S(2)}, u32[]{:S(2)}) collective-permute-start(f32[25,8,128]{2,1,0:T(8,128)S(1)} %get-tuple-element.39), channel_id=1, source_target_pairs={{0,258},{1,259},{64,322},{65,323},{128,386},{129,387},{192,450},{1... | collective-permute-start | bytes 307208 | tf_op jit(solution)/shard_map/reduce_a/ppermute | solution.py:39
  99.6 15.0 %collective-permute-start.4 = (f32[25,8,128]{2,1,0:T(8,128)S(1)}, f32[25,8,128]{2,1,0:T(8,128)S(1)}, u32[]{:S(2)}, u32[]{:S(2)}) collective-permute-start(f32[25,8,128]{2,1,0:T(8,128)S(1)} %get-tuple-element.38), channel_id=1, source_target_pairs={{0,256},{1,257},{64,320},{65,321},{128,384},{129,385},{192,448},{1... | collective-permute-start | bytes 307208 | tf_op jit(solution)/shard_map/reduce_a/ppermute | solution.py:39
  159.0 5.3 %collective-permute-start.5 = (f32[448,896]{1,0:T(8,128)S(1)}, f32[448,896]{1,0:T(8,128)S(1)}, u32[]{:S(2)}, u32[]{:S(2)}) collective-permute-start(f32[448,896]{1,0:T(8,128)S(1)} %bitcast.40), channel_id=1, source_target_pairs={{0,1},{1,0},{64,65},{65,64},{128,129},{129,128},{192,193},{193,192... | collective-permute-start | bytes 4816904 | tf_op jit(solution)/shard_map/gather_core/ppermute | solution.py:39
  164.4 3.1 %copy-start.2 = (f32[448,896]{1,0:T(8,128)}, f32[448,896]{1,0:T(8,128)S(1)}, u32[]{:S(2)}) copy-start(f32[448,896]{1,0:T(8,128)S(1)} %collective-permute-done.5) | copy-start | bytes 4816900
  167.5 22.9 %all-to-all-start.3 = ((f32[4,72,896]{2,1,0:T(8,128)}), f32[4,72,896]{2,1,0:T(8,128)S(1)}, u32[]{:S(2)}, u32[]{:S(2)}) async-start(f32[4,72,896]{2,1,0:T(8,128)} %bitcast.44), calls=%async_computation.3 | async-start | bytes 2064384 | tf_op jit(solution)/shard_map/first_product/all_to_all | solution.py:277
  205.8 2.1 copy-start.3
  209.9 35.6 %copy-start.1 = (f32[112,576]{1,0:T(8,128)S(1)}, f32[112,576]{1,0:T(8,128)}, u32[]{:S(2)}) copy-start(f32[112,576]{1,0:T(8,128)} %iterate.3) | copy-start | bytes 774148
  211.1 14.8 %collective-permute-start.10 = (f32[256,128]{1,0:T(8,128)S(1)}, f32[256,128]{1,0:T(8,128)S(1)}, u32[]{:S(2)}, u32[]{:S(2)}) collective-permute-start(f32[256,128]{1,0:T(8,128)S(1)} %get-tuple-element.35), channel_id=1, source_target_pairs={{0,128},{1,129},{64,192},{65,193},{128,0},{129,1},{192,64},{193,65... | collective-permute-start | bytes 393224 | tf_op jit(solution)/shard_map/second_product/ppermute | solution.py:39
  213.0 17.5 %collective-permute-start.11 = (f32[256,128]{1,0:T(8,128)S(1)}, f32[256,128]{1,0:T(8,128)S(1)}, u32[]{:S(2)}, u32[]{:S(2)}) collective-permute-start(f32[256,128]{1,0:T(8,128)S(1)} %get-tuple-element.36), channel_id=1, source_target_pairs={{0,192},{1,193},{64,0},{65,1},{128,64},{129,65},{192,128},{193,129... | collective-permute-start | bytes 393224 | tf_op jit(solution)/shard_map/second_product/ppermute | solution.py:39
  215.7 14.8 %collective-permute-start.9 = (f32[256,128]{1,0:T(8,128)S(1)}, f32[256,128]{1,0:T(8,128)S(1)}, u32[]{:S(2)}, u32[]{:S(2)}) collective-permute-start(f32[256,128]{1,0:T(8,128)S(1)} %get-tuple-element.34), channel_id=1, source_target_pairs={{0,64},{1,65},{64,128},{65,129},{128,192},{129,193},{192,0},{193,1... | collective-permute-start | bytes 393224 | tf_op jit(solution)/shard_map/second_product/ppermute | solution.py:39
  218.9 16.1 %collective-permute-start.6 = (f32[256,128]{1,0:T(8,128)S(1)}, f32[256,128]{1,0:T(8,128)S(1)}, u32[]{:S(2)}, u32[]{:S(2)}) collective-permute-start(f32[256,128]{1,0:T(8,128)S(1)} %get-tuple-element.30), channel_id=1, source_target_pairs={{0,64},{1,65},{64,128},{65,129},{128,192},{129,193},{192,0},{193,1... | collective-permute-start | bytes 393224 | tf_op jit(solution)/shard_map/second_product/ppermute | solution.py:39
  222.3 12.8 %collective-permute-start.7 = (f32[256,128]{1,0:T(8,128)S(1)}, f32[256,128]{1,0:T(8,128)S(1)}, u32[]{:S(2)}, u32[]{:S(2)}) collective-permute-start(f32[256,128]{1,0:T(8,128)S(1)} %get-tuple-element.31), channel_id=1, source_target_pairs={{0,128},{1,129},{64,192},{65,193},{128,0},{129,1},{192,64},{193,65... | collective-permute-start | bytes 393224 | tf_op jit(solution)/shard_map/second_product/ppermute | solution.py:39
  225.9 9.2 %collective-permute-start.8 = (f32[256,128]{1,0:T(8,128)S(1)}, f32[256,128]{1,0:T(8,128)S(1)}, u32[]{:S(2)}, u32[]{:S(2)}) collective-permute-start(f32[256,128]{1,0:T(8,128)S(1)} %get-tuple-element.32), channel_id=1, source_target_pairs={{0,192},{1,193},{64,0},{65,1},{128,64},{129,65},{192,128},{193,129... | collective-permute-start | bytes 393224 | tf_op jit(solution)/shard_map/second_product/ppermute | solution.py:39
  230.5 15.0 %collective-permute-start.12 = (f32[256,128]{1,0:T(8,128)S(1)}, f32[256,128]{1,0:T(8,128)S(1)}, u32[]{:S(2)}, u32[]{:S(2)}) collective-permute-start(f32[256,128]{1,0:T(8,128)S(1)} %add_add_fusion), channel_id=1, source_target_pairs={{0,256},{1,257},{64,320},{65,321},{128,384},{129,385},{192,448},{1... | collective-permute-start | bytes 393224 | tf_op jit(solution)/shard_map/swap_back/ppermute | solution.py:39

commit v9 on v7

--- a/solution.py
+++ b/solution.py
@@ -48,7 +48,7 @@
 
 
 def b_shift(value, step):
-    return permute(value, lambda x, y, z, c: (x, y, z // 4 * 4 + (z + step) % 4, c))
+    return permute(value, lambda x, y, z, c: (x, y, z ^ step, c))
 
 
 def dot(left, right, dims):
@@ -132,7 +132,7 @@
             rows, lanes = pl.ds(k * part, part), pl.ds(k * wide, wide)
             right[rows, n * wide : (n + 1) * wide] = from_x[n, :, lanes]
             face = (kept, given)[n // 2]
-            source = lax.rem(b + 2 * core + n, 4)
+            source = lax.bitwise_xor(b, lax.rem(2 * core + n, 4))
             face[rows, n % 2 * wide : (n % 2 + 1) * wide] = from_b[source, :, lanes]
     mine[...] = COEF_B * right[pl.ds(pl.multiple_of(x * part, 8), part), :]
 

time: 247 us -> 247 us (level)
  transfers between devices with their start and end apart: 16 -> 16, of which waited for: 10 -> 9; matrix products, arithmetic and copies ran while one was open for 1% -> 1% of each run, Pallas kernels for 1% -> 1%
where the time goes in v9:
time: 247 us; the launch traced here: 246 us
  blocking collectives  81 us (33%)
  starting transfers between devices  75.3 us (30%)
  waiting for transfers between devices  68.7 us (28%)
  matrix products  9.26 us (4%)
  Pallas kernels  8.46 us (3%)
    ppermute x13, starting transfers between devices, permute(): return lax.ppermute(value, AXES, pairs)  61.5 us
    ppermute x13, waiting for transfers between devices, permute(): return lax.ppermute(value, AXES, pairs)  33.6 us
    all_gather x1, blocking collectives, body(): pieces = lax.all_gather(piece, AXES, axis=0, axis_index_groups=A_GROUPS)  23.1 us
    all_gather x1, blocking collectives, body(): from_b = lax.all_gather(block, 'row', axis=0, axis_index_groups=B_GROUPS)  21.5 us
    all_to_all x1, blocking collectives, body(): parts = lax.all_to_all(parts, 'col', 0, 0, axis_index_groups=Y_GROUPS)  21.1 us
    all_to_all x1, waiting for transfers between devices, body(): lax.all_to_all(total.reshape(4, chunk, size), 'col', 0, 0, axis_index_gro...  19.9 us
    all_gather x1, blocking collectives, body(): lax.all_gather(inner, 'row', axis=0, tiled=True, axis_index_groups=X_GROUPS)  15.3 us
    all_to_all x1, waiting for transfers between devices, body(): parts = lax.all_to_all(parts, 'row', 0, 0, axis_index_groups=X_GROUPS)  15.1 us
  transfers between devices with their start and end apart: 16, of which 9 were waited for; matrix products, arithmetic and copies ran while one was open for 1% of the time, Pallas kernels for 1%

profile of v9, /device:TPU:8, one launch (start us, length us, event | category | flops | bytes accessed | tf_op | source)
XLA Modules:
  0.0 245.9 jit_solution(18187211810811609328)
XLA Ops:
  1.1 9.1 %collective-permute-start = (f32[256,128]{1,0:T(8,128)S(1)}, f32[256,128]{1,0:T(8,128)S(1)}, u32[]{:S(2)}, u32[]{:S(2)}) collective-permute-start(f32[256,128]{1,0:T(8,128)S(1)} %get-tuple-element.22), channel_id=1, source_target_pairs={{0,256},{1,257},{64,320},{65,321},{128,384},{129,385},{192,448},{1... | collective-permute-start | bytes 393224 | tf_op jit(solution)/shard_map/swap_columns/ppermute | solution.py:39
  10.2 11.9 %collective-permute-done.other = f32[256,128]{1,0:T(8,128)S(1)} collective-permute-done((f32[256,128]{1,0:T(8,128)S(1)}, f32[256,128]{1,0:T(8,128)S(1)}, u32[]{:S(2)}, u32[]{:S(2)}) %collective-permute-start) | collective-permute-done | bytes 131104 | tf_op jit(solution)/shard_map/swap_columns/ppermute | solution.py:39
  23.5 4.3 %all-to-all-start = ((f32[4,72,896]{2,1,0:T(8,128)}), f32[4,72,896]{2,1,0:T(8,128)S(1)}, u32[]{:S(2)}, u32[]{:S(2)}) async-start(f32[4,72,896]{2,1,0:T(8,128)} %get-tuple-element.23), calls=%async_computation | async-start | bytes 2064384 | tf_op jit(solution)/shard_map/faces/all_to_all | solution.py:228
  27.9 21.5 %all-gather = f32[288,896]{1,0:T(8,128)S(1)} all-gather(f32[72,896]{1,0:T(8,128)S(1)} %get-tuple-element.24), channel_id=2, replica_groups={{0,64,128,192},{16,80,144,208},{32,96,160,224},{48,112,176,240},{256,32..., dimensions={0}, use_global_device_ids=true | all-gather | bytes 1290240 | tf_op jit(solution)/shard_map/faces/all_gather | solution.py:229
  59.1 4.9 %all-to-all-start.1 = ((f32[4,112,896]{2,1,0:T(8,128)}), f32[4,112,896]{2,1,0:T(8,128)S(1)}, u32[]{:S(2)}, u32[]{:S(2)}) async-start(f32[4,112,896]{2,1,0:T(8,128)} %bitcast.43), calls=%async_computation.1 | async-start | bytes 3211264 | tf_op jit(solution)/shard_map/reduce_y/all_to_all | solution.py:244
  64.0 19.9 %all-to-all-done.1 = f32[4,112,896]{2,1,0:T(8,128)S(1)} async-done(((f32[4,112,896]{2,1,0:T(8,128)}), f32[4,112,896]{2,1,0:T(8,128)S(1)}, u32[]{:S(2)}, u32[]{:S(2)}) %all-to-all-start.1) | async-done | bytes 1605664 | tf_op jit(solution)/shard_map/reduce_y/all_to_all | solution.py:244
  84.1 13.2 %collective-permute-start.2 = (f32[25,8,128]{2,1,0:T(8,128)S(1)}, f32[25,8,128]{2,1,0:T(8,128)S(1)}, u32[]{:S(2)}, u32[]{:S(2)}) collective-permute-start(f32[25,8,128]{2,1,0:T(8,128)S(1)} %get-tuple-element.37), channel_id=1, source_target_pairs={{0,2},{1,3},{64,66},{65,67},{128,130},{129,131},{192,194},{193,195... | collective-permute-start | bytes 307208 | tf_op jit(solution)/shard_map/reduce_a/ppermute | solution.py:39
  97.4 4.7 %collective-permute-start.3 = (f32[25,8,128]{2,1,0:T(8,128)S(1)}, f32[25,8,128]{2,1,0:T(8,128)S(1)}, u32[]{:S(2)}, u32[]{:S(2)}) collective-permute-start(f32[25,8,128]{2,1,0:T(8,128)S(1)} %get-tuple-element.39), channel_id=1, source_target_pairs={{0,256},{1,257},{64,320},{65,321},{128,384},{129,385},{192,448},{1... | collective-permute-start | bytes 307208 | tf_op jit(solution)/shard_map/reduce_a/ppermute | solution.py:39
  102.1 5.0 %collective-permute-start.4 = (f32[25,8,128]{2,1,0:T(8,128)S(1)}, f32[25,8,128]{2,1,0:T(8,128)S(1)}, u32[]{:S(2)}, u32[]{:S(2)}) collective-permute-start(f32[25,8,128]{2,1,0:T(8,128)S(1)} %get-tuple-element.38), channel_id=1, source_target_pairs={{0,258},{1,259},{64,322},{65,323},{128,386},{129,387},{192,450},{1... | collective-permute-start | bytes 307208 | tf_op jit(solution)/shard_map/reduce_a/ppermute | solution.py:39
  107.1 5.5 %collective-permute-done.3 = f32[25,8,128]{2,1,0:T(8,128)S(1)} collective-permute-done((f32[25,8,128]{2,1,0:T(8,128)S(1)}, f32[25,8,128]{2,1,0:T(8,128)S(1)}, u32[]{:S(2)}, u32[]{:S(2)}) %collective-permute-start.3) | collective-permute-done | bytes 102432 | tf_op jit(solution)/shard_map/reduce_a/ppermute | solution.py:39
  112.7 3.0 %collective-permute-done.4 = f32[25,8,128]{2,1,0:T(8,128)S(1)} collective-permute-done((f32[25,8,128]{2,1,0:T(8,128)S(1)}, f32[25,8,128]{2,1,0:T(8,128)S(1)}, u32[]{:S(2)}, u32[]{:S(2)}) %collective-permute-start.4) | collective-permute-done | bytes 102432 | tf_op jit(solution)/shard_map/reduce_a/ppermute | solution.py:39
  115.7 23.1 %all-gather.1 = f32[100,8,128]{2,1,0:T(8,128)S(1)} all-gather(f32[25,8,128]{2,1,0:T(8,128)S(1)} %fusion.1), channel_id=3, replica_groups={{0,256,2,258},{1,257,3,259},{64,320,66,322},{65,321,67,323},{128,384,13..., dimensions={0}, use_global_device_ids=true | all-gather | bytes 512000 | tf_op jit(solution)/shard_map/gather_a/all_gather | solution.py:255
  138.9 21.1 %all_to_all.20 = f32[4,112,896]{2,1,0:T(8,128)S(1)} all-to-all(f32[4,112,896]{2,1,0:T(8,128)S(1)} %broadcast_in_dim.3), channel_id=1, replica_groups={{0,4,8,12},{1,5,9,13},{2,6,10,14},{3,7,11,15},{16,20,24,28},{17,21,25,2..., dimensions={0} | all-to-all | bytes 3211264 | tf_op jit(solution)/shard_map/gather_y/all_to_all | solution.py:259
  165.4 3.1 %convolution_add_fusion = f32[288,896]{1,0:T(8,128)} fusion(f32[288,896]{1,0:T(8,128)S(1)} %fusion.2, f32[288,448]{1,0:T(8,128)S(1)} %get-tuple-element.28.left, f32[448,896]{1,0:T(8,128)S(1)} %collective-permute-done.5), kind=kOutput, calls=%fused_computation | convolution fusion | flops 1387524096 | bytes 4186112 | tf_op jit(solution)/shard_map/first_product/dot_general | solution.py:55
  168.4 4.6 %all-to-all-start.3 = ((f32[4,72,896]{2,1,0:T(8,128)}), f32[4,72,896]{2,1,0:T(8,128)S(1)}, u32[]{:S(2)}, u32[]{:S(2)}) async-start(f32[4,72,896]{2,1,0:T(8,128)} %bitcast.44), calls=%async_computation.3 | async-start | bytes 2064384 | tf_op jit(solution)/shard_map/first_product/all_to_all | solution.py:268
  173.1 15.1 %all-to-all-done.3 = f32[4,72,896]{2,1,0:T(8,128)S(1)} async-done(((f32[4,72,896]{2,1,0:T(8,128)}), f32[4,72,896]{2,1,0:T(8,128)S(1)}, u32[]{:S(2)}, u32[]{:S(2)}) %all-to-all-start.3) | async-done | bytes 1032224 | tf_op jit(solution)/shard_map/first_product/all_to_all | solution.py:268
  188.4 15.3 %all_gather.19 = f32[288,896]{1,0:T(8,128)S(1)} all-gather(f32[72,896]{1,0:T(8,128)S(1)} %multiply_add_fusion), channel_id=1, replica_groups={{0,16,32,48},{64,80,96,112},{128,144,160,176},{192,208,224,240},{256,27..., dimensions={0}, use_global_device_ids=true | all-gather | bytes 1290240 | tf_op jit(solution)/shard_map/first_product/all_gather | solution.py:270
  211.0 5.9 %collective-permute-start.11 = (f32[256,128]{1,0:T(8,128)S(1)}, f32[256,128]{1,0:T(8,128)S(1)}, u32[]{:S(2)}, u32[]{:S(2)}) collective-permute-start(f32[256,128]{1,0:T(8,128)S(1)} %get-tuple-element.36), channel_id=1, source_target_pairs={{0,192},{1,193},{64,128},{65,129},{128,64},{129,65},{192,0},{193,1... | collective-permute-start | bytes 393224 | tf_op jit(solution)/shard_map/second_product/ppermute | solution.py:39
  216.9 2.5 %collective-permute-start.9 = (f32[256,128]{1,0:T(8,128)S(1)}, f32[256,128]{1,0:T(8,128)S(1)}, u32[]{:S(2)}, u32[]{:S(2)}) collective-permute-start(f32[256,128]{1,0:T(8,128)S(1)} %get-tuple-element.34), channel_id=1, source_target_pairs={{0,64},{1,65},{64,0},{65,1},{128,192},{129,193},{192,128},{193,129... | collective-permute-start | bytes 393224 | tf_op jit(solution)/shard_map/second_product/ppermute | solution.py:39
  219.4 3.4 %collective-permute-start.6 = (f32[256,128]{1,0:T(8,128)S(1)}, f32[256,128]{1,0:T(8,128)S(1)}, u32[]{:S(2)}, u32[]{:S(2)}) collective-permute-start(f32[256,128]{1,0:T(8,128)S(1)} %get-tuple-element.30), channel_id=1, source_target_pairs={{0,64},{1,65},{64,0},{65,1},{128,192},{129,193},{192,128},{193,129... | collective-permute-start | bytes 393224 | tf_op jit(solution)/shard_map/second_product/ppermute | solution.py:39
  222.8 3.9 %collective-permute-start.7 = (f32[256,128]{1,0:T(8,128)S(1)}, f32[256,128]{1,0:T(8,128)S(1)}, u32[]{:S(2)}, u32[]{:S(2)}) collective-permute-start(f32[256,128]{1,0:T(8,128)S(1)} %get-tuple-element.31), channel_id=1, source_target_pairs={{0,128},{1,129},{64,192},{65,193},{128,0},{129,1},{192,64},{193,65... | collective-permute-start | bytes 393224 | tf_op jit(solution)/shard_map/second_product/ppermute | solution.py:39
  226.7 2.8 %collective-permute-start.8 = (f32[256,128]{1,0:T(8,128)S(1)}, f32[256,128]{1,0:T(8,128)S(1)}, u32[]{:S(2)}, u32[]{:S(2)}) collective-permute-start(f32[256,128]{1,0:T(8,128)S(1)} %get-tuple-element.32), channel_id=1, source_target_pairs={{0,192},{1,193},{64,128},{65,129},{128,64},{129,65},{192,0},{193,1... | collective-permute-start | bytes 393224 | tf_op jit(solution)/shard_map/second_product/ppermute | solution.py:39
  229.6 5.1 %collective-permute-start.12 = (f32[256,128]{1,0:T(8,128)S(1)}, f32[256,128]{1,0:T(8,128)S(1)}, u32[]{:S(2)}, u32[]{:S(2)}) collective-permute-start(f32[256,128]{1,0:T(8,128)S(1)} %add_add_fusion), channel_id=1, source_target_pairs={{0,256},{1,257},{64,320},{65,321},{128,384},{129,385},{192,448},{1... | collective-permute-start | bytes 393224 | tf_op jit(solution)/shard_map/swap_back/ppermute | solution.py:39
  236.2 8.9 %collective-permute-done.12.other = f32[256,128]{1,0:T(8,128)S(1)} collective-permute-done((f32[256,128]{1,0:T(8,128)S(1)}, f32[256,128]{1,0:T(8,128)S(1)}, u32[]{:S(2)}, u32[]{:S(2)}) %collective-permute-start.12) | collective-permute-done | bytes 131104 | tf_op jit(solution)/shard_map/swap_back/ppermute | solution.py:39
  (44 shorter events, 27.7 us)
Async XLA Ops:
  0.0 1.0 copy-start
  1.1 21.0 %collective-permute-start = (f32[256,128]{1,0:T(8,128)S(1)}, f32[256,128]{1,0:T(8,128)S(1)}, u32[]{:S(2)}, u32[]{:S(2)}) collective-permute-start(f32[256,128]{1,0:T(8,128)S(1)} %get-tuple-element.22), channel_id=1, source_target_pairs={{0,256},{1,257},{64,320},{65,321},{128,384},{129,385},{192,448},{1... | collective-permute-start | bytes 393224 | tf_op jit(solution)/shard_map/swap_columns/ppermute | solution.py:39
  23.5 25.9 %all-to-all-start = ((f32[4,72,896]{2,1,0:T(8,128)}), f32[4,72,896]{2,1,0:T(8,128)S(1)}, u32[]{:S(2)}, u32[]{:S(2)}) async-start(f32[4,72,896]{2,1,0:T(8,128)} %get-tuple-element.23), calls=%async_computation | async-start | bytes 2064384 | tf_op jit(solution)/shard_map/faces/all_to_all | solution.py:228
  52.4 5.4 %collective-permute-start.1 = (f32[448,896]{1,0:T(8,128)S(1)}, f32[448,896]{1,0:T(8,128)S(1)}, u32[]{:S(2)}, u32[]{:S(2)}) collective-permute-start(f32[448,896]{1,0:T(8,128)S(1)} %gram.3), channel_id=1, source_target_pairs={{0,1},{1,0},{64,65},{65,64},{128,129},{129,128},{192,193},{193,192... | collective-permute-start | bytes 4816904 | tf_op jit(solution)/shard_map/gram/ppermute | solution.py:39
  59.1 24.8 %all-to-all-start.1 = ((f32[4,112,896]{2,1,0:T(8,128)}), f32[4,112,896]{2,1,0:T(8,128)S(1)}, u32[]{:S(2)}, u32[]{:S(2)}) async-start(f32[4,112,896]{2,1,0:T(8,128)} %bitcast.43), calls=%async_computation.1 | async-start | bytes 3211264 | tf_op jit(solution)/shard_map/reduce_y/all_to_all | solution.py:244
  84.1 23.0 %collective-permute-start.2 = (f32[25,8,128]{2,1,0:T(8,128)S(1)}, f32[25,8,128]{2,1,0:T(8,128)S(1)}, u32[]{:S(2)}, u32[]{:S(2)}) collective-permute-start(f32[25,8,128]{2,1,0:T(8,128)S(1)} %get-tuple-element.37), channel_id=1, source_target_pairs={{0,2},{1,3},{64,66},{65,67},{128,130},{129,131},{192,194},{193,195... | collective-permute-start | bytes 307208 | tf_op jit(solution)/shard_map/reduce_a/ppermute | solution.py:39
  97.4 15.3 %collective-permute-start.3 = (f32[25,8,128]{2,1,0:T(8,128)S(1)}, f32[25,8,128]{2,1,0:T(8,128)S(1)}, u32[]{:S(2)}, u32[]{:S(2)}) collective-permute-start(f32[25,8,128]{2,1,0:T(8,128)S(1)} %get-tuple-element.39), channel_id=1, source_target_pairs={{0,256},{1,257},{64,320},{65,321},{128,384},{129,385},{192,448},{1... | collective-permute-start | bytes 307208 | tf_op jit(solution)/shard_map/reduce_a/ppermute | solution.py:39
  102.1 13.6 %collective-permute-start.4 = (f32[25,8,128]{2,1,0:T(8,128)S(1)}, f32[25,8,128]{2,1,0:T(8,128)S(1)}, u32[]{:S(2)}, u32[]{:S(2)}) collective-permute-start(f32[25,8,128]{2,1,0:T(8,128)S(1)} %get-tuple-element.38), channel_id=1, source_target_pairs={{0,258},{1,259},{64,322},{65,323},{128,386},{129,387},{192,450},{1... | collective-permute-start | bytes 307208 | tf_op jit(solution)/shard_map/reduce_a/ppermute | solution.py:39
  160.0 5.3 %collective-permute-start.5 = (f32[448,896]{1,0:T(8,128)S(1)}, f32[448,896]{1,0:T(8,128)S(1)}, u32[]{:S(2)}, u32[]{:S(2)}) collective-permute-start(f32[448,896]{1,0:T(8,128)S(1)} %bitcast.40), channel_id=1, source_target_pairs={{0,1},{1,0},{64,65},{65,64},{128,129},{129,128},{192,193},{193,192... | collective-permute-start | bytes 4816904 | tf_op jit(solution)/shard_map/gather_core/ppermute | solution.py:39
  165.4 3.1 %copy-start.2 = (f32[448,896]{1,0:T(8,128)}, f32[448,896]{1,0:T(8,128)S(1)}, u32[]{:S(2)}) copy-start(f32[448,896]{1,0:T(8,128)S(1)} %collective-permute-done.5) | copy-start | bytes 4816900
  168.4 19.8 %all-to-all-start.3 = ((f32[4,72,896]{2,1,0:T(8,128)}), f32[4,72,896]{2,1,0:T(8,128)S(1)}, u32[]{:S(2)}, u32[]{:S(2)}) async-start(f32[4,72,896]{2,1,0:T(8,128)} %bitcast.44), calls=%async_computation.3 | async-start | bytes 2064384 | tf_op jit(solution)/shard_map/first_product/all_to_all | solution.py:268
  203.7 2.1 copy-start.3
  207.9 37.2 %copy-start.1 = (f32[112,576]{1,0:T(8,128)S(1)}, f32[112,576]{1,0:T(8,128)}, u32[]{:S(2)}) copy-start(f32[112,576]{1,0:T(8,128)} %iterate.3) | copy-start | bytes 774148
  209.0 17.7 %collective-permute-start.10 = (f32[256,128]{1,0:T(8,128)S(1)}, f32[256,128]{1,0:T(8,128)S(1)}, u32[]{:S(2)}, u32[]{:S(2)}) collective-permute-start(f32[256,128]{1,0:T(8,128)S(1)} %get-tuple-element.35), channel_id=1, source_target_pairs={{0,128},{1,129},{64,192},{65,193},{128,0},{129,1},{192,64},{193,65... | collective-permute-start | bytes 393224 | tf_op jit(solution)/shard_map/second_product/ppermute | solution.py:39
  211.0 18.6 %collective-permute-start.11 = (f32[256,128]{1,0:T(8,128)S(1)}, f32[256,128]{1,0:T(8,128)S(1)}, u32[]{:S(2)}, u32[]{:S(2)}) collective-permute-start(f32[256,128]{1,0:T(8,128)S(1)} %get-tuple-element.36), channel_id=1, source_target_pairs={{0,192},{1,193},{64,128},{65,129},{128,64},{129,65},{192,0},{193,1... | collective-permute-start | bytes 393224 | tf_op jit(solution)/shard_map/second_product/ppermute | solution.py:39
  216.9 12.6 %collective-permute-start.9 = (f32[256,128]{1,0:T(8,128)S(1)}, f32[256,128]{1,0:T(8,128)S(1)}, u32[]{:S(2)}, u32[]{:S(2)}) collective-permute-start(f32[256,128]{1,0:T(8,128)S(1)} %get-tuple-element.34), channel_id=1, source_target_pairs={{0,64},{1,65},{64,0},{65,1},{128,192},{129,193},{192,128},{193,129... | collective-permute-start | bytes 393224 | tf_op jit(solution)/shard_map/second_product/ppermute | solution.py:39
  219.4 15.4 %collective-permute-start.6 = (f32[256,128]{1,0:T(8,128)S(1)}, f32[256,128]{1,0:T(8,128)S(1)}, u32[]{:S(2)}, u32[]{:S(2)}) collective-permute-start(f32[256,128]{1,0:T(8,128)S(1)} %get-tuple-element.30), channel_id=1, source_target_pairs={{0,64},{1,65},{64,0},{65,1},{128,192},{129,193},{192,128},{193,129... | collective-permute-start | bytes 393224 | tf_op jit(solution)/shard_map/second_product/ppermute | solution.py:39
  222.8 12.0 %collective-permute-start.7 = (f32[256,128]{1,0:T(8,128)S(1)}, f32[256,128]{1,0:T(8,128)S(1)}, u32[]{:S(2)}, u32[]{:S(2)}) collective-permute-start(f32[256,128]{1,0:T(8,128)S(1)} %get-tuple-element.31), channel_id=1, source_target_pairs={{0,128},{1,129},{64,192},{65,193},{128,0},{129,1},{192,64},{193,65... | collective-permute-start | bytes 393224 | tf_op jit(solution)/shard_map/second_product/ppermute | solution.py:39
  226.7 9.5 %collective-permute-start.8 = (f32[256,128]{1,0:T(8,128)S(1)}, f32[256,128]{1,0:T(8,128)S(1)}, u32[]{:S(2)}, u32[]{:S(2)}) collective-permute-start(f32[256,128]{1,0:T(8,128)S(1)} %get-tuple-element.32), channel_id=1, source_target_pairs={{0,192},{1,193},{64,128},{65,129},{128,64},{129,65},{192,0},{193,1... | collective-permute-start | bytes 393224 | tf_op jit(solution)/shard_map/second_product/ppermute | solution.py:39
  229.6 15.5 %collective-permute-start.12 = (f32[256,128]{1,0:T(8,128)S(1)}, f32[256,128]{1,0:T(8,128)S(1)}, u32[]{:S(2)}, u32[]{:S(2)}) collective-permute-start(f32[256,128]{1,0:T(8,128)S(1)} %add_add_fusion), channel_id=1, source_target_pairs={{0,256},{1,257},{64,320},{65,321},{128,384},{129,385},{192,448},{1... | collective-permute-start | bytes 393224 | tf_op jit(solution)/shard_map/swap_back/ppermute | solution.py:39
